TPU v7x, 256 devices: a whole 4x4x8 slice. The times are simulated.
256 devices in a mesh: seg: 32 (over z_lo, x, y), gx: 8 (over z_hi, core).
Axes of the slice: x: 4, y: 4, z: 8 (z_hi: 4, z_lo: 2; z = z_hi * 2 + z_lo), core: 2. Of those that a mesh axis runs over, the one named last changes fastest.
Arguments:
- krylov: float32 [32, 8, 256, 1024], P('seg', None, 'gx')
- advect_x: float32 [32, 256, 1024], P('seg', 'gx'), may hold values from -0.18 to 0.18
- advect_y: float32 [32, 256, 1024], P('seg', 'gx'), may hold values from -0.18 to 0.18
- step_counts: int32 [32], P('seg'), may hold values from 1 to 4, as said below
- drifts: int32 [32], P('seg'), may hold values from 0 to 16, as said below
Outputs:
- product: float32 [32, 8, 256, 1024], P('seg', None, 'gx')
- gram: float32 [8, 8], replicated
Inputs may be any that keep to these rules, and one draw needn't show every extreme that they name: `step_counts`: some segment takes exactly 4 steps. Some segment drifts by exactly 16 cells.
All inputs are finite; a program needn't handle non-finite values.
Results may differ from a plain program's by a relative error of at most 0.0003.
Values sent between devices are 32-bit elements; how exact they have to be, the bound alone decides.
No kernel may reach another device: no remote copies, remote signals or barrier semaphores. Data moves between devices by JAX's collectives and lax.ppermute only.
A program may use at most 64 MiB of HBM per device.

v0:
```python
import jax
import jax.numpy as jnp
from jax import lax
from jax.sharding import PartitionSpec as P

STEPS = 4


def extended_2(cells, sides, width):
    for axis, dim in sides:
        count = lax.axis_size(axis)
        head = lax.slice_in_dim(cells, 0, width, axis=dim)
        tail = lax.slice_in_dim(cells, cells.shape[dim] - width, cells.shape[dim], axis=dim)
        cells = jnp.concatenate(
            [
                lax.ppermute(tail, axis, [(i, (i + 1) % count) for i in range(count)]),
                cells,
                lax.ppermute(head, axis, [((i + 1) % count, i) for i in range(count)]),
            ],
            axis=dim,
        )
    return cells


def from_behind(value, axis, steps):
    count = lax.axis_size(axis)
    pairs = [(source, (source + steps) % count) for source in range(count)]
    return lax.ppermute(value, axis, pairs)


def stencil(extended, coef_x, coef_y):
    centre = extended[:, :, 1:-1, :]
    east = extended[:, :, 2:, :]
    west = extended[:, :, :-2, :]
    zeros = jnp.zeros_like(centre[:, :, :, :1])
    north = jnp.concatenate([centre[:, :, :, 1:], zeros], axis=3)
    south = jnp.concatenate([zeros, centre[:, :, :, :-1]], axis=3)
    return (
        centre
        + 0.2 * (east + west + north + south - 4.0 * centre)
        - coef_x * (east - west)
        - coef_y * (north - south)
    )


def crop_segment(extended, shift_by, rim_width, strip):
    start = rim_width - shift_by
    return lax.dynamic_slice_in_dim(extended, start, strip, 1)


def body(krylov, advect_x, advect_y, step_counts, drifts):
    strip = krylov.shape[2]
    rows_y = krylov.shape[3]
    counts_full = step_counts[:, None, None, None]
    coef_x = advect_x[:, None]
    coef_y = advect_y[:, None]
    field = krylov
    for section in range(STEPS):
        extended = extended_2(field, (("gx", 2),), 1)
        stepped = stencil(extended, coef_x, coef_y)
        field = jnp.where(section < counts_full, stepped, field)
    rim_width = strip // 2
    left_rim = from_behind(field[:, :, strip - rim_width :, :], "gx", 1)
    joined = jnp.concatenate([left_rim, field], axis=2)
    moved = jax.vmap(lambda piece, shift_by: crop_segment(piece, shift_by, rim_width, strip))(
        joined, drifts
    )
    arrived = from_behind(moved, "seg", 1)
    previous = jnp.concatenate([arrived, moved[:-1]], axis=0)
    product = krylov - previous
    local_sum = jnp.einsum("sbxy,scxy->bc", krylov, product, precision=lax.Precision.HIGHEST)
    total = lax.psum(local_sum, ("seg", "gx"))
    cells = lax.axis_size("seg") * krylov.shape[0] * lax.axis_size("gx") * strip * rows_y
    gram = total / jnp.float32(cells)
    return (product, gram)


def solution(mesh):
    return jax.shard_map(
        body,
        mesh=mesh,
        in_specs=(
            P("seg", None, "gx", None),
            P("seg", "gx", None),
            P("seg", "gx", None),
            P("seg"),
            P("seg"),
        ),
        out_specs=(P("seg", None, "gx", None), P()),
        check_vma=False,
    )
```

profile of v0, /device:TPU:1, one launch (start us, length us, event | category | flops | bytes accessed | tf_op | source)
XLA Modules:
  0.0 155.0 jit_solution(10326249961837841508)
XLA Ops:
  0.6 1.1 fusion.9
  1.7 3.3 %collective-permute-start = (f32[1,8,1,1024]{3,2,1,0:T(1,128)S(1)}, f32[1,8,1,1024]{3,2,1,0:T(1,128)S(1)}, u32[]{:S(2)}, u32[]{:S(2)}) collective-permute-start(f32[1,8,1,1024]{3,2,1,0:T(1,128)S(1)} %get-tuple-element.28), channel_id=1, source_target_pairs={{1,0},{2,1},{3,2},{4,3},{5,4},{6,5},{7,6},{0,7},{9,8},{10,9},{11,1... | collective-permute-start | bytes 98312 | tf_op jit(solution)/shard_map/ppermute | solution.py:18
  5.0 1.3 collective-permute-start.1
  6.3 2.0 %fusion.10 = (f32[1,8,32,1023]{3,2,1,0:T(8,128)S(1)}, f32[1,8,32,1023]{3,2,1,0:T(8,128)S(1)}) fusion(f32[1,8,32,1024]{3,2,1,0:T(8,128)} %param.5), kind=kLoop, calls=%fused_computation.26 | loop fusion | bytes 4190208 | tf_op jit(solution)/shard_map/slice | solution.py:36
  9.0 0.7 collective-permute-done.1
  9.8 0.8 subtract_select_fusion.3
  10.6 4.8 %collective-permute-start.2 = (f32[1,8,1,1024]{3,2,1,0:T(1,128)S(1)}, f32[1,8,1,1024]{3,2,1,0:T(1,128)S(1)}, u32[]{:S(2)}, u32[]{:S(2)}) collective-permute-start(f32[1,8,1,1024]{3,2,1,0:T(1,128)S(1)} %get-tuple-element.24), channel_id=1, source_target_pairs={{1,0},{2,1},{3,2},{4,3},{5,4},{6,5},{7,6},{0,7},{9,8},{10,9},{11,1... | collective-permute-start | bytes 98312 | tf_op jit(solution)/shard_map/ppermute | solution.py:18
  15.4 0.4 fusion.8
  15.8 0.5 collective-permute-done.2
  16.3 1.0 collective-permute-done.3
  17.3 0.8 subtract_select_fusion.2
  18.1 4.8 %collective-permute-start.4 = (f32[1,8,1,1024]{3,2,1,0:T(1,128)S(1)}, f32[1,8,1,1024]{3,2,1,0:T(1,128)S(1)}, u32[]{:S(2)}, u32[]{:S(2)}) collective-permute-start(f32[1,8,1,1024]{3,2,1,0:T(1,128)S(1)} %get-tuple-element.20), channel_id=1, source_target_pairs={{1,0},{2,1},{3,2},{4,3},{5,4},{6,5},{7,6},{0,7},{9,8},{10,9},{11,1... | collective-permute-start | bytes 98312 | tf_op jit(solution)/shard_map/ppermute | solution.py:18
  23.3 0.5 collective-permute-done.4
  24.1 0.8 subtract_select_fusion.1
  24.9 4.4 %collective-permute-start.6 = (f32[1,8,1,1024]{3,2,1,0:T(1,128)S(1)}, f32[1,8,1,1024]{3,2,1,0:T(1,128)S(1)}, u32[]{:S(2)}, u32[]{:S(2)}) collective-permute-start(f32[1,8,1,1024]{3,2,1,0:T(1,128)S(1)} %get-tuple-element.16), channel_id=1, source_target_pairs={{1,0},{2,1},{3,2},{4,3},{5,4},{6,5},{7,6},{0,7},{9,8},{10,9},{11,1... | collective-permute-start | bytes 98312 | tf_op jit(solution)/shard_map/ppermute | solution.py:18
  29.7 0.5 collective-permute-done.6
  30.6 0.8 subtract_select_fusion
  31.4 3.1 %collective-permute-start.8 = (f32[1,8,16,1024]{3,2,1,0:T(8,128)S(1)}, f32[1,8,16,1024]{3,2,1,0:T(8,128)S(1)}, u32[]{:S(2)}, u32[]{:S(2)}) collective-permute-start(f32[1,8,16,1024]{3,2,1,0:T(8,128)S(1)} %slice.140), channel_id=1, source_target_pairs={{0,1},{1,2},{2,3},{3,4},{4,5},{5,6},{6,7},{7,0},{8,9},{9,10},{10,1... | collective-permute-start | bytes 1572872 | tf_op jit(solution)/shard_map/ppermute | solution.py:28
  35.1 6.6 %collective-permute-done.8 = f32[1,8,16,1024]{3,2,1,0:T(8,128)S(1)} collective-permute-done((f32[1,8,16,1024]{3,2,1,0:T(8,128)S(1)}, f32[1,8,16,1024]{3,2,1,0:T(8,128)S(1)}, u32[]{:S(2)}, u32[]{:S(2)}) %collective-permute-start.8) | collective-permute-done | bytes 524320 | tf_op jit(solution)/shard_map/ppermute | solution.py:28
  42.0 1.6 %collective-permute-start.9 = (f32[1,8,32,1024]{3,2,1,0:T(8,128)S(1)}, f32[1,8,32,1024]{3,2,1,0:T(8,128)S(1)}, u32[]{:S(2)}, u32[]{:S(2)}) collective-permute-start(f32[1,8,32,1024]{3,2,1,0:T(8,128)S(1)} %fusion), channel_id=1, source_target_pairs={{0,8},{8,16},{16,24},{24,32},{32,40},{40,48},{48,56},{56,64},{64,7... | collective-permute-start | bytes 3145736 | tf_op jit(solution)/shard_map/ppermute | solution.py:28
  43.6 25.9 %collective-permute-done.9 = f32[1,8,32,1024]{3,2,1,0:T(8,128)S(1)} collective-permute-done((f32[1,8,32,1024]{3,2,1,0:T(8,128)S(1)}, f32[1,8,32,1024]{3,2,1,0:T(8,128)S(1)}, u32[]{:S(2)}, u32[]{:S(2)}) %collective-permute-start.9) | collective-permute-done | bytes 1048608 | tf_op jit(solution)/shard_map/ppermute | solution.py:28
  69.7 3.2 %convolution_bitcast_fusion = f32[8,8]{0,1:T(8,128)S(1)} fusion(f32[8,32,1024]{2,1,0:T(8,128)S(1)} %bitcast.13, f32[8,32,1024]{2,1,0:T(8,128)S(1)} %bitcast.14), kind=kOutput, calls=%fused_computation.2 | convolution fusion | flops 25165824 | bytes 2097408 | tf_op jit(solution)/shard_map/sbxy,scxy->bc/dot_general | solution.py:71
  72.9 81.4 %psum.7 = f32[8,8]{0,1:T(8,128)S(1)} all-reduce(f32[8,8]{0,1:T(8,128)S(1)} %convolution_bitcast_fusion), channel_id=1, replica_groups=mesh['seg'=32,'gx'=8] {'seg','gx'}, use_global_device_ids=true, to_apply=%region_0.1 | all-reduce | flops 64 | bytes 512 | tf_op jit(solution)/shard_map/psum | solution.py:72
  154.3 0.7 copy.9
  (23 shorter events, 2.1 us)
Async XLA Ops:
  1.7 7.3 %collective-permute-start = (f32[1,8,1,1024]{3,2,1,0:T(1,128)S(1)}, f32[1,8,1,1024]{3,2,1,0:T(1,128)S(1)}, u32[]{:S(2)}, u32[]{:S(2)}) collective-permute-start(f32[1,8,1,1024]{3,2,1,0:T(1,128)S(1)} %get-tuple-element.28), channel_id=1, source_target_pairs={{1,0},{2,1},{3,2},{4,3},{5,4},{6,5},{7,6},{0,7},{9,8},{10,9},{11,1... | collective-permute-start | bytes 98312 | tf_op jit(solution)/shard_map/ppermute | solution.py:18
  5.0 4.7 %copy-start = (f32[1,8,32,1024]{3,2,1,0:T(8,128)S(1)}, f32[1,8,32,1024]{3,2,1,0:T(8,128)}, u32[]{:S(2)}) copy-start(f32[1,8,32,1024]{3,2,1,0:T(8,128)} %param.5) | copy-start | bytes 3145732
  5.0 4.7 %copy-start.2 = (f32[1,32,1024]{2,1,0:T(8,128)S(1)}, f32[1,32,1024]{2,1,0:T(8,128)}, u32[]{:S(2)}) copy-start(f32[1,32,1024]{2,1,0:T(8,128)} %param.7) | copy-start | bytes 393220
  5.0 4.7 %copy-start.3 = (f32[1,32,1024]{2,1,0:T(8,128)S(1)}, f32[1,32,1024]{2,1,0:T(8,128)}, u32[]{:S(2)}) copy-start(f32[1,32,1024]{2,1,0:T(8,128)} %param.6) | copy-start | bytes 393220
  5.0 4.7 %collective-permute-start.1 = (f32[1,8,1,1024]{3,2,1,0:T(1,128)S(1)}, f32[1,8,1,1024]{3,2,1,0:T(1,128)S(1)}, u32[]{:S(2)}, u32[]{:S(2)}) collective-permute-start(f32[1,8,1,1024]{3,2,1,0:T(1,128)S(1)} %get-tuple-element.27), channel_id=1, source_target_pairs={{0,1},{1,2},{2,3},{3,4},{4,5},{5,6},{6,7},{7,0},{8,9},{9,10},{10,1... | collective-permute-start | bytes 98312 | tf_op jit(solution)/shard_map/ppermute | solution.py:16
  10.6 5.7 %collective-permute-start.2 = (f32[1,8,1,1024]{3,2,1,0:T(1,128)S(1)}, f32[1,8,1,1024]{3,2,1,0:T(1,128)S(1)}, u32[]{:S(2)}, u32[]{:S(2)}) collective-permute-start(f32[1,8,1,1024]{3,2,1,0:T(1,128)S(1)} %get-tuple-element.24), channel_id=1, source_target_pairs={{1,0},{2,1},{3,2},{4,3},{5,4},{6,5},{7,6},{0,7},{9,8},{10,9},{11,1... | collective-permute-start | bytes 98312 | tf_op jit(solution)/shard_map/ppermute | solution.py:18
  15.4 1.9 %collective-permute-start.3 = (f32[1,8,1,1024]{3,2,1,0:T(1,128)S(1)}, f32[1,8,1,1024]{3,2,1,0:T(1,128)S(1)}, u32[]{:S(2)}, u32[]{:S(2)}) collective-permute-start(f32[1,8,1,1024]{3,2,1,0:T(1,128)S(1)} %get-tuple-element.23), channel_id=1, source_target_pairs={{0,1},{1,2},{2,3},{3,4},{4,5},{5,6},{6,7},{7,0},{8,9},{9,10},{10,1... | collective-permute-start | bytes 98312 | tf_op jit(solution)/shard_map/ppermute | solution.py:16
  18.1 5.7 %collective-permute-start.4 = (f32[1,8,1,1024]{3,2,1,0:T(1,128)S(1)}, f32[1,8,1,1024]{3,2,1,0:T(1,128)S(1)}, u32[]{:S(2)}, u32[]{:S(2)}) collective-permute-start(f32[1,8,1,1024]{3,2,1,0:T(1,128)S(1)} %get-tuple-element.20), channel_id=1, source_target_pairs={{1,0},{2,1},{3,2},{4,3},{5,4},{6,5},{7,6},{0,7},{9,8},{10,9},{11,1... | collective-permute-start | bytes 98312 | tf_op jit(solution)/shard_map/ppermute | solution.py:18
  22.9 1.2 collective-permute-start.5
  24.9 5.3 %collective-permute-start.6 = (f32[1,8,1,1024]{3,2,1,0:T(1,128)S(1)}, f32[1,8,1,1024]{3,2,1,0:T(1,128)S(1)}, u32[]{:S(2)}, u32[]{:S(2)}) collective-permute-start(f32[1,8,1,1024]{3,2,1,0:T(1,128)S(1)} %get-tuple-element.16), channel_id=1, source_target_pairs={{1,0},{2,1},{3,2},{4,3},{5,4},{6,5},{7,6},{0,7},{9,8},{10,9},{11,1... | collective-permute-start | bytes 98312 | tf_op jit(solution)/shard_map/ppermute | solution.py:18
  29.3 1.2 collective-permute-start.7
  31.4 10.4 %collective-permute-start.8 = (f32[1,8,16,1024]{3,2,1,0:T(8,128)S(1)}, f32[1,8,16,1024]{3,2,1,0:T(8,128)S(1)}, u32[]{:S(2)}, u32[]{:S(2)}) collective-permute-start(f32[1,8,16,1024]{3,2,1,0:T(8,128)S(1)} %slice.140), channel_id=1, source_target_pairs={{0,1},{1,2},{2,3},{3,4},{4,5},{5,6},{6,7},{7,0},{8,9},{9,10},{10,1... | collective-permute-start | bytes 1572872 | tf_op jit(solution)/shard_map/ppermute | solution.py:28
  42.0 27.5 %collective-permute-start.9 = (f32[1,8,32,1024]{3,2,1,0:T(8,128)S(1)}, f32[1,8,32,1024]{3,2,1,0:T(8,128)S(1)}, u32[]{:S(2)}, u32[]{:S(2)}) collective-permute-start(f32[1,8,32,1024]{3,2,1,0:T(8,128)S(1)} %fusion), channel_id=1, source_target_pairs={{0,8},{8,16},{16,24},{24,32},{32,40},{40,48},{48,56},{56,64},{64,7... | collective-permute-start | bytes 3145736 | tf_op jit(solution)/shard_map/ppermute | solution.py:28
  69.7 3.3 %copy-start.1 = (f32[1,8,32,1024]{3,2,1,0:T(8,128)}, f32[1,8,32,1024]{3,2,1,0:T(8,128)S(1)}, u32[]{:S(2)}) copy-start(f32[1,8,32,1024]{3,2,1,0:T(8,128)S(1)} %sub.87) | copy-start | bytes 3145732
where the time goes:
time: 155 us
  blocking collectives  81.4 us (53%)
  waiting for transfers between devices  36.4 us (23%)
  starting transfers between devices  23.3 us (15%)
  local copies, waits for them, and re-layouts  5.14 us (3%)
  other arithmetic  3.44 us (2%)
  matrix products  3.24 us (2%)
  between operations  2.07 us (1%)
    psum x1, blocking collectives, body(): total = lax.psum(local_sum, ('seg', 'gx'))  81.4 us
    ppermute x2, waiting for transfers between devices, from_behind(): return lax.ppermute(value, axis, pairs)  32.6 us
    ppermute x4, starting transfers between devices, extended_2(): lax.ppermute(head, axis, [((i + 1) % count, i) for i in range(count)])  17.4 us
    ppermute x2, starting transfers between devices, from_behind(): return lax.ppermute(value, axis, pairs)  4.66 us
    dot_general x1, matrix products, body(): jnp.einsum('sbxy,scxy->bc', krylov, product, precision=lax.Precision.HIGH...  3.24 us
    slice x4, local copies, waits for them, and re-layouts, stencil(): north = jnp.concatenate([centre[:, :, :, 1:], zeros], axis=3)  3.19 us
  transfers between devices with their start and end apart: 10, of which 9 were waited for; matrix products, arithmetic and copies ran while one was open for 2% of the time, Pallas kernels for 0%

commit v1 on v0

v1 whole, which is shorter than its diff:
```python
import functools
import jax
import jax.numpy as jnp
from jax import lax
from jax.experimental import pallas as pl
from jax.experimental.pallas import tpu as pltpu
from jax.sharding import PartitionSpec as P

STEPS = 4
DRIFT = 16
TILE = 8

VMEM = pl.BlockSpec(memory_space=pltpu.VMEM)
SMEM = pl.BlockSpec(memory_space=pltpu.SMEM)
LIMIT = 32 * 1024 * 1024


def shift_pairs(count, by):
    return [(i, (i + by) % count) for i in range(count)]


def weights(ax, ay):
    col = lax.broadcasted_iota(jnp.int32, ax.shape, 1)
    last = ax.shape[1] - 1
    return (
        0.2 - ax,
        0.2 + ax,
        jnp.where(col == last, 0.0, 0.2 - ay),
        jnp.where(col == 0, 0.0, 0.2 + ay),
    )


def step(q, we, ww, wn, ws):
    rows, cols = q.shape
    return (
        0.2 * q
        + we * pltpu.roll(q, rows - 1, 0)
        + ww * pltpu.roll(q, 1, 0)
        + wn * pltpu.roll(q, cols - 1, 1)
        + ws * pltpu.roll(q, 1, 1)
    )


def inner_kernel(count_ref, k_ref, ax_ref, ay_ref, mid_ref, low_ref, high_ref, q_ref, w_ref):
    vectors, rows, _ = k_ref.shape
    for i, w in enumerate(weights(ax_ref[...], ay_ref[...])):
        w_ref[i] = w
    q_ref[...] = k_ref[...]

    @pl.loop(0, count_ref[0])
    def _(_):
        for b in range(vectors):
            q_ref[b] = step(q_ref[b], w_ref[0], w_ref[1], w_ref[2], w_ref[3])

    mid_ref[...] = q_ref[:, TILE : rows - TILE]
    low_ref[...] = q_ref[:, :TILE]
    high_ref[...] = q_ref[:, rows - TILE :]


def outer_kernel(
    count_ref, k_ref, ax_ref, ay_ref, left_ref, right_ref, low_ref, high_ref, lo_ref, hi_ref, q_ref, w_ref
):
    vectors, rows, _ = k_ref.shape

    def around(strip, at):
        return jnp.concatenate(
            [strip[rows - TILE :], right_ref[at], left_ref[at], strip[:TILE]], axis=0
        )

    for i, w in enumerate(weights(around(ax_ref, vectors), around(ay_ref, vectors + 1))):
        w_ref[i] = w
    for b in range(vectors):
        q_ref[b] = around(k_ref.at[b], b)

    @pl.loop(0, count_ref[0])
    def _(_):
        for b in range(vectors):
            q_ref[b] = step(q_ref[b], w_ref[0], w_ref[1], w_ref[2], w_ref[3])

    row = lax.broadcasted_iota(jnp.int32, lo_ref.shape[1:], 0)
    for b in range(vectors):
        hi_ref[b] = jnp.where(row < TILE - STEPS, high_ref[b], q_ref[b, :TILE])
        lo_ref[b] = jnp.where(row < STEPS, q_ref[b, 2 * TILE :], low_ref[b])


def last_kernel(drift_ref, k_ref, mid_ref, lo_ref, hi_ref, rim_mid_ref, rim_hi_ref, product_ref, gram_ref):
    vectors, rows, cols = k_ref.shape
    total = DRIFT + rows
    by = lax.rem(drift_ref[0] + (total - DRIFT), total)
    for b in range(vectors):
        joined = jnp.concatenate(
            [rim_mid_ref[b], rim_hi_ref[b], lo_ref[b], mid_ref[b], hi_ref[b]], axis=0
        )
        product_ref[b] = k_ref[b] - pltpu.roll(joined, by, 0)[:rows]
    sums = []
    for a in range(vectors):
        for c in range(vectors):
            acc = jnp.sum((k_ref[a] * product_ref[c]).reshape(rows, cols // 128, 128), axis=1)
            sums.append(jnp.sum(acc, axis=0, keepdims=True))
    table = jnp.concatenate(sums, axis=0)
    ones = jnp.ones((gram_ref.shape[0], 128), jnp.float32)
    gram_ref[...] = lax.dot_general(
        ones, table, (((1,), (1,)), ((), ())),
        precision=lax.Precision.HIGHEST, preferred_element_type=jnp.float32,
    )


def call(kernel, outs, ins, scratch, flops):
    return pl.pallas_call(
        kernel,
        out_shape=[jax.ShapeDtypeStruct(o, jnp.float32) for o in outs],
        in_specs=ins,
        out_specs=[VMEM] * len(outs),
        scratch_shapes=[pltpu.VMEM(s, jnp.float32) for s in scratch],
        compiler_params=pltpu.CompilerParams(vmem_limit_bytes=LIMIT),
        cost_estimate=pl.CostEstimate(flops=flops, bytes_accessed=4 << 20, transcendentals=0),
    )


def body(krylov, advect_x, advect_y, step_counts, drifts):
    k, ax, ay = krylov[0], advect_x[0], advect_y[0]
    vectors, rows, cols = k.shape
    segs, strips = lax.axis_size("seg"), lax.axis_size("gx")
    fields = jnp.concatenate

    tail = fields([k[:, rows - STEPS :], ax[None, rows - STEPS :], ay[None, rows - STEPS :]], axis=0)
    head = fields([k[:, :STEPS], ax[None, :STEPS], ay[None, :STEPS]], axis=0)
    left = lax.ppermute(tail, "gx", shift_pairs(strips, 1))
    right = lax.ppermute(head, "gx", shift_pairs(strips, -1))
    drift = lax.ppermute(drifts, "seg", shift_pairs(segs, 1))

    flops = vectors * rows * cols * STEPS * 9
    mid, low, high = call(
        inner_kernel,
        [(vectors, rows - 2 * TILE, cols), (vectors, TILE, cols), (vectors, TILE, cols)],
        [SMEM, VMEM, VMEM, VMEM],
        [(vectors, rows, cols), (4, rows, cols)],
        flops,
    )(step_counts, k, ax, ay)
    onward = functools.partial(lax.ppermute, axis_name="seg", perm=shift_pairs(segs, 1))
    sideways = functools.partial(lax.ppermute, axis_name="gx", perm=shift_pairs(strips, 1))
    mid = onward(mid)
    lo, hi = call(
        outer_kernel,
        [(vectors, TILE, cols), (vectors, TILE, cols)],
        [SMEM] + [VMEM] * 7,
        [(vectors, 3 * TILE, cols), (4, 3 * TILE, cols)],
        flops,
    )(step_counts, k, ax, ay, left, right, low, high)
    hi = onward(hi)
    lo = onward(lo)
    rim_mid = sideways(mid[:, -(DRIFT - TILE) :])
    rim_hi = sideways(hi)
    world = segs * strips
    product, gram = call(
        last_kernel,
        [k.shape, (world, vectors * vectors)],
        [SMEM] + [VMEM] * 6,
        [],
        flops,
    )(drift, k, mid, lo, hi, rim_mid, rim_hi)
    gram = lax.all_to_all(gram, ("seg", "gx"), 0, 0)
    cells = world * rows * cols
    gram = jnp.sum(gram, axis=0).reshape(vectors, vectors) / jnp.float32(cells)
    return product[None], gram


def solution(mesh):
    return jax.shard_map(
        body,
        mesh=mesh,
        in_specs=(
            P("seg", None, "gx", None),
            P("seg", "gx", None),
            P("seg", "gx", None),
            P("seg"),
            P("seg"),
        ),
        out_specs=(P("seg", None, "gx", None), P()),
        check_vma=False,
    )
```

time: 155 us -> 79.7 us (0.51)
  blocking collectives: 81.4 us -> 23.4 us
  starting transfers between devices: 23.3 us -> 8.9 us
  Pallas kernels: 0 us -> 10.1 us
  waiting for transfers between devices: 36.4 us -> 33 us
  matrix products: 3.24 us -> 0 us
  other arithmetic: 3.44 us -> 0.38 us
  local copies, waits for them, and re-layouts: 5.14 us -> 3.06 us
    psum x1 -> x0, blocking collectives: 81.4 us -> none  [body(): total = lax.psum(local_sum, ('seg', 'gx'))]
    all_to_all x0 -> x1, blocking collectives: none -> 23.4 us  [body(): gram = lax.all_to_all(gram, ('seg', 'gx'), 0, 0)]
    ppermute x10 -> x8, starting transfers between devices: 23.3 us -> 8.9 us  [the longest x1 4.46 us: body(): left = lax.ppermute(tail, 'gx', shift_pairs(strips, 1))]
    pallas_call x0 -> x3, Pallas kernels: none -> 10.1 us  [the longest x1 5.37 us: body(): call(last_kernel, [k.shape, (world, vectors * vectors)], [SMEM] + [VMEM]...]
    ppermute x10 -> x8, waiting for transfers between devices: 36.4 us -> 33 us  [the longest x1 18.6 us: body(): hi = onward(hi)]
    slice x9 -> x3, local copies, waits for them, and re-layouts: 4.46 us -> 1.15 us  [the longest x2 1.14 us: body(): head = fields([k[:, :STEPS], ax[None, :STEPS], ay[None, :STEPS]], axis=0)]
    dot_general x1 -> x0, matrix products: 3.24 us -> none  [body(): jnp.einsum('sbxy,scxy->bc', krylov, product, precision=lax.Precision.HIGH...]
    select_n x4 -> x0, other arithmetic: 3.04 us -> none  [body(): field = jnp.where(section < counts_full, stepped, field)]
  transfers between devices with their start and end apart: 10 -> 8, of which waited for: 9 -> 3; matrix products, arithmetic and copies ran while one was open for 2% -> 0% of each run, Pallas kernels for 0% -> 6%
where the time goes in v1:
time: 79.7 us; the launch traced here: 80.3 us
  waiting for transfers between devices  33 us (41%)
  blocking collectives  23.4 us (29%)
  Pallas kernels  10.1 us (13%)
  starting transfers between devices  8.9 us (11%)
  local copies, waits for them, and re-layouts  3.06 us (4%)
  between operations  1.4 us (2%)
    all_to_all x1, blocking collectives, body(): gram = lax.all_to_all(gram, ('seg', 'gx'), 0, 0)  23.4 us
    ppermute x1, waiting for transfers between devices, body(): hi = onward(hi)  18.6 us
    ppermute x1, waiting for transfers between devices, body(): right = lax.ppermute(head, 'gx', shift_pairs(strips, -1))  7.67 us
    ppermute x1, waiting for transfers between devices, body(): drift = lax.ppermute(drifts, 'seg', shift_pairs(segs, 1))  6.69 us
    pallas_call x1, Pallas kernels, body(): call(last_kernel, [k.shape, (world, vectors * vectors)], [SMEM] + [VMEM]...  5.37 us
    ppermute x1, starting transfers between devices, body(): left = lax.ppermute(tail, 'gx', shift_pairs(strips, 1))  4.46 us
    ppermute x1, starting transfers between devices, body(): rim_mid = sideways(mid[:, -(DRIFT - TILE):])  3.28 us
    pallas_call x1, Pallas kernels, body(): call(inner_kernel, [(vectors, rows - 2 * TILE, cols), (vectors, TILE, col...  2.66 us
  transfers between devices with their start and end apart: 8, of which 3 were waited for; matrix products, arithmetic and copies ran while one was open for 0% of the time, Pallas kernels for 6%

profile of v1, /device:TPU:1, one launch (start us, length us, event | category | flops | bytes accessed | tf_op | source)
XLA Modules:
  0.0 80.3 jit_solution(12935202430945665798)
XLA Ops:
  0.6 1.1 %fusion = (f32[8,4,1024]{2,1,0:T(4,128)S(1)}, f32[8,4,1024]{2,1,0:T(4,128)S(1)}) fusion(f32[8,32,1024]{2,1,0:T(8,128)} %bitcast.7), kind=kLoop, calls=%fused_computation.3 | loop fusion | bytes 524288 | tf_op jit(solution)/shard_map/slice | solution.py:127
  1.9 4.5 %collective-permute-start.2 = (f32[10,4,1024]{2,1,0:T(4,128)S(1)}, f32[10,4,1024]{2,1,0:T(4,128)S(1)}, u32[]{:S(2)}, u32[]{:S(2)}) collective-permute-start(f32[10,4,1024]{2,1,0:T(4,128)S(1)} %pad_maximum_fusion), channel_id=1, source_target_pairs={{0,1},{1,2},{2,3},{3,4},{4,5},{5,6},{6,7},{7,0},{8,9},{9,10},{10,1... | collective-permute-start | bytes 491528 | tf_op jit(solution)/shard_map/ppermute | solution.py:128
  7.0 0.0 copy-start
  7.0 1.2 %copy-done = f32[1,8,32,1024]{3,2,1,0:T(8,128)S(1)} copy-done((f32[1,8,32,1024]{3,2,1,0:T(8,128)S(1)}, f32[1,8,32,1024]{3,2,1,0:T(8,128)}, u32[]{:S(2)}) %copy-start) | copy-done | bytes 1048600
  8.2 2.7 %shard_map.68 = (f32[8,16,1024]{2,1,0:T(8,128)S(1)}, f32[8,8,1024]{2,1,0:T(8,128)S(1)}, f32[8,8,1024]{2,1,0:T(8,128)S(1)}) custom-call(s32[1]{0:T(128)S(6)} %copy.8.count_ref, f32[8,32,1024]{2,1,0:T(8,128)S(1)} %bitcast.8, f32[32,1024]{1,0:T(8,128)S(1)} %bitcast.11, f32[32,1024]{1,0:T(8,128)S(1)} %bitcast.13), custom_call_target="tpu_custom_call" | custom-call | flops 9437184 | bytes 4194304 | tf_op jit(solution)/shard_map/pallas_call | solution.py:133
  10.9 0.1 collective-permute-start.1
  11.1 0.1 collective-permute-start.3
  11.1 0.0 collective-permute-done.2.left_ref
  11.2 7.7 %collective-permute-done.3.right_ref = f32[10,4,1024]{2,1,0:T(4,128)S(1)} collective-permute-done((f32[10,4,1024]{2,1,0:T(4,128)S(1)}, f32[10,4,1024]{2,1,0:T(4,128)S(1)}, u32[]{:S(2)}, u32[]{:S(2)}) %collective-permute-start.3) | collective-permute-done | bytes 163872 | tf_op jit(solution)/shard_map/ppermute | solution.py:129
  18.8 2.1 %shard_map.69 = (f32[8,8,1024]{2,1,0:T(8,128)S(1)}, f32[8,8,1024]{2,1,0:T(8,128)S(1)}) custom-call(s32[1]{0:T(128)S(6)} %copy.8.count_ref, f32[8,32,1024]{2,1,0:T(8,128)S(1)} %bitcast.9, f32[32,1024]{1,0:T(8,128)S(1)} %bitcast.12, f32[32,1024]{1,0:T(8,128)S(1)} %bitcast.14, f32[10,4,1024]{2,1,0:T(4,128)S(1)} %collective-permute-done.2.left_ref, ...), custom_call_target="tpu_custom_call" | custom-call | flops 9437184 | bytes 4194304 | tf_op jit(solution)/shard_map/pallas_call | solution.py:143
  20.9 0.9 %collective-permute-start.5 = (f32[8,8,1024]{2,1,0:T(8,128)S(1)}, f32[8,8,1024]{2,1,0:T(8,128)S(1)}, u32[]{:S(2)}, u32[]{:S(2)}) collective-permute-start(f32[8,8,1024]{2,1,0:T(8,128)S(1)} %get-tuple-element.13), channel_id=1, source_target_pairs={{0,8},{8,16},{16,24},{24,32},{32,40},{40,48},{48,56},{56,64},{64,7... | collective-permute-start | bytes 786440 | tf_op jit(solution)/shard_map/ppermute | solution.py:150
  21.8 0.1 collective-permute-start.4
  21.9 18.6 %collective-permute-done.5.hi_ref = f32[8,8,1024]{2,1,0:T(8,128)S(1)} collective-permute-done((f32[8,8,1024]{2,1,0:T(8,128)S(1)}, f32[8,8,1024]{2,1,0:T(8,128)S(1)}, u32[]{:S(2)}, u32[]{:S(2)}) %collective-permute-start.5) | collective-permute-done | bytes 262176 | tf_op jit(solution)/shard_map/ppermute | solution.py:150
  40.5 0.0 collective-permute-start.7
  40.5 3.3 %collective-permute-start.6 = (f32[8,8,1024]{2,1,0:T(8,128)S(1)}, f32[8,8,1024]{2,1,0:T(8,128)S(1)}, u32[]{:S(2)}, u32[]{:S(2)}) collective-permute-start(f32[8,8,1024]{2,1,0:T(8,128)S(1)} %slice.34), channel_id=1, source_target_pairs={{0,1},{1,2},{2,3},{3,4},{4,5},{5,6},{6,7},{7,0},{8,9},{9,10},{10,1... | collective-permute-start | bytes 786440 | tf_op jit(solution)/shard_map/ppermute | solution.py:152
  43.8 0.0 collective-permute-start
  43.8 6.7 %collective-permute-done.drift_ref = s32[1]{0:T(128)} collective-permute-done((s32[1]{0:T(128)}, s32[1]{0:T(128)}, u32[]{:S(2)}, u32[]{:S(2)}) %collective-permute-start) | collective-permute-done | bytes 36 | tf_op jit(solution)/shard_map/ppermute | solution.py:130
  50.5 0.0 collective-permute-done.4.lo_ref
  50.5 0.0 collective-permute-done.7.rim_hi_ref
  50.5 0.0 collective-permute-done.6.rim_mid_ref
  50.5 5.4 %shard_map.70 = (f32[8,32,1024]{2,1,0:T(8,128)}, f32[256,64]{1,0:T(8,128)S(1)}) custom-call(s32[1]{0:T(128)} %collective-permute-done.drift_ref, f32[8,32,1024]{2,1,0:T(8,128)S(1)} %bitcast.10, f32[8,16,1024]{2,1,0:T(8,128)S(1)} %collective-permute-done.1.mid_ref, f32[8,8,1024]{2,1,0:T(8,128)S(1)} %collective-permute-done.4.lo_ref, ...), custom_call_target="tpu_custom_call" | custom-call | flops 9437184 | bytes 4194304 | tf_op jit(solution)/shard_map/pallas_call | solution.py:155
  55.9 23.4 %all_to_all.9 = f32[256,1,64]{2,1,0:T(1,128)S(1)} all-to-all(f32[256,1,64]{2,1,0:T(1,128)S(1)} %bitcast.15), channel_id=1, replica_groups=mesh['seg'=32,'gx'=8] {'seg','gx'}, dimensions={0} | all-to-all | bytes 131072 | tf_op jit(solution)/shard_map/all_to_all | solution.py:162
  79.3 0.3 reduce_sum.9
  79.6 0.7 div.10
  (10 shorter events, 0.1 us)
Async XLA Ops:
  0.6 1.2 %copy-start.1 = (f32[1,32,1024]{2,1,0:T(8,128)S(1)}, f32[1,32,1024]{2,1,0:T(8,128)}, u32[]{:S(2)}) copy-start(f32[1,32,1024]{2,1,0:T(8,128)} %param.6) | copy-start | bytes 393220
  0.6 1.2 %copy-start.2 = (f32[1,32,1024]{2,1,0:T(8,128)S(1)}, f32[1,32,1024]{2,1,0:T(8,128)}, u32[]{:S(2)}) copy-start(f32[1,32,1024]{2,1,0:T(8,128)} %param.7) | copy-start | bytes 393220
  1.9 9.3 %collective-permute-start.2 = (f32[10,4,1024]{2,1,0:T(4,128)S(1)}, f32[10,4,1024]{2,1,0:T(4,128)S(1)}, u32[]{:S(2)}, u32[]{:S(2)}) collective-permute-start(f32[10,4,1024]{2,1,0:T(4,128)S(1)} %pad_maximum_fusion), channel_id=1, source_target_pairs={{0,1},{1,2},{2,3},{3,4},{4,5},{5,6},{6,7},{7,0},{8,9},{9,10},{10,1... | collective-permute-start | bytes 491528 | tf_op jit(solution)/shard_map/ppermute | solution.py:128
  7.0 1.2 %copy-start = (f32[1,8,32,1024]{3,2,1,0:T(8,128)S(1)}, f32[1,8,32,1024]{3,2,1,0:T(8,128)}, u32[]{:S(2)}) copy-start(f32[1,8,32,1024]{3,2,1,0:T(8,128)} %param.5) | copy-start | bytes 3145732
  10.9 29.6 %collective-permute-start.1 = (f32[8,16,1024]{2,1,0:T(8,128)S(1)}, f32[8,16,1024]{2,1,0:T(8,128)S(1)}, u32[]{:S(2)}, u32[]{:S(2)}) collective-permute-start(f32[8,16,1024]{2,1,0:T(8,128)S(1)} %get-tuple-element.9), channel_id=1, source_target_pairs={{0,8},{8,16},{16,24},{24,32},{32,40},{40,48},{48,56},{56,64},{64,7... | collective-permute-start | bytes 1572872 | tf_op jit(solution)/shard_map/ppermute | solution.py:142
  11.1 7.8 %collective-permute-start.3 = (f32[10,4,1024]{2,1,0:T(4,128)S(1)}, f32[10,4,1024]{2,1,0:T(4,128)S(1)}, u32[]{:S(2)}, u32[]{:S(2)}) collective-permute-start(f32[10,4,1024]{2,1,0:T(4,128)S(1)} %pad_maximum_fusion.1), channel_id=1, source_target_pairs={{0,7},{1,0},{2,1},{3,2},{4,3},{5,4},{6,5},{7,6},{8,15},{9,8},{10,9... | collective-permute-start | bytes 491528 | tf_op jit(solution)/shard_map/ppermute | solution.py:129
  20.9 19.6 %collective-permute-start.5 = (f32[8,8,1024]{2,1,0:T(8,128)S(1)}, f32[8,8,1024]{2,1,0:T(8,128)S(1)}, u32[]{:S(2)}, u32[]{:S(2)}) collective-permute-start(f32[8,8,1024]{2,1,0:T(8,128)S(1)} %get-tuple-element.13), channel_id=1, source_target_pairs={{0,8},{8,16},{16,24},{24,32},{32,40},{40,48},{48,56},{56,64},{64,7... | collective-permute-start | bytes 786440 | tf_op jit(solution)/shard_map/ppermute | solution.py:150
  21.8 28.7 %collective-permute-start.4 = (f32[8,8,1024]{2,1,0:T(8,128)S(1)}, f32[8,8,1024]{2,1,0:T(8,128)S(1)}, u32[]{:S(2)}, u32[]{:S(2)}) collective-permute-start(f32[8,8,1024]{2,1,0:T(8,128)S(1)} %get-tuple-element.12), channel_id=1, source_target_pairs={{0,8},{8,16},{16,24},{24,32},{32,40},{40,48},{48,56},{56,64},{64,7... | collective-permute-start | bytes 786440 | tf_op jit(solution)/shard_map/ppermute | solution.py:151
  40.5 10.0 %collective-permute-start.7 = (f32[8,8,1024]{2,1,0:T(8,128)S(1)}, f32[8,8,1024]{2,1,0:T(8,128)S(1)}, u32[]{:S(2)}, u32[]{:S(2)}) collective-permute-start(f32[8,8,1024]{2,1,0:T(8,128)S(1)} %collective-permute-done.5.hi_ref), channel_id=1, source_target_pairs={{0,1},{1,2},{2,3},{3,4},{4,5},{5,6},{6,7},{7,0},{8,9},{9,10},{10,1... | collective-permute-start | bytes 786440 | tf_op jit(solution)/shard_map/ppermute | solution.py:153
  40.5 10.0 %collective-permute-start.6 = (f32[8,8,1024]{2,1,0:T(8,128)S(1)}, f32[8,8,1024]{2,1,0:T(8,128)S(1)}, u32[]{:S(2)}, u32[]{:S(2)}) collective-permute-start(f32[8,8,1024]{2,1,0:T(8,128)S(1)} %slice.34), channel_id=1, source_target_pairs={{0,1},{1,2},{2,3},{3,4},{4,5},{5,6},{6,7},{7,0},{8,9},{9,10},{10,1... | collective-permute-start | bytes 786440 | tf_op jit(solution)/shard_map/ppermute | solution.py:152
  43.8 6.7 %collective-permute-start = (s32[1]{0:T(128)}, s32[1]{0:T(128)}, u32[]{:S(2)}, u32[]{:S(2)}) collective-permute-start(s32[1]{0:T(128)} %param.9), channel_id=1, source_target_pairs={{0,8},{8,16},{16,24},{24,32},{32,40},{40,48},{48,56},{56,64},{64,7... | collective-permute-start | bytes 20 | tf_op jit(solution)/shard_map/ppermute | solution.py:130

commit v2 on v1

--- a/solution.py
+++ b/solution.py
@@ -83,8 +83,59 @@
         lo_ref[b] = jnp.where(row < STEPS, q_ref[b, 2 * TILE :], low_ref[b])
 
 
-def last_kernel(drift_ref, k_ref, mid_ref, lo_ref, hi_ref, rim_mid_ref, rim_hi_ref, product_ref, gram_ref):
+def pair_sums(left, right, blocks, vectors, cols):
+    sums = []
+    half = vectors // 2
+    for first in range(0, vectors, half):
+        accs = {}
+        for block in range(blocks):
+            for lane in range(0, cols, 128):
+                rs = [right(c, block, lane) for c in range(vectors)]
+                for a in range(first, first + half):
+                    value = left(a, block, lane)
+                    for c in range(vectors):
+                        term = value * rs[c]
+                        accs[a, c] = accs[a, c] + term if (a, c) in accs else term
+        sums += [jnp.sum(accs[a, c], axis=0, keepdims=True) for a in range(first, first + half) for c in range(vectors)]
+    return jnp.concatenate(sums, axis=0)
+
+
+def tile_of(ref, v, block, lane):
+    return ref[v, block * TILE : (block + 1) * TILE, lane : lane + 128]
+
+
+def own_kernel(k_ref, table_ref):
     vectors, rows, cols = k_ref.shape
+    tile = functools.partial(tile_of, k_ref)
+    table_ref[...] = pair_sums(tile, tile, rows // TILE, vectors, cols)
+
+
+def gram_kernel(drift_ref, k_ref, beyond_ref, lo_ref, mid_ref, hi_ref, own_ref, gram_ref, shifted_ref):
+    vectors, rows, cols = k_ref.shape
+    total = rows + beyond_ref.shape[1]
+    by = lax.rem(total - drift_ref[0], total)
+    for b in range(vectors):
+        joined = jnp.concatenate([k_ref[b], beyond_ref[b]], axis=0)
+        shifted_ref[b] = pltpu.roll(joined, by, 0)[:rows]
+    blocks = rows // TILE
+
+    def arrived(c, block, lane):
+        if block == 0:
+            return tile_of(lo_ref, c, 0, lane)
+        if block == blocks - 1:
+            return tile_of(hi_ref, c, 0, lane)
+        return tile_of(mid_ref, c, block - 1, lane)
+
+    table = own_ref[...] - pair_sums(functools.partial(tile_of, shifted_ref), arrived, blocks, vectors, cols)
+    ones = jnp.ones((gram_ref.shape[0], 128), jnp.float32)
+    gram_ref[...] = lax.dot_general(
+        ones, table, (((1,), (1,)), ((), ())),
+        precision=lax.Precision.HIGHEST, preferred_element_type=jnp.float32,
+    )
+
+
+def last_kernel(drift_ref, k_ref, mid_ref, lo_ref, hi_ref, rim_mid_ref, rim_hi_ref, product_ref):
+    vectors, rows, _ = k_ref.shape
     total = DRIFT + rows
     by = lax.rem(drift_ref[0] + (total - DRIFT), total)
     for b in range(vectors):
@@ -92,20 +143,9 @@
             [rim_mid_ref[b], rim_hi_ref[b], lo_ref[b], mid_ref[b], hi_ref[b]], axis=0
         )
         product_ref[b] = k_ref[b] - pltpu.roll(joined, by, 0)[:rows]
-    sums = []
-    for a in range(vectors):
-        for c in range(vectors):
-            acc = jnp.sum((k_ref[a] * product_ref[c]).reshape(rows, cols // 128, 128), axis=1)
-            sums.append(jnp.sum(acc, axis=0, keepdims=True))
-    table = jnp.concatenate(sums, axis=0)
-    ones = jnp.ones((gram_ref.shape[0], 128), jnp.float32)
-    gram_ref[...] = lax.dot_general(
-        ones, table, (((1,), (1,)), ((), ())),
-        precision=lax.Precision.HIGHEST, preferred_element_type=jnp.float32,
-    )
-
-
-def call(kernel, outs, ins, scratch, flops):
+
+
+def call(kernel, outs, ins, scratch, cost):
     return pl.pallas_call(
         kernel,
         out_shape=[jax.ShapeDtypeStruct(o, jnp.float32) for o in outs],
@@ -113,7 +153,7 @@
         out_specs=[VMEM] * len(outs),
         scratch_shapes=[pltpu.VMEM(s, jnp.float32) for s in scratch],
         compiler_params=pltpu.CompilerParams(vmem_limit_bytes=LIMIT),
-        cost_estimate=pl.CostEstimate(flops=flops, bytes_accessed=4 << 20, transcendentals=0),
+        cost_estimate=pl.CostEstimate(flops=cost << 30, bytes_accessed=4 << 20, transcendentals=0),
     )
 
 
@@ -125,17 +165,19 @@
 
     tail = fields([k[:, rows - STEPS :], ax[None, rows - STEPS :], ay[None, rows - STEPS :]], axis=0)
     head = fields([k[:, :STEPS], ax[None, :STEPS], ay[None, :STEPS]], axis=0)
+    beyond = k[:, :DRIFT]
+    tail, head, beyond, k, ax, ay = lax.optimization_barrier((tail, head, beyond, k, ax, ay))
+    right = lax.ppermute(head, "gx", shift_pairs(strips, -1))
     left = lax.ppermute(tail, "gx", shift_pairs(strips, 1))
-    right = lax.ppermute(head, "gx", shift_pairs(strips, -1))
     drift = lax.ppermute(drifts, "seg", shift_pairs(segs, 1))
-
-    flops = vectors * rows * cols * STEPS * 9
+    beyond = lax.ppermute(beyond, "gx", shift_pairs(strips, -1))
+
     mid, low, high = call(
         inner_kernel,
         [(vectors, rows - 2 * TILE, cols), (vectors, TILE, cols), (vectors, TILE, cols)],
         [SMEM, VMEM, VMEM, VMEM],
         [(vectors, rows, cols), (4, rows, cols)],
-        flops,
+        64,
     )(step_counts, k, ax, ay)
     onward = functools.partial(lax.ppermute, axis_name="seg", perm=shift_pairs(segs, 1))
     sideways = functools.partial(lax.ppermute, axis_name="gx", perm=shift_pairs(strips, 1))
@@ -145,21 +187,24 @@
         [(vectors, TILE, cols), (vectors, TILE, cols)],
         [SMEM] + [VMEM] * 7,
         [(vectors, 3 * TILE, cols), (4, 3 * TILE, cols)],
-        flops,
+        64,
     )(step_counts, k, ax, ay, left, right, low, high)
+    pairs = vectors * vectors
+    hi, kept = lax.optimization_barrier((hi, k))
     hi = onward(hi)
     lo = onward(lo)
+    (own,) = call(own_kernel, [(pairs, 128)], [VMEM], [], 4)(kept)
     rim_mid = sideways(mid[:, -(DRIFT - TILE) :])
     rim_hi = sideways(hi)
     world = segs * strips
-    product, gram = call(
-        last_kernel,
-        [k.shape, (world, vectors * vectors)],
-        [SMEM] + [VMEM] * 6,
-        [],
-        flops,
-    )(drift, k, mid, lo, hi, rim_mid, rim_hi)
+    (gram,) = call(
+        gram_kernel, [(world, pairs)], [SMEM] + [VMEM] * 6, [k.shape], 4
+    )(drift, k, beyond, lo, mid, hi, own)
     gram = lax.all_to_all(gram, ("seg", "gx"), 0, 0)
+    gram, rim_mid, rim_hi = lax.optimization_barrier((gram, rim_mid, rim_hi))
+    (product,) = call(last_kernel, [k.shape], [SMEM] + [VMEM] * 6, [], 4)(
+        drift, k, mid, lo, hi, rim_mid, rim_hi
+    )
     cells = world * rows * cols
     gram = jnp.sum(gram, axis=0).reshape(vectors, vectors) / jnp.float32(cells)
     return product[None], gram

time: 79.7 us -> 79.2 us (level)
  starting transfers between devices: 8.9 us -> 19.9 us
  waiting for transfers between devices: 33 us -> 25.3 us
  Pallas kernels: 10.1 us -> 7.61 us
  blocking collectives: 23.4 us -> 21.7 us
    ppermute x1, starting transfers between devices: 0.01 us -> 7.06 us  [body(): rim_hi = sideways(hi)]
    ppermute x1, waiting for transfers between devices: 6.69 us -> 0.01 us  [body(): drift = lax.ppermute(drifts, 'seg', shift_pairs(segs, 1))]
    ppermute x1, waiting for transfers between devices: 7.67 us -> 2.19 us  [body(): right = lax.ppermute(head, 'gx', shift_pairs(strips, -1))]
    ppermute x1, waiting for transfers between devices: 18.6 us -> 23.1 us  [body(): hi = onward(hi)]
    ppermute x1, starting transfers between devices: 3.28 us -> 0.08 us  [body(): rim_mid = sideways(mid[:, -(DRIFT - TILE):])]
    ppermute x0 -> x1, starting transfers between devices: none -> 2.67 us  [body(): beyond = lax.ppermute(beyond, 'gx', shift_pairs(strips, -1))]
    ppermute x1, starting transfers between devices: 0.01 us -> 2.2 us  [body(): drift = lax.ppermute(drifts, 'seg', shift_pairs(segs, 1))]
    ppermute x1, starting transfers between devices: 0.13 us -> 2 us  [body(): mid = onward(mid)]
  transfers between devices with their start and end apart: 8 -> 9, of which waited for: 3 -> 2; matrix products, arithmetic and copies ran while one was open for 0% -> 3% of each run, Pallas kernels for 6% -> 7%
where the time goes in v2:
time: 79.2 us; the launch traced here: 79.1 us
  waiting for transfers between devices  25.3 us (32%)
  blocking collectives  21.7 us (27%)
  starting transfers between devices  19.9 us (25%)
  Pallas kernels  7.61 us (10%)
  local copies, waits for them, and re-layouts  3.02 us (4%)
  between operations  1.42 us (2%)
    ppermute x1, waiting for transfers between devices, body(): hi = onward(hi)  23.1 us
    all_to_all x1, blocking collectives, body(): gram = lax.all_to_all(gram, ('seg', 'gx'), 0, 0)  21.7 us
    ppermute x1, starting transfers between devices, body(): rim_hi = sideways(hi)  7.06 us
    ppermute x1, starting transfers between devices, body(): left = lax.ppermute(tail, 'gx', shift_pairs(strips, 1))  3.91 us
    ppermute x1, starting transfers between devices, body(): beyond = lax.ppermute(beyond, 'gx', shift_pairs(strips, -1))  2.67 us
    ppermute x1, starting transfers between devices, body(): drift = lax.ppermute(drifts, 'seg', shift_pairs(segs, 1))  2.2 us
    ppermute x1, waiting for transfers between devices, body(): right = lax.ppermute(head, 'gx', shift_pairs(strips, -1))  2.19 us
    pallas_call x1, Pallas kernels, body(): call(inner_kernel, [(vectors, rows - 2 * TILE, cols), (vectors, TILE, col...  2.04 us
  transfers between devices with their start and end apart: 9, of which 2 were waited for; matrix products, arithmetic and copies ran while one was open for 3% of the time, Pallas kernels for 7%

profile of v2, /device:TPU:1, one launch (start us, length us, event | category | flops | bytes accessed | tf_op | source)
XLA Modules:
  0.0 79.1 jit_solution(10635811549693503036)
XLA Ops:
  0.6 2.2 %collective-permute-start = (s32[1]{0:T(128)}, s32[1]{0:T(128)}, u32[]{:S(2)}, u32[]{:S(2)}) collective-permute-start(s32[1]{0:T(128)} %param.9), channel_id=1, source_target_pairs={{0,8},{8,16},{16,24},{24,32},{32,40},{40,48},{48,56},{56,64},{64,7... | collective-permute-start | bytes 20 | tf_op jit(solution)/shard_map/ppermute | solution.py:172
  2.8 1.1 %fusion = (f32[8,4,1024]{2,1,0:T(4,128)S(1)}, f32[8,4,1024]{2,1,0:T(4,128)S(1)}) fusion(f32[8,32,1024]{2,1,0:T(8,128)} %bitcast.8), kind=kLoop, calls=%fused_computation.3 | loop fusion | bytes 524288 | tf_op jit(solution)/shard_map/slice | solution.py:167
  4.0 0.0 copy-start
  4.0 1.2 %slice.38 = f32[8,16,1024]{2,1,0:T(8,128)S(1)} slice(f32[8,32,1024]{2,1,0:T(8,128)} %bitcast.9), slice={[0:8], [0:16], [0:1024]} | slice | bytes 1048576 | tf_op jit(solution)/shard_map/slice | solution.py:168
  5.2 0.1 pad_maximum_fusion
  5.3 3.9 %collective-permute-start.2 = (f32[10,4,1024]{2,1,0:T(4,128)S(1)}, f32[10,4,1024]{2,1,0:T(4,128)S(1)}, u32[]{:S(2)}, u32[]{:S(2)}) collective-permute-start(f32[10,4,1024]{2,1,0:T(4,128)S(1)} %get-tuple-element.22), channel_id=1, source_target_pairs={{0,1},{1,2},{2,3},{3,4},{4,5},{5,6},{6,7},{7,0},{8,9},{9,10},{10,1... | collective-permute-start | bytes 491528 | tf_op jit(solution)/shard_map/ppermute | solution.py:171
  9.2 0.0 collective-permute-start.3
  9.2 2.7 %collective-permute-start.6 = (f32[8,16,1024]{2,1,0:T(8,128)S(1)}, f32[8,16,1024]{2,1,0:T(8,128)S(1)}, u32[]{:S(2)}, u32[]{:S(2)}) collective-permute-start(f32[8,16,1024]{2,1,0:T(8,128)S(1)} %slice.38), channel_id=1, source_target_pairs={{0,7},{1,0},{2,1},{3,2},{4,3},{5,4},{6,5},{7,6},{8,15},{9,8},{10,9... | collective-permute-start | bytes 1572872 | tf_op jit(solution)/shard_map/ppermute | solution.py:173
  12.6 2.0 %shard_map.68 = (f32[8,16,1024]{2,1,0:T(8,128)S(1)}, f32[8,8,1024]{2,1,0:T(8,128)S(1)}, f32[8,8,1024]{2,1,0:T(8,128)S(1)}) custom-call(s32[1]{0:T(128)S(6)} %copy.8.count_ref, f32[8,32,1024]{2,1,0:T(8,128)S(1)} %bitcast.10, f32[32,1024]{1,0:T(8,128)S(1)} %bitcast.16, f32[32,1024]{1,0:T(8,128)S(1)} %bitcast.18), custom_call_target="tpu_custom_call" | custom-call | flops 68719476736 | bytes 4194304 | tf_op jit(solution)/shard_map/pallas_call | solution.py:175
  14.6 2.0 %collective-permute-start.1 = (f32[8,16,1024]{2,1,0:T(8,128)S(1)}, f32[8,16,1024]{2,1,0:T(8,128)S(1)}, u32[]{:S(2)}, u32[]{:S(2)}) collective-permute-start(f32[8,16,1024]{2,1,0:T(8,128)S(1)} %get-tuple-element.21), channel_id=1, source_target_pairs={{0,8},{8,16},{16,24},{24,32},{32,40},{40,48},{48,56},{56,64},{64,7... | collective-permute-start | bytes 1572872 | tf_op jit(solution)/shard_map/ppermute | solution.py:184
  16.6 2.2 %collective-permute-done.3.right_ref = f32[10,4,1024]{2,1,0:T(4,128)S(1)} collective-permute-done((f32[10,4,1024]{2,1,0:T(4,128)S(1)}, f32[10,4,1024]{2,1,0:T(4,128)S(1)}, u32[]{:S(2)}, u32[]{:S(2)}) %collective-permute-start.3) | collective-permute-done | bytes 163872 | tf_op jit(solution)/shard_map/ppermute | solution.py:170
  18.8 1.6 %shard_map.69 = (f32[8,8,1024]{2,1,0:T(8,128)S(1)}, f32[8,8,1024]{2,1,0:T(8,128)S(1)}) custom-call(s32[1]{0:T(128)S(6)} %copy.8.count_ref, f32[8,32,1024]{2,1,0:T(8,128)S(1)} %bitcast.11, f32[32,1024]{1,0:T(8,128)S(1)} %bitcast.17, f32[32,1024]{1,0:T(8,128)S(1)} %bitcast.19, f32[10,4,1024]{2,1,0:T(4,128)S(1)} %collective-permute-done.2.left_ref, ...), custom_call_target="tpu_custom_call" | custom-call | flops 68719476736 | bytes 4194304 | tf_op jit(solution)/shard_map/pallas_call | solution.py:185
  20.4 1.9 %collective-permute-start.5 = (f32[8,8,1024]{2,1,0:T(8,128)S(1)}, f32[8,8,1024]{2,1,0:T(8,128)S(1)}, u32[]{:S(2)}, u32[]{:S(2)}) collective-permute-start(f32[8,8,1024]{2,1,0:T(8,128)S(1)} %get-tuple-element.28), channel_id=1, source_target_pairs={{0,8},{8,16},{16,24},{24,32},{32,40},{40,48},{48,56},{56,64},{64,7... | collective-permute-start | bytes 786440 | tf_op jit(solution)/shard_map/ppermute | solution.py:194
  22.2 0.1 collective-permute-start.4
  22.3 0.4 shard_map.70.own_ref
  22.7 23.1 %collective-permute-done.5.hi_ref = f32[8,8,1024]{2,1,0:T(8,128)S(1)} collective-permute-done((f32[8,8,1024]{2,1,0:T(8,128)S(1)}, f32[8,8,1024]{2,1,0:T(8,128)S(1)}, u32[]{:S(2)}, u32[]{:S(2)}) %collective-permute-start.5) | collective-permute-done | bytes 262176 | tf_op jit(solution)/shard_map/ppermute | solution.py:194
  45.8 7.1 %collective-permute-start.8 = (f32[8,8,1024]{2,1,0:T(8,128)S(1)}, f32[8,8,1024]{2,1,0:T(8,128)S(1)}, u32[]{:S(2)}, u32[]{:S(2)}) collective-permute-start(f32[8,8,1024]{2,1,0:T(8,128)S(1)} %collective-permute-done.5.hi_ref), channel_id=1, source_target_pairs={{0,1},{1,2},{2,3},{3,4},{4,5},{5,6},{6,7},{7,0},{8,9},{9,10},{10,1... | collective-permute-start | bytes 786440 | tf_op jit(solution)/shard_map/ppermute | solution.py:198
  52.9 0.1 collective-permute-start.7
  53.0 0.0 collective-permute-done.6.beyond_ref
  53.0 1.7 %shard_map.71 = f32[256,64]{1,0:T(8,128)S(1)} custom-call(s32[1]{0:T(128)} %collective-permute-done.drift_ref, f32[8,32,1024]{2,1,0:T(8,128)S(1)} %bitcast.13, f32[8,16,1024]{2,1,0:T(8,128)S(1)} %collective-permute-done.6.beyond_ref, f32[8,8,1024]{2,1,0:T(8,128)S(1)} %collective-permute-done.4.lo_ref, f32[8,16,1024]{2,1,0:T(8,128)S(1)} %collective-permute-done.1.mid_ref, ...), custom_call_target="tpu_custom_call" | custom-call | flops 4294967296 | bytes 4194304 | tf_op jit(solution)/shard_map/pallas_call | solution.py:200
  54.8 21.7 %all_to_all.12 = f32[256,1,64]{2,1,0:T(1,128)S(1)} all-to-all(f32[256,1,64]{2,1,0:T(1,128)S(1)} %bitcast.15), channel_id=1, replica_groups=mesh['seg'=32,'gx'=8] {'seg','gx'}, dimensions={0} | all-to-all | bytes 131072 | tf_op jit(solution)/shard_map/all_to_all | solution.py:203
  76.4 0.1 reduce_sum.9
  76.5 0.7 div.10
  77.2 1.9 %shard_map.72 = f32[8,32,1024]{2,1,0:T(8,128)} custom-call(s32[1]{0:T(128)} %collective-permute-done.drift_ref, f32[8,32,1024]{2,1,0:T(8,128)S(1)} %bitcast.14, f32[8,16,1024]{2,1,0:T(8,128)S(1)} %collective-permute-done.1.mid_ref, f32[8,8,1024]{2,1,0:T(8,128)S(1)} %collective-permute-done.4.lo_ref, f32[8,8,1024]{2,1,0:T(8,128)S(1)} %collective-permute-done.5.hi_ref, ...), custom_call_target="tpu_custom_call" | custom-call | flops 4294967296 | bytes 4194304 | tf_op jit(solution)/shard_map/pallas_call | solution.py:205
  (15 shorter events, 0.1 us)
Async XLA Ops:
  0.6 52.4 %collective-permute-start = (s32[1]{0:T(128)}, s32[1]{0:T(128)}, u32[]{:S(2)}, u32[]{:S(2)}) collective-permute-start(s32[1]{0:T(128)} %param.9), channel_id=1, source_target_pairs={{0,8},{8,16},{16,24},{24,32},{32,40},{40,48},{48,56},{56,64},{64,7... | collective-permute-start | bytes 20 | tf_op jit(solution)/shard_map/ppermute | solution.py:172
  2.8 2.3 %copy-start.1 = (f32[1,32,1024]{2,1,0:T(8,128)S(1)}, f32[1,32,1024]{2,1,0:T(8,128)}, u32[]{:S(2)}) copy-start(f32[1,32,1024]{2,1,0:T(8,128)} %param.6) | copy-start | bytes 393220
  2.8 2.4 %copy-start.2 = (f32[1,32,1024]{2,1,0:T(8,128)S(1)}, f32[1,32,1024]{2,1,0:T(8,128)}, u32[]{:S(2)}) copy-start(f32[1,32,1024]{2,1,0:T(8,128)} %param.7) | copy-start | bytes 393220
  4.0 8.6 %copy-start = (f32[1,8,32,1024]{3,2,1,0:T(8,128)S(1)}, f32[1,8,32,1024]{3,2,1,0:T(8,128)}, u32[]{:S(2)}) copy-start(f32[1,8,32,1024]{3,2,1,0:T(8,128)} %param.5) | copy-start | bytes 3145732
  5.3 11.3 %collective-permute-start.2 = (f32[10,4,1024]{2,1,0:T(4,128)S(1)}, f32[10,4,1024]{2,1,0:T(4,128)S(1)}, u32[]{:S(2)}, u32[]{:S(2)}) collective-permute-start(f32[10,4,1024]{2,1,0:T(4,128)S(1)} %get-tuple-element.22), channel_id=1, source_target_pairs={{0,1},{1,2},{2,3},{3,4},{4,5},{5,6},{6,7},{7,0},{8,9},{9,10},{10,1... | collective-permute-start | bytes 491528 | tf_op jit(solution)/shard_map/ppermute | solution.py:171
  9.2 9.6 %collective-permute-start.3 = (f32[10,4,1024]{2,1,0:T(4,128)S(1)}, f32[10,4,1024]{2,1,0:T(4,128)S(1)}, u32[]{:S(2)}, u32[]{:S(2)}) collective-permute-start(f32[10,4,1024]{2,1,0:T(4,128)S(1)} %get-tuple-element.23), channel_id=1, source_target_pairs={{0,7},{1,0},{2,1},{3,2},{4,3},{5,4},{6,5},{7,6},{8,15},{9,8},{10,9... | collective-permute-start | bytes 491528 | tf_op jit(solution)/shard_map/ppermute | solution.py:170
  9.2 43.8 %collective-permute-start.6 = (f32[8,16,1024]{2,1,0:T(8,128)S(1)}, f32[8,16,1024]{2,1,0:T(8,128)S(1)}, u32[]{:S(2)}, u32[]{:S(2)}) collective-permute-start(f32[8,16,1024]{2,1,0:T(8,128)S(1)} %slice.38), channel_id=1, source_target_pairs={{0,7},{1,0},{2,1},{3,2},{4,3},{5,4},{6,5},{7,6},{8,15},{9,8},{10,9... | collective-permute-start | bytes 1572872 | tf_op jit(solution)/shard_map/ppermute | solution.py:173
  14.6 38.3 %collective-permute-start.1 = (f32[8,16,1024]{2,1,0:T(8,128)S(1)}, f32[8,16,1024]{2,1,0:T(8,128)S(1)}, u32[]{:S(2)}, u32[]{:S(2)}) collective-permute-start(f32[8,16,1024]{2,1,0:T(8,128)S(1)} %get-tuple-element.21), channel_id=1, source_target_pairs={{0,8},{8,16},{16,24},{24,32},{32,40},{40,48},{48,56},{56,64},{64,7... | collective-permute-start | bytes 1572872 | tf_op jit(solution)/shard_map/ppermute | solution.py:184
  20.4 25.4 %collective-permute-start.5 = (f32[8,8,1024]{2,1,0:T(8,128)S(1)}, f32[8,8,1024]{2,1,0:T(8,128)S(1)}, u32[]{:S(2)}, u32[]{:S(2)}) collective-permute-start(f32[8,8,1024]{2,1,0:T(8,128)S(1)} %get-tuple-element.28), channel_id=1, source_target_pairs={{0,8},{8,16},{16,24},{24,32},{32,40},{40,48},{48,56},{56,64},{64,7... | collective-permute-start | bytes 786440 | tf_op jit(solution)/shard_map/ppermute | solution.py:194
  22.2 30.8 %collective-permute-start.4 = (f32[8,8,1024]{2,1,0:T(8,128)S(1)}, f32[8,8,1024]{2,1,0:T(8,128)S(1)}, u32[]{:S(2)}, u32[]{:S(2)}) collective-permute-start(f32[8,8,1024]{2,1,0:T(8,128)S(1)} %get-tuple-element.26), channel_id=1, source_target_pairs={{0,8},{8,16},{16,24},{24,32},{32,40},{40,48},{48,56},{56,64},{64,7... | collective-permute-start | bytes 786440 | tf_op jit(solution)/shard_map/ppermute | solution.py:195
  45.8 30.6 %collective-permute-start.8 = (f32[8,8,1024]{2,1,0:T(8,128)S(1)}, f32[8,8,1024]{2,1,0:T(8,128)S(1)}, u32[]{:S(2)}, u32[]{:S(2)}) collective-permute-start(f32[8,8,1024]{2,1,0:T(8,128)S(1)} %collective-permute-done.5.hi_ref), channel_id=1, source_target_pairs={{0,1},{1,2},{2,3},{3,4},{4,5},{5,6},{6,7},{7,0},{8,9},{9,10},{10,1... | collective-permute-start | bytes 786440 | tf_op jit(solution)/shard_map/ppermute | solution.py:198
  52.9 23.6 %collective-permute-start.7 = (f32[8,8,1024]{2,1,0:T(8,128)S(1)}, f32[8,8,1024]{2,1,0:T(8,128)S(1)}, u32[]{:S(2)}, u32[]{:S(2)}) collective-permute-start(f32[8,8,1024]{2,1,0:T(8,128)S(1)} %slice.39), channel_id=1, source_target_pairs={{0,1},{1,2},{2,3},{3,4},{4,5},{5,6},{6,7},{7,0},{8,9},{9,10},{10,1... | collective-permute-start | bytes 786440 | tf_op jit(solution)/shard_map/ppermute | solution.py:197

commit v3 on v2

v3 whole, which is shorter than its diff:
```python
import functools
import jax
import jax.numpy as jnp
from jax import lax
from jax.experimental import pallas as pl
from jax.experimental.pallas import tpu as pltpu
from jax.sharding import PartitionSpec as P

STEPS = 4
DRIFT = 16
TILE = 8

ANY = pl.BlockSpec(memory_space=pl.ANY)
VMEM = pl.BlockSpec(memory_space=pltpu.VMEM)
SMEM = pl.BlockSpec(memory_space=pltpu.SMEM)
LIMIT = 32 * 1024 * 1024
FULL = 60 * 1024 * 1024


def shift_pairs(count, by):
    return [(i, (i + by) % count) for i in range(count)]


def weights(ax, ay):
    col = lax.broadcasted_iota(jnp.int32, ax.shape, 1)
    last = ax.shape[1] - 1
    return (
        0.2 - ax,
        0.2 + ax,
        jnp.where(col == last, 0.0, 0.2 - ay),
        jnp.where(col == 0, 0.0, 0.2 + ay),
    )


def step(q, we, ww, wn, ws):
    rows, cols = q.shape
    return (
        0.2 * q
        + we * pltpu.roll(q, rows - 1, 0)
        + ww * pltpu.roll(q, 1, 0)
        + wn * pltpu.roll(q, cols - 1, 1)
        + ws * pltpu.roll(q, 1, 1)
    )


def inner_kernel(
    count_ref, k_any, ax_any, ay_any,
    mid_ref, edge_ref, head_ref, tail_ref, beyond_ref,
    k_ref, a_ref, w_ref, sems,
):
    vectors, rows, _ = k_ref.shape
    copies = [
        pltpu.make_async_copy(source, target, sems.at[i])
        for i, (source, target) in enumerate(
            [(k_any.at[b], k_ref.at[b]) for b in range(vectors)]
            + [(ax_any, a_ref.at[0]), (ay_any, a_ref.at[1])]
        )
    ]
    for copy in copies[vectors:] + copies[:vectors]:
        copy.start()
    for i in range(2):
        copies[vectors + i].wait()
        head_ref[vectors + i] = a_ref[i, :STEPS]
        tail_ref[vectors + i] = a_ref[i, rows - STEPS :]
    for i, w in enumerate(weights(a_ref[0], a_ref[1])):
        w_ref[i] = w
    for b in range(vectors):
        copies[b].wait()
        q = lax.fori_loop(
            0, count_ref[0], lambda _, q: step(q, w_ref[0], w_ref[1], w_ref[2], w_ref[3]), k_ref[b]
        )
        mid_ref[b] = q[TILE : rows - TILE]
        edge_ref[b, :TILE] = q[:TILE]
        edge_ref[b, TILE:] = q[rows - TILE :]
        beyond_ref[b] = k_ref[b, :DRIFT]
        head_ref[b] = k_ref[b, :STEPS]
        tail_ref[b] = k_ref[b, rows - STEPS :]


def outer_kernel(
    count_ref, k_ref, ax_ref, ay_ref, left_ref, right_ref, edge_ref, lo_ref, hi_ref, w_ref
):
    vectors, rows, _ = k_ref.shape

    def around(strip, at):
        return jnp.concatenate(
            [strip[rows - TILE :], right_ref[at], left_ref[at], strip[:TILE]], axis=0
        )

    for i, w in enumerate(weights(around(ax_ref, vectors), around(ay_ref, vectors + 1))):
        w_ref[i] = w
    row = lax.broadcasted_iota(jnp.int32, lo_ref.shape[1:], 0)
    for b in range(vectors):
        q = lax.fori_loop(
            0, count_ref[0], lambda _, q: step(q, w_ref[0], w_ref[1], w_ref[2], w_ref[3]), around(k_ref.at[b], b)
        )
        hi_ref[b] = jnp.where(row < TILE - STEPS, edge_ref[b, TILE:], q[:TILE])
        lo_ref[b] = jnp.where(row < STEPS, q[2 * TILE :], edge_ref[b, :TILE])


def pair_sums(left, right, blocks, vectors, cols):
    sums = []
    half = vectors // 2
    for first in range(0, vectors, half):
        accs = {}
        for block in range(blocks):
            for lane in range(0, cols, 128):
                rs = [right(c, block, lane) for c in range(vectors)]
                for a in range(first, first + half):
                    value = left(a, block, lane)
                    for c in range(vectors):
                        term = value * rs[c]
                        accs[a, c] = accs[a, c] + term if (a, c) in accs else term
        sums += [jnp.sum(accs[a, c], axis=0, keepdims=True) for a in range(first, first + half) for c in range(vectors)]
    return jnp.concatenate(sums, axis=0)


def tile_of(ref, v, block, lane):
    return ref[v, block * TILE : (block + 1) * TILE, lane : lane + 128]


def own_kernel(drift_ref, k_ref, beyond_ref, table_ref, shifted_ref):
    vectors, rows, cols = k_ref.shape
    tile = functools.partial(tile_of, k_ref)
    table_ref[...] = pair_sums(tile, tile, rows // TILE, vectors, cols)
    total = rows + beyond_ref.shape[1]
    by = lax.rem(total - drift_ref[0], total)
    for b in range(vectors):
        joined = jnp.concatenate([k_ref[b], beyond_ref[b]], axis=0)
        shifted_ref[b] = pltpu.roll(joined, by, 0)[:rows]


def gram_kernel(shifted_ref, lo_ref, mid_ref, hi_ref, own_ref, gram_ref):
    vectors, rows, cols = shifted_ref.shape
    blocks = rows // TILE

    def arrived(c, block, lane):
        if block == 0:
            return tile_of(lo_ref, c, 0, lane)
        if block == blocks - 1:
            return tile_of(hi_ref, c, 0, lane)
        return tile_of(mid_ref, c, block - 1, lane)

    table = own_ref[...] - pair_sums(functools.partial(tile_of, shifted_ref), arrived, blocks, vectors, cols)
    ones = jnp.ones((gram_ref.shape[0], 128), jnp.float32)
    gram_ref[...] = lax.dot_general(
        ones, table, (((1,), (1,)), ((), ())),
        precision=lax.Precision.HIGHEST, preferred_element_type=jnp.float32,
    )


def last_kernel(drift_ref, k_ref, mid_ref, lo_ref, hi_ref, rim_mid_ref, rim_hi_ref, product_ref):
    vectors, rows, _ = k_ref.shape
    total = DRIFT + rows
    by = lax.rem(drift_ref[0] + (total - DRIFT), total)
    for b in range(vectors):
        joined = jnp.concatenate(
            [rim_mid_ref[b], rim_hi_ref[b], lo_ref[b], mid_ref[b], hi_ref[b]], axis=0
        )
        product_ref[b] = k_ref[b] - pltpu.roll(joined, by, 0)[:rows]


def buffer(*shape):
    return pltpu.VMEM(shape, jnp.float32)


def call(kernel, outs, ins, scratch, cost, limit=LIMIT):
    return pl.pallas_call(
        kernel,
        out_shape=[jax.ShapeDtypeStruct(o, jnp.float32) for o in outs],
        in_specs=ins,
        out_specs=[VMEM] * len(outs),
        scratch_shapes=scratch,
        compiler_params=pltpu.CompilerParams(vmem_limit_bytes=limit),
        cost_estimate=pl.CostEstimate(flops=cost << 30, bytes_accessed=4 << 20, transcendentals=0),
    )


def body(krylov, advect_x, advect_y, step_counts, drifts):
    k, ax, ay = krylov[0], advect_x[0], advect_y[0]
    vectors, rows, cols = k.shape
    segs, strips = lax.axis_size("seg"), lax.axis_size("gx")
    world, pairs = segs * strips, vectors * vectors
    fields = vectors + 2
    half = segs // 2
    onward = functools.partial(lax.ppermute, axis_name="seg", perm=shift_pairs(segs, 1))
    sideways = functools.partial(lax.ppermute, axis_name="gx", perm=shift_pairs(strips, 1))
    backward = functools.partial(lax.ppermute, axis_name="gx", perm=shift_pairs(strips, -1))

    mid, edge, head, tail, beyond = call(
        inner_kernel,
        [(vectors, rows - 2 * TILE, cols), (vectors, 2 * TILE, cols)]
        + [(fields, STEPS, cols)] * 2
        + [(vectors, DRIFT, cols)],
        [SMEM, ANY, ANY, ANY],
        [buffer(vectors, rows, cols), buffer(2, rows, cols), buffer(4, rows, cols), pltpu.SemaphoreType.DMA((fields,))],
        64,
        limit=FULL,
    )(step_counts, k, ax, ay)
    mid = lax.ppermute(mid, "seg", [(s, s // half * half + (s + 1) % half) for s in range(segs)])
    right = backward(head)
    left = sideways(tail)
    drift = onward(drifts)
    beyond = backward(beyond)
    lo, hi = call(
        outer_kernel,
        [(vectors, TILE, cols), (vectors, TILE, cols)],
        [SMEM] + [VMEM] * 6,
        [buffer(4, 3 * TILE, cols)],
        64,
    )(step_counts, k, ax, ay, left, right, edge)
    sent_lo, sent_hi, kept = lax.optimization_barrier((lo, hi, k))
    hi = onward(hi)
    lo = onward(lo)
    own, shifted = call(own_kernel, [(pairs, 128), k.shape], [SMEM, VMEM, VMEM], [], 4)(drift, kept, beyond)
    held, _, _ = lax.optimization_barrier((mid, sent_lo, sent_hi))
    crossed = lax.ppermute(held, "seg", [(0, half), (half, 0)])
    mid = jnp.where(lax.axis_index("seg") % half == 0, crossed, mid)
    rim_mid = sideways(mid[:, -(DRIFT - TILE) :])
    rim_hi = sideways(hi)
    (gram,) = call(gram_kernel, [(world, pairs)], [VMEM] * 5, [], 4)(shifted, lo, mid, hi, own)
    gram = lax.all_to_all(gram, ("seg", "gx"), 0, 0)
    (product,) = call(last_kernel, [k.shape], [SMEM] + [VMEM] * 6, [], 64)(
        drift, k, mid, lo, hi, rim_mid, rim_hi
    )
    product, gram = lax.optimization_barrier((product, gram))
    cells = world * rows * cols
    gram = jnp.sum(gram, axis=0).reshape(vectors, vectors) / jnp.float32(cells)
    return product[None], gram


def solution(mesh):
    return jax.shard_map(
        body,
        mesh=mesh,
        in_specs=(
            P("seg", None, "gx", None),
            P("seg", "gx", None),
            P("seg", "gx", None),
            P("seg"),
            P("seg"),
        ),
        out_specs=(P("seg", None, "gx", None), P()),
        check_vma=False,
    )
```

time: 79.2 us -> 83.4 us (1.053)
  blocking collectives: 21.7 us -> 0 us
  starting transfers between devices: 19.9 us -> 39 us
  Pallas kernels: 7.61 us -> 11.8 us
  waiting for transfers between devices: 25.3 us -> 28.7 us
  local copies, waits for them, and re-layouts: 3.02 us -> 1.74 us
  other arithmetic: 0.14 us -> 1.16 us
    ppermute x1, waiting for transfers between devices: 23.1 us -> 0.01 us  [body(): hi = onward(hi)]
    all_to_all x1 -> x0, blocking collectives: 21.7 us -> none  [body(): gram = lax.all_to_all(gram, ('seg', 'gx'), 0, 0)]
    ppermute x5 -> x6, waiting for transfers between devices: 2.2 us -> 17.6 us  [the longest x1 8.45 us: body(): lax.ppermute(mid, 'seg', [(s, s // half * half + (s + 1) % half) for s in...]
    all_to_all x0 -> x1, waiting for transfers between devices: none -> 11 us  [body(): gram = lax.all_to_all(gram, ('seg', 'gx'), 0, 0)]
    all_to_all x0 -> x1, starting transfers between devices: none -> 8.96 us  [body(): gram = lax.all_to_all(gram, ('seg', 'gx'), 0, 0)]
    ppermute x5 -> x6, starting transfers between devices: 10.8 us -> 19.5 us  [the longest x1 9.5 us: body(): crossed = lax.ppermute(held, 'seg', [(0, half), (half, 0)])]
    ppermute x1, starting transfers between devices: 7.06 us -> 2.5 us  [body(): rim_hi = sideways(hi)]
    ppermute x1, starting transfers between devices: 0.08 us -> 4.35 us  [body(): rim_mid = sideways(mid[:, -(DRIFT - TILE):])]
  transfers between devices with their start and end apart: 9 -> 11, of which waited for: 2 -> 5; matrix products, arithmetic and copies ran while one was open for 3% -> 1% of each run, Pallas kernels for 7% -> 8%
where the time goes in v3:
time: 83.4 us; the launch traced here: 83.8 us
  starting transfers between devices  39 us (47%)
  waiting for transfers between devices  28.7 us (34%)
  Pallas kernels  11.8 us (14%)
  local copies, waits for them, and re-layouts  1.74 us (2%)
  between operations  1.43 us (2%)
  other arithmetic  1.16 us (1%)
    all_to_all x1, waiting for transfers between devices, body(): gram = lax.all_to_all(gram, ('seg', 'gx'), 0, 0)  11 us
    ppermute x1, starting transfers between devices, body(): crossed = lax.ppermute(held, 'seg', [(0, half), (half, 0)])  9.5 us
    all_to_all x1, starting transfers between devices, body(): gram = lax.all_to_all(gram, ('seg', 'gx'), 0, 0)  8.96 us
    ppermute x1, waiting for transfers between devices, body(): lax.ppermute(mid, 'seg', [(s, s // half * half + (s + 1) % half) for s in...  8.45 us
    pallas_call x1, Pallas kernels, body(): call(inner_kernel, [(vectors, rows - 2 * TILE, cols), (vectors, 2 * TILE,...  5.16 us
    ppermute x1, waiting for transfers between devices, body(): crossed = lax.ppermute(held, 'seg', [(0, half), (half, 0)])  4.77 us
    ppermute x1, starting transfers between devices, body(): left = sideways(tail)  4.46 us
    ppermute x1, starting transfers between devices, body(): rim_mid = sideways(mid[:, -(DRIFT - TILE):])  4.35 us
  transfers between devices with their start and end apart: 11, of which 5 were waited for; matrix products, arithmetic and copies ran while one was open for 1% of the time, Pallas kernels for 8%

profile of v3, /device:TPU:1, one launch (start us, length us, event | category | flops | bytes accessed | tf_op | source)
XLA Modules:
  0.0 83.8 jit_solution(8288065247221442686)
XLA Ops:
  1.3 5.2 %shard_map.68 = (f32[8,16,1024]{2,1,0:T(8,128)}, f32[8,16,1024]{2,1,0:T(8,128)}, f32[10,4,1024]{2,1,0:T(4,128)}, f32[10,4,1024]{2,1,0:T(4,128)}, f32[8,16,1024]{2,1,0:T(8,128)}) custom-call(s32[1]{0:T(128)S(6)} %copy.8.count_ref, f32[8,32,1024]{2,1,0:T(8,128)} %bitcast.8, f32[32,1024]{1,0:T(8,128)} %bitcast.12, f32[32,1024]{1,0:T(8,128)} %bitcast.14), custom_call_target="tpu_custom_call" | custom-call | flops 68719476736 | bytes 4194304 | tf_op jit(solution)/shard_map/pallas_call | solution.py:190
  6.5 4.5 %collective-permute-start.3 = (f32[10,4,1024]{2,1,0:T(4,128)}, f32[10,4,1024]{2,1,0:T(4,128)S(1)}, u32[]{:S(2)}, u32[]{:S(2)}) collective-permute-start(f32[10,4,1024]{2,1,0:T(4,128)} %get-tuple-element.15), channel_id=1, source_target_pairs={{0,1},{1,2},{2,3},{3,4},{4,5},{5,6},{6,7},{7,0},{8,9},{9,10},{10,1... | collective-permute-start | bytes 491528 | tf_op jit(solution)/shard_map/ppermute | solution.py:202
  10.9 3.0 %collective-permute-start.9 = (f32[8,16,1024]{2,1,0:T(8,128)}, f32[8,16,1024]{2,1,0:T(8,128)S(1)}, u32[]{:S(2)}, u32[]{:S(2)}) collective-permute-start(f32[8,16,1024]{2,1,0:T(8,128)} %get-tuple-element.21), channel_id=1, source_target_pairs={{0,7},{1,0},{2,1},{3,2},{4,3},{5,4},{6,5},{7,6},{8,15},{9,8},{10,9... | collective-permute-start | bytes 1572872 | tf_op jit(solution)/shard_map/ppermute | solution.py:204
  13.9 2.5 %collective-permute-start.1 = (f32[8,16,1024]{2,1,0:T(8,128)}, f32[8,16,1024]{2,1,0:T(8,128)S(1)}, u32[]{:S(2)}, u32[]{:S(2)}) collective-permute-start(f32[8,16,1024]{2,1,0:T(8,128)} %get-tuple-element.14), channel_id=1, source_target_pairs={{0,8},{8,16},{16,24},{24,32},{32,40},{40,48},{48,56},{56,64},{64,7... | collective-permute-start | bytes 1572872 | tf_op jit(solution)/shard_map/ppermute | solution.py:200
  16.4 0.4 collective-permute-done.4.right_ref
  16.8 1.0 %copy-done.3 = f32[8,16,1024]{2,1,0:T(8,128)S(1)} copy-done((f32[8,16,1024]{2,1,0:T(8,128)S(1)}, f32[8,16,1024]{2,1,0:T(8,128)}, u32[]{:S(2)}) %copy-start.3) | copy-done | bytes 524312
  17.8 2.0 %shard_map.69 = (f32[8,8,1024]{2,1,0:T(8,128)S(1)}, f32[8,8,1024]{2,1,0:T(8,128)S(1)}) custom-call(s32[1]{0:T(128)S(6)} %copy.8.count_ref, f32[8,32,1024]{2,1,0:T(8,128)S(1)} %bitcast.9, f32[32,1024]{1,0:T(8,128)S(1)} %bitcast.13, f32[32,1024]{1,0:T(8,128)S(1)} %bitcast.15, f32[10,4,1024]{2,1,0:T(4,128)S(1)} %collective-permute-done.3.left_ref, ...), custom_call_target="tpu_custom_call" | custom-call | flops 68719476736 | bytes 4194304 | tf_op jit(solution)/shard_map/pallas_call | solution.py:205
  19.9 3.6 %collective-permute-start.6 = (f32[8,8,1024]{2,1,0:T(8,128)S(1)}, f32[8,8,1024]{2,1,0:T(8,128)S(1)}, u32[]{:S(2)}, u32[]{:S(2)}) collective-permute-start(f32[8,8,1024]{2,1,0:T(8,128)S(1)} %get-tuple-element.19), channel_id=1, source_target_pairs={{0,8},{8,16},{16,24},{24,32},{32,40},{40,48},{48,56},{56,64},{64,7... | collective-permute-start | bytes 786440 | tf_op jit(solution)/shard_map/ppermute | solution.py:213
  23.5 8.4 %collective-permute-done.1 = f32[8,16,1024]{2,1,0:T(8,128)S(1)} collective-permute-done((f32[8,16,1024]{2,1,0:T(8,128)}, f32[8,16,1024]{2,1,0:T(8,128)S(1)}, u32[]{:S(2)}, u32[]{:S(2)}) %collective-permute-start.1) | collective-permute-done | bytes 524320 | tf_op jit(solution)/shard_map/ppermute | solution.py:200
  31.9 9.5 %collective-permute-start.2 = (f32[8,16,1024]{2,1,0:T(8,128)S(1)}, f32[8,16,1024]{2,1,0:T(8,128)}, u32[]{:S(2)}, u32[]{:S(2)}) collective-permute-start(f32[8,16,1024]{2,1,0:T(8,128)S(1)} %collective-permute-done.1), channel_id=1, source_target_pairs={{0,128},{128,0},{1,129},{129,1},{2,130},{130,2},{3,131},{131,3},{4... | collective-permute-start | bytes 1572872 | tf_op jit(solution)/shard_map/ppermute | solution.py:217
  41.4 0.1 collective-permute-start
  41.5 0.1 collective-permute-start.5
  41.6 2.5 %collective-permute-start.8 = (f32[8,8,1024]{2,1,0:T(8,128)S(1)}, f32[8,8,1024]{2,1,0:T(8,128)S(1)}, u32[]{:S(2)}, u32[]{:S(2)}) collective-permute-start(f32[8,8,1024]{2,1,0:T(8,128)S(1)} %collective-permute-done.6.hi_ref), channel_id=1, source_target_pairs={{0,1},{1,2},{2,3},{3,4},{4,5},{5,6},{6,7},{7,0},{8,9},{9,10},{10,1... | collective-permute-start | bytes 786440 | tf_op jit(solution)/shard_map/ppermute | solution.py:220
  44.1 4.1 %collective-permute-done.drift_ref = s32[1]{0:T(128)} collective-permute-done((s32[1]{0:T(128)}, s32[1]{0:T(128)}, u32[]{:S(2)}, u32[]{:S(2)}) %collective-permute-start) | collective-permute-done | bytes 36 | tf_op jit(solution)/shard_map/ppermute | solution.py:203
  48.2 1.2 %shard_map.71 = (f32[64,128]{1,0:T(8,128)S(1)}, f32[8,32,1024]{2,1,0:T(8,128)S(1)}) custom-call(s32[1]{0:T(128)} %collective-permute-done.drift_ref, f32[8,32,1024]{2,1,0:T(8,128)S(1)} %bitcast.10, f32[8,16,1024]{2,1,0:T(8,128)S(1)} %collective-permute-done.9.beyond_ref), custom_call_target="tpu_custom_call" | custom-call | flops 4294967296 | bytes 4194304 | tf_op jit(solution)/shard_map/pallas_call | solution.py:215
  49.4 4.8 %collective-permute-done.2 = f32[8,16,1024]{2,1,0:T(8,128)} collective-permute-done((f32[8,16,1024]{2,1,0:T(8,128)S(1)}, f32[8,16,1024]{2,1,0:T(8,128)}, u32[]{:S(2)}, u32[]{:S(2)}) %collective-permute-start.2) | collective-permute-done | bytes 524320 | tf_op jit(solution)/shard_map/ppermute | solution.py:217
  54.2 1.1 %broadcast_select_fusion.mid_ref = f32[8,16,1024]{2,1,0:T(8,128)S(1)} fusion(f32[8,16,1024]{2,1,0:T(8,128)} %collective-permute-done.2, f32[8,16,1024]{2,1,0:T(8,128)S(1)} %collective-permute-done.1, pred[]{:T(512)S(6)} %eq.5), kind=kLoop, calls=%fused_computation | loop fusion | flops 131072 | bytes 1572865 | tf_op jit(solution)/shard_map/jit(_where)/select_n | solution.py:218
  55.3 4.3 %collective-permute-start.7 = (f32[8,8,1024]{2,1,0:T(8,128)S(1)}, f32[8,8,1024]{2,1,0:T(8,128)S(1)}, u32[]{:S(2)}, u32[]{:S(2)}) collective-permute-start(f32[8,8,1024]{2,1,0:T(8,128)S(1)} %slice.4), channel_id=1, source_target_pairs={{0,1},{1,2},{2,3},{3,4},{4,5},{5,6},{6,7},{7,0},{8,9},{9,10},{10,1... | collective-permute-start | bytes 786440 | tf_op jit(solution)/shard_map/ppermute | solution.py:219
  59.7 1.5 %shard_map.72 = f32[256,64]{1,0:T(8,128)} custom-call(f32[8,32,1024]{2,1,0:T(8,128)S(1)} %get-tuple-element.22.shifted_ref, f32[8,8,1024]{2,1,0:T(8,128)S(1)} %collective-permute-done.5.lo_ref, f32[8,16,1024]{2,1,0:T(8,128)S(1)} %broadcast_select_fusion.mid_ref, f32[8,8,1024]{2,1,0:T(8,128)S(1)} %collective-permute-done.6.hi_ref, ...), custom_call_target="tpu_custom_call" | custom-call | flops 4294967296 | bytes 4194304 | tf_op jit(solution)/shard_map/pallas_call | solution.py:221
  61.2 9.0 %all-to-all-start = ((f32[256,1,64]{2,1,0:T(1,128)}), f32[256,1,64]{2,1,0:T(1,128)S(1)}, u32[]{:S(2)}, u32[]{:S(2)}) async-start(f32[256,1,64]{2,1,0:T(1,128)} %bitcast.4), calls=%async_computation | async-start | bytes 262144 | tf_op jit(solution)/shard_map/all_to_all | solution.py:222
  70.2 1.9 %shard_map.70 = f32[8,32,1024]{2,1,0:T(8,128)} custom-call(s32[1]{0:T(128)} %collective-permute-done.drift_ref, f32[8,32,1024]{2,1,0:T(8,128)S(1)} %bitcast.11, f32[8,16,1024]{2,1,0:T(8,128)S(1)} %broadcast_select_fusion.mid_ref, f32[8,8,1024]{2,1,0:T(8,128)S(1)} %collective-permute-done.5.lo_ref, f32[8,8,1024]{2,1,0:T(8,128)S(1)} %collective-permute-done.6.hi_ref, ...), custom_call_target="tpu_custom_call" | custom-call | flops 68719476736 | bytes 4194304 | tf_op jit(solution)/shard_map/pallas_call | solution.py:223
  72.1 11.0 %all-to-all-done = f32[256,1,64]{2,1,0:T(1,128)S(1)} async-done(((f32[256,1,64]{2,1,0:T(1,128)}), f32[256,1,64]{2,1,0:T(1,128)S(1)}, u32[]{:S(2)}, u32[]{:S(2)}) %all-to-all-start) | async-done | bytes 65568 | tf_op jit(solution)/shard_map/all_to_all | solution.py:222
  83.1 0.1 reduce_sum.9
  83.1 0.7 div.10
  (16 shorter events, 0.1 us)
Async XLA Ops:
  1.3 15.5 %copy-start = (f32[1,8,32,1024]{3,2,1,0:T(8,128)S(1)}, f32[1,8,32,1024]{3,2,1,0:T(8,128)}, u32[]{:S(2)}) copy-start(f32[1,8,32,1024]{3,2,1,0:T(8,128)} %param.5) | copy-start | bytes 3145732
  1.3 15.5 %copy-start.1 = (f32[1,32,1024]{2,1,0:T(8,128)S(1)}, f32[1,32,1024]{2,1,0:T(8,128)}, u32[]{:S(2)}) copy-start(f32[1,32,1024]{2,1,0:T(8,128)} %param.6) | copy-start | bytes 393220
  1.3 15.5 %copy-start.2 = (f32[1,32,1024]{2,1,0:T(8,128)S(1)}, f32[1,32,1024]{2,1,0:T(8,128)}, u32[]{:S(2)}) copy-start(f32[1,32,1024]{2,1,0:T(8,128)} %param.7) | copy-start | bytes 393220
  6.5 10.0 %collective-permute-start.3 = (f32[10,4,1024]{2,1,0:T(4,128)}, f32[10,4,1024]{2,1,0:T(4,128)S(1)}, u32[]{:S(2)}, u32[]{:S(2)}) collective-permute-start(f32[10,4,1024]{2,1,0:T(4,128)} %get-tuple-element.15), channel_id=1, source_target_pairs={{0,1},{1,2},{2,3},{3,4},{4,5},{5,6},{6,7},{7,0},{8,9},{9,10},{10,1... | collective-permute-start | bytes 491528 | tf_op jit(solution)/shard_map/ppermute | solution.py:202
  10.9 5.9 %collective-permute-start.4 = (f32[10,4,1024]{2,1,0:T(4,128)}, f32[10,4,1024]{2,1,0:T(4,128)S(1)}, u32[]{:S(2)}, u32[]{:S(2)}) collective-permute-start(f32[10,4,1024]{2,1,0:T(4,128)} %get-tuple-element.16), channel_id=1, source_target_pairs={{0,7},{1,0},{2,1},{3,2},{4,3},{5,4},{6,5},{7,6},{8,15},{9,8},{10,9... | collective-permute-start | bytes 491528 | tf_op jit(solution)/shard_map/ppermute | solution.py:201
  10.9 37.3 %collective-permute-start.9 = (f32[8,16,1024]{2,1,0:T(8,128)}, f32[8,16,1024]{2,1,0:T(8,128)S(1)}, u32[]{:S(2)}, u32[]{:S(2)}) collective-permute-start(f32[8,16,1024]{2,1,0:T(8,128)} %get-tuple-element.21), channel_id=1, source_target_pairs={{0,7},{1,0},{2,1},{3,2},{4,3},{5,4},{6,5},{7,6},{8,15},{9,8},{10,9... | collective-permute-start | bytes 1572872 | tf_op jit(solution)/shard_map/ppermute | solution.py:204
  13.9 18.0 %collective-permute-start.1 = (f32[8,16,1024]{2,1,0:T(8,128)}, f32[8,16,1024]{2,1,0:T(8,128)S(1)}, u32[]{:S(2)}, u32[]{:S(2)}) collective-permute-start(f32[8,16,1024]{2,1,0:T(8,128)} %get-tuple-element.14), channel_id=1, source_target_pairs={{0,8},{8,16},{16,24},{24,32},{32,40},{40,48},{48,56},{56,64},{64,7... | collective-permute-start | bytes 1572872 | tf_op jit(solution)/shard_map/ppermute | solution.py:200
  16.8 1.0 %copy-start.3 = (f32[8,16,1024]{2,1,0:T(8,128)S(1)}, f32[8,16,1024]{2,1,0:T(8,128)}, u32[]{:S(2)}) copy-start(f32[8,16,1024]{2,1,0:T(8,128)} %get-tuple-element.17.edge_ref) | copy-start | bytes 1572868
  19.9 21.7 %collective-permute-start.6 = (f32[8,8,1024]{2,1,0:T(8,128)S(1)}, f32[8,8,1024]{2,1,0:T(8,128)S(1)}, u32[]{:S(2)}, u32[]{:S(2)}) collective-permute-start(f32[8,8,1024]{2,1,0:T(8,128)S(1)} %get-tuple-element.19), channel_id=1, source_target_pairs={{0,8},{8,16},{16,24},{24,32},{32,40},{40,48},{48,56},{56,64},{64,7... | collective-permute-start | bytes 786440 | tf_op jit(solution)/shard_map/ppermute | solution.py:213
  31.9 22.3 %collective-permute-start.2 = (f32[8,16,1024]{2,1,0:T(8,128)S(1)}, f32[8,16,1024]{2,1,0:T(8,128)}, u32[]{:S(2)}, u32[]{:S(2)}) collective-permute-start(f32[8,16,1024]{2,1,0:T(8,128)S(1)} %collective-permute-done.1), channel_id=1, source_target_pairs={{0,128},{128,0},{1,129},{129,1},{2,130},{130,2},{3,131},{131,3},{4... | collective-permute-start | bytes 1572872 | tf_op jit(solution)/shard_map/ppermute | solution.py:217
  41.4 6.8 %collective-permute-start = (s32[1]{0:T(128)}, s32[1]{0:T(128)}, u32[]{:S(2)}, u32[]{:S(2)}) collective-permute-start(s32[1]{0:T(128)} %param.9), channel_id=1, source_target_pairs={{0,8},{8,16},{16,24},{24,32},{32,40},{40,48},{48,56},{56,64},{64,7... | collective-permute-start | bytes 20 | tf_op jit(solution)/shard_map/ppermute | solution.py:203
  41.5 18.1 %collective-permute-start.5 = (f32[8,8,1024]{2,1,0:T(8,128)S(1)}, f32[8,8,1024]{2,1,0:T(8,128)S(1)}, u32[]{:S(2)}, u32[]{:S(2)}) collective-permute-start(f32[8,8,1024]{2,1,0:T(8,128)S(1)} %get-tuple-element.18), channel_id=1, source_target_pairs={{0,8},{8,16},{16,24},{24,32},{32,40},{40,48},{48,56},{56,64},{64,7... | collective-permute-start | bytes 786440 | tf_op jit(solution)/shard_map/ppermute | solution.py:214
  41.6 28.5 %collective-permute-start.8 = (f32[8,8,1024]{2,1,0:T(8,128)S(1)}, f32[8,8,1024]{2,1,0:T(8,128)S(1)}, u32[]{:S(2)}, u32[]{:S(2)}) collective-permute-start(f32[8,8,1024]{2,1,0:T(8,128)S(1)} %collective-permute-done.6.hi_ref), channel_id=1, source_target_pairs={{0,1},{1,2},{2,3},{3,4},{4,5},{5,6},{6,7},{7,0},{8,9},{9,10},{10,1... | collective-permute-start | bytes 786440 | tf_op jit(solution)/shard_map/ppermute | solution.py:220
  55.3 14.8 %collective-permute-start.7 = (f32[8,8,1024]{2,1,0:T(8,128)S(1)}, f32[8,8,1024]{2,1,0:T(8,128)S(1)}, u32[]{:S(2)}, u32[]{:S(2)}) collective-permute-start(f32[8,8,1024]{2,1,0:T(8,128)S(1)} %slice.4), channel_id=1, source_target_pairs={{0,1},{1,2},{2,3},{3,4},{4,5},{5,6},{6,7},{7,0},{8,9},{9,10},{10,1... | collective-permute-start | bytes 786440 | tf_op jit(solution)/shard_map/ppermute | solution.py:219
  61.2 21.9 %all-to-all-start = ((f32[256,1,64]{2,1,0:T(1,128)}), f32[256,1,64]{2,1,0:T(1,128)S(1)}, u32[]{:S(2)}, u32[]{:S(2)}) async-start(f32[256,1,64]{2,1,0:T(1,128)} %bitcast.4), calls=%async_computation | async-start | bytes 262144 | tf_op jit(solution)/shard_map/all_to_all | solution.py:222

commit v4 on v2

v4 whole, which is shorter than its diff:
```python
import functools
import jax
import jax.numpy as jnp
from jax import lax
from jax.experimental import pallas as pl
from jax.experimental.pallas import tpu as pltpu
from jax.sharding import PartitionSpec as P

STEPS = 4
DRIFT = 16
TILE = 8

VMEM = pl.BlockSpec(memory_space=pltpu.VMEM)
SMEM = pl.BlockSpec(memory_space=pltpu.SMEM)
LIMIT = 12 * 1024 * 1024


def shift_pairs(count, by):
    return [(i, (i + by) % count) for i in range(count)]


def weights(ax, ay):
    col = lax.broadcasted_iota(jnp.int32, ax.shape, 1)
    last = ax.shape[1] - 1
    return (
        0.2 - ax,
        0.2 + ax,
        jnp.where(col == last, 0.0, 0.2 - ay),
        jnp.where(col == 0, 0.0, 0.2 + ay),
    )


def step(q, we, ww, wn, ws):
    rows, cols = q.shape
    return (
        0.2 * q
        + we * pltpu.roll(q, rows - 1, 0)
        + ww * pltpu.roll(q, 1, 0)
        + wn * pltpu.roll(q, cols - 1, 1)
        + ws * pltpu.roll(q, 1, 1)
    )


def inner_kernel(count_ref, k_ref, ax_ref, ay_ref, mid_ref, beyond_ref, q_ref, w_ref):
    vectors, rows, _ = k_ref.shape
    for i, w in enumerate(weights(ax_ref[...], ay_ref[...])):
        w_ref[i] = w
    q_ref[...] = k_ref[...]
    beyond_ref[...] = k_ref[:, :DRIFT]

    @pl.loop(0, count_ref[0])
    def _(_):
        for b in range(vectors):
            q_ref[b] = step(q_ref[b], w_ref[0], w_ref[1], w_ref[2], w_ref[3])

    mid_ref[...] = q_ref[:, TILE : rows - TILE]


def outer_kernel(count_ref, k_ref, ax_ref, ay_ref, left_ref, right_ref, out_ref, q_ref, w_ref):
    vectors, rows, _ = k_ref.shape

    def around(strip, at):
        return jnp.concatenate(
            [strip[rows - 2 * TILE :], right_ref[at], left_ref[at], strip[: 2 * TILE]], axis=0
        )

    for i, w in enumerate(weights(around(ax_ref, vectors), around(ay_ref, vectors + 1))):
        w_ref[i] = w
    for b in range(vectors):
        q_ref[b] = around(k_ref.at[b], b)

    @pl.loop(0, count_ref[0])
    def _(_):
        for b in range(vectors):
            q_ref[b] = step(q_ref[b], w_ref[0], w_ref[1], w_ref[2], w_ref[3])

    out_ref[:, :TILE] = q_ref[:, TILE : 2 * TILE]
    out_ref[:, TILE:] = q_ref[:, 3 * TILE : 4 * TILE]


def pair_sums(left, right, blocks, vectors, cols):
    sums = []
    half = vectors // 2
    for first in range(0, vectors, half):
        accs = {}
        for block in range(blocks):
            for lane in range(0, cols, 128):
                rs = [right(c, block, lane) for c in range(vectors)]
                for a in range(first, first + half):
                    value = left(a, block, lane)
                    for c in range(vectors):
                        term = value * rs[c]
                        accs[a, c] = accs[a, c] + term if (a, c) in accs else term
        sums += [jnp.sum(accs[a, c], axis=0, keepdims=True) for a in range(first, first + half) for c in range(vectors)]
    return jnp.concatenate(sums, axis=0)


def tile_of(ref, v, block, lane):
    return ref[v, block * TILE : (block + 1) * TILE, lane : lane + 128]


def own_kernel(drift_ref, k_ref, beyond_ref, table_ref, shifted_ref):
    vectors, rows, cols = k_ref.shape
    tile = functools.partial(tile_of, k_ref)
    table_ref[...] = pair_sums(tile, tile, rows // TILE, vectors, cols)
    total = rows + beyond_ref.shape[1]
    by = lax.rem(total - drift_ref[0], total)
    for b in range(vectors):
        joined = jnp.concatenate([k_ref[b], beyond_ref[b]], axis=0)
        shifted_ref[b] = pltpu.roll(joined, by, 0)[:rows]


def gram_kernel(shifted_ref, mid_ref, edge_ref, own_ref, gram_ref):
    vectors, rows, cols = shifted_ref.shape
    blocks = rows // TILE

    def arrived(c, block, lane):
        if block == 0:
            return tile_of(edge_ref, c, 1, lane)
        if block == blocks - 1:
            return tile_of(edge_ref, c, 0, lane)
        return tile_of(mid_ref, c, block - 1, lane)

    table = own_ref[...] - pair_sums(functools.partial(tile_of, shifted_ref), arrived, blocks, vectors, cols)
    ones = jnp.ones((gram_ref.shape[0], 128), jnp.float32)
    gram_ref[...] = lax.dot_general(
        ones, table, (((1,), (1,)), ((), ())),
        precision=lax.Precision.HIGHEST, preferred_element_type=jnp.float32,
    )


def last_kernel(drift_ref, k_ref, mid_ref, edge_ref, rim_mid_ref, rim_hi_ref, product_ref):
    vectors, rows, _ = k_ref.shape
    total = DRIFT + rows
    by = lax.rem(drift_ref[0] + (total - DRIFT), total)
    for b in range(vectors):
        joined = jnp.concatenate(
            [rim_mid_ref[b], rim_hi_ref[b], edge_ref[b, TILE:], mid_ref[b], edge_ref[b, :TILE]], axis=0
        )
        product_ref[b] = k_ref[b] - pltpu.roll(joined, by, 0)[:rows]


def buffer(*shape):
    return pltpu.VMEM(shape, jnp.float32)


def call(kernel, outs, ins, scratch, cost):
    return pl.pallas_call(
        kernel,
        out_shape=[jax.ShapeDtypeStruct(o, jnp.float32) for o in outs],
        in_specs=ins,
        out_specs=[VMEM] * len(outs),
        scratch_shapes=scratch,
        compiler_params=pltpu.CompilerParams(vmem_limit_bytes=LIMIT),
        cost_estimate=pl.CostEstimate(flops=cost << 30, bytes_accessed=4 << 20, transcendentals=0),
    )


def body(krylov, advect_x, advect_y, step_counts, drifts):
    k, ax, ay = krylov[0], advect_x[0], advect_y[0]
    vectors, rows, cols = k.shape
    segs, strips = lax.axis_size("seg"), lax.axis_size("gx")
    world, pairs = segs * strips, vectors * vectors
    half = segs // 2
    onward = functools.partial(lax.ppermute, axis_name="seg", perm=shift_pairs(segs, 1))
    sideways = functools.partial(lax.ppermute, axis_name="gx", perm=shift_pairs(strips, 1))
    backward = functools.partial(lax.ppermute, axis_name="gx", perm=shift_pairs(strips, -1))

    tail = jnp.concatenate([k[:, rows - STEPS :], ax[None, rows - STEPS :], ay[None, rows - STEPS :]], axis=0)
    head = jnp.concatenate([k[:, :STEPS], ax[None, :STEPS], ay[None, :STEPS]], axis=0)
    tail, head, k, ax, ay = lax.optimization_barrier((tail, head, k, ax, ay))
    right = backward(head)
    left = sideways(tail)
    drift = onward(drifts)
    mid, beyond = call(
        inner_kernel,
        [(vectors, rows - 2 * TILE, cols), (vectors, DRIFT, cols)],
        [SMEM, VMEM, VMEM, VMEM],
        [buffer(vectors, rows, cols), buffer(4, rows, cols)],
        64,
    )(step_counts, k, ax, ay)
    beyond, right = lax.optimization_barrier((beyond, right))
    beyond = backward(beyond)
    mid = lax.ppermute(mid, "seg", [(s, s // half * half + (s + 1) % half) for s in range(segs)])
    (edge,) = call(
        outer_kernel,
        [(vectors, 2 * TILE, cols)],
        [SMEM] + [VMEM] * 5,
        [buffer(vectors, 5 * TILE, cols), buffer(4, 5 * TILE, cols)],
        1,
    )(step_counts, k, ax, ay, left, right)
    sent, kept = lax.optimization_barrier((edge, k))
    edge = onward(edge)
    own, shifted = call(own_kernel, [(pairs, 128), k.shape], [SMEM, VMEM, VMEM], [], 16)(drift, kept, beyond)
    held, _ = lax.optimization_barrier((mid, sent))
    crossed = lax.ppermute(held, "seg", [(0, half), (half, 0)])
    mid = jnp.where(lax.axis_index("seg") % half == 0, crossed, mid)
    rim_mid = sideways(mid[:, -(DRIFT - TILE) :])
    edge, own, _ = lax.optimization_barrier((edge, own, mid))
    rim_hi = sideways(edge[:, :TILE])
    (gram,) = call(gram_kernel, [(world, pairs)], [VMEM] * 4, [], 1)(shifted, mid, edge, own)
    gram = lax.all_to_all(gram, ("seg", "gx"), 0, 0)
    (product,) = call(last_kernel, [k.shape], [SMEM] + [VMEM] * 5, [], 1)(
        drift, k, mid, edge, rim_mid, rim_hi
    )
    product, gram = lax.optimization_barrier((product, gram))
    cells = world * rows * cols
    gram = jnp.sum(gram, axis=0).reshape(vectors, vectors) / jnp.float32(cells)
    return product[None], gram


def solution(mesh):
    return jax.shard_map(
        body,
        mesh=mesh,
        in_specs=(
            P("seg", None, "gx", None),
            P("seg", "gx", None),
            P("seg", "gx", None),
            P("seg"),
            P("seg"),
        ),
        out_specs=(P("seg", None, "gx", None), P()),
        check_vma=False,
    )
```

time: 79.2 us -> 71 us (0.90); the launches traced: 79.1 us -> 69.9 us
  blocking collectives: 21.7 us -> 0 us
  starting transfers between devices: 19.9 us -> 26.2 us
  waiting for transfers between devices: 25.3 us -> 28.5 us
  Pallas kernels: 7.61 us -> 10.1 us
    all_to_all x1 -> x0, blocking collectives: 21.7 us -> none  [body(): gram = lax.all_to_all(gram, ('seg', 'gx'), 0, 0)]
    all_to_all x0 -> x1, waiting for transfers between devices: none -> 11 us  [body(): gram = lax.all_to_all(gram, ('seg', 'gx'), 0, 0)]
    ppermute x8, waiting for transfers between devices: 25.3 us -> 17.5 us  [the longest x1 9.84 us: body(): crossed = lax.ppermute(held, 'seg', [(0, half), (half, 0)])]
    ppermute x8, starting transfers between devices: 19.8 us -> 12.2 us  [the longest x1 3.32 us: body(): right = backward(head)]
    all_to_all x0 -> x1, starting transfers between devices: none -> 7.06 us  [body(): gram = lax.all_to_all(gram, ('seg', 'gx'), 0, 0)]
    ppermute x1, starting transfers between devices: 0.08 us -> 6.92 us  [body(): rim_mid = sideways(mid[:, -(DRIFT - TILE):])]
    pallas_call x5, Pallas kernels: 7.61 us -> 10.1 us  [the longest x1 2.84 us: body(): call(inner_kernel, [(vectors, rows - 2 * TILE, cols), (vectors, DRIFT, co...]
  transfers between devices with their start and end apart: 9 -> 10, of which waited for: 2 -> 6; matrix products, arithmetic and copies ran while one was open for 3% -> 0% of each run, Pallas kernels for 7% -> 14%
where the time goes in v4:
time: 71 us; the launch traced here: 69.9 us
  waiting for transfers between devices  28.5 us (40%)
  starting transfers between devices  26.2 us (37%)
  Pallas kernels  10.1 us (14%)
  local copies, waits for them, and re-layouts  3.46 us (5%)
  between operations  1.43 us (2%)
    all_to_all x1, waiting for transfers between devices, body(): gram = lax.all_to_all(gram, ('seg', 'gx'), 0, 0)  11 us
    ppermute x1, waiting for transfers between devices, body(): crossed = lax.ppermute(held, 'seg', [(0, half), (half, 0)])  9.84 us
    all_to_all x1, starting transfers between devices, body(): gram = lax.all_to_all(gram, ('seg', 'gx'), 0, 0)  7.06 us
    ppermute x1, starting transfers between devices, body(): rim_mid = sideways(mid[:, -(DRIFT - TILE):])  6.92 us
    ppermute x1, waiting for transfers between devices, body(): left = sideways(tail)  3.57 us
    ppermute x1, starting transfers between devices, body(): right = backward(head)  3.32 us
    ppermute x1, starting transfers between devices, body(): crossed = lax.ppermute(held, 'seg', [(0, half), (half, 0)])  3.14 us
    pallas_call x1, Pallas kernels, body(): call(inner_kernel, [(vectors, rows - 2 * TILE, cols), (vectors, DRIFT, co...  2.84 us
  transfers between devices with their start and end apart: 10, of which 6 were waited for; matrix products, arithmetic and copies ran while one was open for 0% of the time, Pallas kernels for 14%

profile of v4, /device:TPU:1, one launch (start us, length us, event | category | flops | bytes accessed | tf_op | source)
XLA Modules:
  0.0 69.9 jit_solution(17376674493769777469)
XLA Ops:
  0.6 0.9 %fusion.1 = (f32[1,4,1024]{2,1,0:T(4,128)S(1)}, f32[1,4,1024]{2,1,0:T(4,128)S(1)}) fusion(f32[1,32,1024]{2,1,0:T(8,128)} %param.6), kind=kLoop, calls=%fused_computation.5 | loop fusion | bytes 65536 | tf_op jit(solution)/shard_map/slice | solution.py:170
  1.5 0.8 %fusion.2 = (f32[1,4,1024]{2,1,0:T(4,128)S(1)}, f32[1,4,1024]{2,1,0:T(4,128)S(1)}) fusion(f32[1,32,1024]{2,1,0:T(8,128)} %param.7), kind=kLoop, calls=%fused_computation.6 | loop fusion | bytes 65536 | tf_op jit(solution)/shard_map/slice | solution.py:170
  2.3 1.1 %fusion = (f32[8,4,1024]{2,1,0:T(4,128)S(1)}, f32[8,4,1024]{2,1,0:T(4,128)S(1)}) fusion(f32[8,32,1024]{2,1,0:T(8,128)} %bitcast.8), kind=kLoop, calls=%fused_computation.4 | loop fusion | bytes 524288 | tf_op jit(solution)/shard_map/slice | solution.py:170
  3.4 0.1 pad_maximum_fusion
  3.5 3.3 %collective-permute-start.4 = (f32[10,4,1024]{2,1,0:T(4,128)S(1)}, f32[10,4,1024]{2,1,0:T(4,128)S(1)}, u32[]{:S(2)}, u32[]{:S(2)}) collective-permute-start(f32[10,4,1024]{2,1,0:T(4,128)S(1)} %get-tuple-element.24), channel_id=1, source_target_pairs={{0,7},{1,0},{2,1},{3,2},{4,3},{5,4},{6,5},{7,6},{8,15},{9,8},{10,9... | collective-permute-start | bytes 491528 | tf_op jit(solution)/shard_map/ppermute | solution.py:172
  7.5 2.8 %shard_map.68 = (f32[8,16,1024]{2,1,0:T(8,128)}, f32[8,16,1024]{2,1,0:T(8,128)S(1)}) custom-call(s32[1]{0:T(128)S(6)} %copy.8.count_ref, f32[8,32,1024]{2,1,0:T(8,128)S(1)} %bitcast.9, f32[32,1024]{1,0:T(8,128)S(1)} %bitcast.13, f32[32,1024]{1,0:T(8,128)S(1)} %bitcast.15), custom_call_target="tpu_custom_call" | custom-call | flops 68719476736 | bytes 4194304 | tf_op jit(solution)/shard_map/pallas_call | solution.py:175
  10.3 2.4 %collective-permute-done.4.right_ref = f32[10,4,1024]{2,1,0:T(4,128)S(1)} collective-permute-done((f32[10,4,1024]{2,1,0:T(4,128)S(1)}, f32[10,4,1024]{2,1,0:T(4,128)S(1)}, u32[]{:S(2)}, u32[]{:S(2)}) %collective-permute-start.4) | collective-permute-done | bytes 163872 | tf_op jit(solution)/shard_map/ppermute | solution.py:172
  12.7 2.7 %collective-permute-start.6 = (f32[8,16,1024]{2,1,0:T(8,128)S(1)}, f32[8,16,1024]{2,1,0:T(8,128)S(1)}, u32[]{:S(2)}, u32[]{:S(2)}) collective-permute-start(f32[8,16,1024]{2,1,0:T(8,128)S(1)} %get-tuple-element.27), channel_id=1, source_target_pairs={{0,7},{1,0},{2,1},{3,2},{4,3},{5,4},{6,5},{7,6},{8,15},{9,8},{10,9... | collective-permute-start | bytes 1572872 | tf_op jit(solution)/shard_map/ppermute | solution.py:183
  15.4 1.3 %collective-permute-start = (s32[1]{0:T(128)}, s32[1]{0:T(128)}, u32[]{:S(2)}, u32[]{:S(2)}) collective-permute-start(s32[1]{0:T(128)} %param.9), channel_id=1, source_target_pairs={{0,8},{8,16},{16,24},{24,32},{32,40},{40,48},{48,56},{56,64},{64,7... | collective-permute-start | bytes 20 | tf_op jit(solution)/shard_map/ppermute | solution.py:174
  16.7 3.6 %collective-permute-done.3.left_ref = f32[10,4,1024]{2,1,0:T(4,128)S(1)} collective-permute-done((f32[10,4,1024]{2,1,0:T(4,128)S(1)}, f32[10,4,1024]{2,1,0:T(4,128)S(1)}, u32[]{:S(2)}, u32[]{:S(2)}) %collective-permute-start.3) | collective-permute-done | bytes 163872 | tf_op jit(solution)/shard_map/ppermute | solution.py:173
  20.3 2.6 %shard_map.69 = f32[8,16,1024]{2,1,0:T(8,128)S(1)} custom-call(s32[1]{0:T(128)S(6)} %copy.8.count_ref, f32[8,32,1024]{2,1,0:T(8,128)S(1)} %bitcast.10, f32[32,1024]{1,0:T(8,128)S(1)} %bitcast.14, f32[32,1024]{1,0:T(8,128)S(1)} %bitcast.16, f32[10,4,1024]{2,1,0:T(4,128)S(1)} %collective-permute-done.3.left_ref, ...), custom_call_target="tpu_custom_call" | custom-call | flops 1073741824 | bytes 4194304 | tf_op jit(solution)/shard_map/pallas_call | solution.py:185
  22.9 0.1 collective-permute-start.5
  23.0 0.4 collective-permute-done.1
  23.4 3.1 %collective-permute-start.2 = (f32[8,16,1024]{2,1,0:T(8,128)}, f32[8,16,1024]{2,1,0:T(8,128)S(1)}, u32[]{:S(2)}, u32[]{:S(2)}) collective-permute-start(f32[8,16,1024]{2,1,0:T(8,128)} %collective-permute-done.1), channel_id=1, source_target_pairs={{0,128},{128,0},{1,129},{129,1},{2,130},{130,2},{3,131},{131,3},{4... | collective-permute-start | bytes 1572872 | tf_op jit(solution)/shard_map/ppermute | solution.py:196
  26.5 1.4 %collective-permute-done.6.beyond_ref = f32[8,16,1024]{2,1,0:T(8,128)S(1)} collective-permute-done((f32[8,16,1024]{2,1,0:T(8,128)S(1)}, f32[8,16,1024]{2,1,0:T(8,128)S(1)}, u32[]{:S(2)}, u32[]{:S(2)}) %collective-permute-start.6) | collective-permute-done | bytes 524320 | tf_op jit(solution)/shard_map/ppermute | solution.py:183
  27.9 1.2 %shard_map.70 = (f32[64,128]{1,0:T(8,128)S(1)}, f32[8,32,1024]{2,1,0:T(8,128)S(1)}) custom-call(s32[1]{0:T(128)} %collective-permute-done.drift_ref, f32[8,32,1024]{2,1,0:T(8,128)S(1)} %bitcast.11, f32[8,16,1024]{2,1,0:T(8,128)S(1)} %collective-permute-done.6.beyond_ref), custom_call_target="tpu_custom_call" | custom-call | flops 17179869184 | bytes 4194304 | tf_op jit(solution)/shard_map/pallas_call | solution.py:194
  29.2 9.8 %collective-permute-done.2 = f32[8,16,1024]{2,1,0:T(8,128)S(1)} collective-permute-done((f32[8,16,1024]{2,1,0:T(8,128)}, f32[8,16,1024]{2,1,0:T(8,128)S(1)}, u32[]{:S(2)}, u32[]{:S(2)}) %collective-permute-start.2) | collective-permute-done | bytes 524320 | tf_op jit(solution)/shard_map/ppermute | solution.py:196
  39.1 6.9 %collective-permute-start.7 = (f32[8,8,1024]{2,1,0:T(8,128)S(1)}, f32[8,8,1024]{2,1,0:T(8,128)S(1)}, u32[]{:S(2)}, u32[]{:S(2)}) collective-permute-start(f32[8,8,1024]{2,1,0:T(8,128)S(1)} %slice.38), channel_id=1, source_target_pairs={{0,1},{1,2},{2,3},{3,4},{4,5},{5,6},{6,7},{7,0},{8,9},{9,10},{10,1... | collective-permute-start | bytes 786440 | tf_op jit(solution)/shard_map/ppermute | solution.py:198
  46.1 1.7 %collective-permute-start.8 = (f32[8,8,1024]{2,1,0:T(8,128)S(1)}, f32[8,8,1024]{2,1,0:T(8,128)S(1)}, u32[]{:S(2)}, u32[]{:S(2)}) collective-permute-start(f32[8,8,1024]{2,1,0:T(8,128)S(1)} %slice.35), channel_id=1, source_target_pairs={{0,1},{1,2},{2,3},{3,4},{4,5},{5,6},{6,7},{7,0},{8,9},{9,10},{10,1... | collective-permute-start | bytes 786440 | tf_op jit(solution)/shard_map/ppermute | solution.py:200
  47.7 1.5 %shard_map.72 = f32[256,64]{1,0:T(8,128)} custom-call(f32[8,32,1024]{2,1,0:T(8,128)S(1)} %get-tuple-element.30.shifted_ref, f32[8,16,1024]{2,1,0:T(8,128)S(1)} %broadcast_select_fusion.mid_ref, f32[8,16,1024]{2,1,0:T(8,128)S(1)} %collective-permute-done.5.edge_ref, f32[64,128]{1,0:T(8,128)S(1)} %get-tuple-element.31.own_ref), custom_call_target="tpu_custom_call" | custom-call | flops 1073741824 | bytes 4194304 | tf_op jit(solution)/shard_map/pallas_call | solution.py:201
  49.2 7.1 %all-to-all-start = ((f32[256,1,64]{2,1,0:T(1,128)}), f32[256,1,64]{2,1,0:T(1,128)S(1)}, u32[]{:S(2)}, u32[]{:S(2)}) async-start(f32[256,1,64]{2,1,0:T(1,128)} %bitcast.4), calls=%async_computation | async-start | bytes 262144 | tf_op jit(solution)/shard_map/all_to_all | solution.py:202
  56.3 1.9 %shard_map.71 = f32[8,32,1024]{2,1,0:T(8,128)} custom-call(s32[1]{0:T(128)} %collective-permute-done.drift_ref, f32[8,32,1024]{2,1,0:T(8,128)S(1)} %bitcast.12, f32[8,16,1024]{2,1,0:T(8,128)S(1)} %broadcast_select_fusion.mid_ref, f32[8,16,1024]{2,1,0:T(8,128)S(1)} %collective-permute-done.5.edge_ref, f32[8,8,1024]{2,1,0:T(8,128)S(1)} %collective-permute-done.7.rim_mid_ref, ...), custom_call_target="tpu_custom_call" | custom-call | flops 1073741824 | bytes 4194304 | tf_op jit(solution)/shard_map/pallas_call | solution.py:203
  58.2 11.0 %all-to-all-done = f32[256,1,64]{2,1,0:T(1,128)S(1)} async-done(((f32[256,1,64]{2,1,0:T(1,128)}), f32[256,1,64]{2,1,0:T(1,128)S(1)}, u32[]{:S(2)}, u32[]{:S(2)}) %all-to-all-start) | async-done | bytes 65568 | tf_op jit(solution)/shard_map/all_to_all | solution.py:202
  69.3 0.7 div.10
  (17 shorter events, 0.2 us)
Async XLA Ops:
  0.6 6.8 %copy-start = (f32[1,8,32,1024]{3,2,1,0:T(8,128)S(1)}, f32[1,8,32,1024]{3,2,1,0:T(8,128)}, u32[]{:S(2)}) copy-start(f32[1,8,32,1024]{3,2,1,0:T(8,128)} %param.5) | copy-start | bytes 3145732
  3.4 4.1 %copy-start.1 = (f32[1,32,1024]{2,1,0:T(8,128)S(1)}, f32[1,32,1024]{2,1,0:T(8,128)}, u32[]{:S(2)}) copy-start(f32[1,32,1024]{2,1,0:T(8,128)} %param.6) | copy-start | bytes 393220
  3.4 4.1 %copy-start.2 = (f32[1,32,1024]{2,1,0:T(8,128)S(1)}, f32[1,32,1024]{2,1,0:T(8,128)}, u32[]{:S(2)}) copy-start(f32[1,32,1024]{2,1,0:T(8,128)} %param.7) | copy-start | bytes 393220
  3.5 9.2 %collective-permute-start.4 = (f32[10,4,1024]{2,1,0:T(4,128)S(1)}, f32[10,4,1024]{2,1,0:T(4,128)S(1)}, u32[]{:S(2)}, u32[]{:S(2)}) collective-permute-start(f32[10,4,1024]{2,1,0:T(4,128)S(1)} %get-tuple-element.24), channel_id=1, source_target_pairs={{0,7},{1,0},{2,1},{3,2},{4,3},{5,4},{6,5},{7,6},{8,15},{9,8},{10,9... | collective-permute-start | bytes 491528 | tf_op jit(solution)/shard_map/ppermute | solution.py:172
  10.3 13.1 %collective-permute-start.1 = (f32[8,16,1024]{2,1,0:T(8,128)}, f32[8,16,1024]{2,1,0:T(8,128)}, u32[]{:S(2)}, u32[]{:S(2)}) collective-permute-start(f32[8,16,1024]{2,1,0:T(8,128)} %get-tuple-element.21), channel_id=1, source_target_pairs={{0,8},{8,16},{16,24},{24,32},{32,40},{40,48},{48,56},{56,64},{64,7... | collective-permute-start | bytes 1572872 | tf_op jit(solution)/shard_map/ppermute | solution.py:184
  12.7 15.2 %collective-permute-start.6 = (f32[8,16,1024]{2,1,0:T(8,128)S(1)}, f32[8,16,1024]{2,1,0:T(8,128)S(1)}, u32[]{:S(2)}, u32[]{:S(2)}) collective-permute-start(f32[8,16,1024]{2,1,0:T(8,128)S(1)} %get-tuple-element.27), channel_id=1, source_target_pairs={{0,7},{1,0},{2,1},{3,2},{4,3},{5,4},{6,5},{7,6},{8,15},{9,8},{10,9... | collective-permute-start | bytes 1572872 | tf_op jit(solution)/shard_map/ppermute | solution.py:183
  15.4 4.9 %collective-permute-start.3 = (f32[10,4,1024]{2,1,0:T(4,128)S(1)}, f32[10,4,1024]{2,1,0:T(4,128)S(1)}, u32[]{:S(2)}, u32[]{:S(2)}) collective-permute-start(f32[10,4,1024]{2,1,0:T(4,128)S(1)} %get-tuple-element.22), channel_id=1, source_target_pairs={{0,1},{1,2},{2,3},{3,4},{4,5},{5,6},{6,7},{7,0},{8,9},{9,10},{10,1... | collective-permute-start | bytes 491528 | tf_op jit(solution)/shard_map/ppermute | solution.py:173
  15.4 11.1 %collective-permute-start = (s32[1]{0:T(128)}, s32[1]{0:T(128)}, u32[]{:S(2)}, u32[]{:S(2)}) collective-permute-start(s32[1]{0:T(128)} %param.9), channel_id=1, source_target_pairs={{0,8},{8,16},{16,24},{24,32},{32,40},{40,48},{48,56},{56,64},{64,7... | collective-permute-start | bytes 20 | tf_op jit(solution)/shard_map/ppermute | solution.py:174
  22.9 23.1 %collective-permute-start.5 = (f32[8,16,1024]{2,1,0:T(8,128)S(1)}, f32[8,16,1024]{2,1,0:T(8,128)S(1)}, u32[]{:S(2)}, u32[]{:S(2)}) collective-permute-start(f32[8,16,1024]{2,1,0:T(8,128)S(1)} %shard_map.69), channel_id=1, source_target_pairs={{0,8},{8,16},{16,24},{24,32},{32,40},{40,48},{48,56},{56,64},{64,7... | collective-permute-start | bytes 1572872 | tf_op jit(solution)/shard_map/ppermute | solution.py:193
  23.4 15.6 %collective-permute-start.2 = (f32[8,16,1024]{2,1,0:T(8,128)}, f32[8,16,1024]{2,1,0:T(8,128)S(1)}, u32[]{:S(2)}, u32[]{:S(2)}) collective-permute-start(f32[8,16,1024]{2,1,0:T(8,128)} %collective-permute-done.1), channel_id=1, source_target_pairs={{0,128},{128,0},{1,129},{129,1},{2,130},{130,2},{3,131},{131,3},{4... | collective-permute-start | bytes 1572872 | tf_op jit(solution)/shard_map/ppermute | solution.py:196
  39.1 17.2 %collective-permute-start.7 = (f32[8,8,1024]{2,1,0:T(8,128)S(1)}, f32[8,8,1024]{2,1,0:T(8,128)S(1)}, u32[]{:S(2)}, u32[]{:S(2)}) collective-permute-start(f32[8,8,1024]{2,1,0:T(8,128)S(1)} %slice.38), channel_id=1, source_target_pairs={{0,1},{1,2},{2,3},{3,4},{4,5},{5,6},{6,7},{7,0},{8,9},{9,10},{10,1... | collective-permute-start | bytes 786440 | tf_op jit(solution)/shard_map/ppermute | solution.py:198
  46.1 10.3 %collective-permute-start.8 = (f32[8,8,1024]{2,1,0:T(8,128)S(1)}, f32[8,8,1024]{2,1,0:T(8,128)S(1)}, u32[]{:S(2)}, u32[]{:S(2)}) collective-permute-start(f32[8,8,1024]{2,1,0:T(8,128)S(1)} %slice.35), channel_id=1, source_target_pairs={{0,1},{1,2},{2,3},{3,4},{4,5},{5,6},{6,7},{7,0},{8,9},{9,10},{10,1... | collective-permute-start | bytes 786440 | tf_op jit(solution)/shard_map/ppermute | solution.py:200
  49.2 20.0 %all-to-all-start = ((f32[256,1,64]{2,1,0:T(1,128)}), f32[256,1,64]{2,1,0:T(1,128)S(1)}, u32[]{:S(2)}, u32[]{:S(2)}) async-start(f32[256,1,64]{2,1,0:T(1,128)} %bitcast.4), calls=%async_computation | async-start | bytes 262144 | tf_op jit(solution)/shard_map/all_to_all | solution.py:202

commit v5 on v4

v5 whole, which is shorter than its diff:
```python
import functools
import jax
import jax.numpy as jnp
from jax import lax
from jax.experimental import pallas as pl
from jax.experimental.pallas import tpu as pltpu
from jax.sharding import PartitionSpec as P

STEPS = 4
DRIFT = 16
TILE = 8

ANY = pl.BlockSpec(memory_space=pl.ANY)
VMEM = pl.BlockSpec(memory_space=pltpu.VMEM)
SMEM = pl.BlockSpec(memory_space=pltpu.SMEM)
LIMIT = 12 * 1024 * 1024
FULL = 60 * 1024 * 1024


def shift_pairs(count, by):
    return [(i, (i + by) % count) for i in range(count)]


def weights(ax, ay):
    col = lax.broadcasted_iota(jnp.int32, ax.shape, 1)
    last = ax.shape[1] - 1
    return (
        0.2 - ax,
        0.2 + ax,
        jnp.where(col == last, 0.0, 0.2 - ay),
        jnp.where(col == 0, 0.0, 0.2 + ay),
    )


def step(q, we, ww, wn, ws):
    rows, cols = q.shape
    return (
        0.2 * q
        + we * pltpu.roll(q, rows - 1, 0)
        + ww * pltpu.roll(q, 1, 0)
        + wn * pltpu.roll(q, cols - 1, 1)
        + ws * pltpu.roll(q, 1, 1)
    )


def pack_kernel(k_any, ax_any, ay_any, head_ref, tail_ref, low_ref, high_ref, sems):
    rows = k_any.shape[1]
    vectors = k_any.shape[0]
    copies = []
    for i, (at, target) in enumerate(((0, low_ref), (rows - TILE, high_ref))):
        copies += [
            pltpu.make_async_copy(k_any.at[:, pl.ds(at, TILE)], target.at[pl.ds(0, vectors)], sems.at[i, 0]),
            pltpu.make_async_copy(ax_any.at[pl.ds(at, TILE)], target.at[vectors], sems.at[i, 1]),
            pltpu.make_async_copy(ay_any.at[pl.ds(at, TILE)], target.at[vectors + 1], sems.at[i, 2]),
        ]
    for copy in copies:
        copy.start()
    for copy in copies:
        copy.wait()
    head_ref[...] = low_ref[:, :STEPS]
    tail_ref[...] = high_ref[:, TILE - STEPS :]


def inner_kernel(count_ref, k_ref, ax_ref, ay_ref, mid_ref, q_ref, w_ref):
    vectors, rows, _ = k_ref.shape
    for i, w in enumerate(weights(ax_ref[...], ay_ref[...])):
        w_ref[i] = w
    q_ref[...] = k_ref[...]

    @pl.loop(0, count_ref[0])
    def _(_):
        for b in range(vectors):
            q_ref[b] = step(q_ref[b], w_ref[0], w_ref[1], w_ref[2], w_ref[3])

    mid_ref[...] = q_ref[:, TILE : rows - TILE]


def outer_kernel(count_ref, k_ref, ax_ref, ay_ref, left_ref, right_ref, mid_ref, lo_ref, hi_ref, upper_ref, q_ref, w_ref):
    vectors, rows, _ = k_ref.shape

    def around(strip, at):
        return jnp.concatenate(
            [strip[rows - 2 * TILE :], right_ref[at], left_ref[at], strip[: 2 * TILE]], axis=0
        )

    for i, w in enumerate(weights(around(ax_ref, vectors), around(ay_ref, vectors + 1))):
        w_ref[i] = w
    for b in range(vectors):
        q_ref[b] = around(k_ref.at[b], b)

    @pl.loop(0, count_ref[0])
    def _(_):
        for b in range(vectors):
            q_ref[b] = step(q_ref[b], w_ref[0], w_ref[1], w_ref[2], w_ref[3])

    hi_ref[...] = q_ref[:, TILE : 2 * TILE]
    lo_ref[...] = q_ref[:, 3 * TILE : 4 * TILE]
    upper_ref[:, :TILE] = mid_ref[:, TILE:]
    upper_ref[:, TILE:] = q_ref[:, TILE : 2 * TILE]


def pair_sums(left, right, blocks, vectors, cols):
    sums = []
    half = vectors // 2
    for first in range(0, vectors, half):
        accs = {}
        for block in range(blocks):
            for lane in range(0, cols, 128):
                rs = [right(c, block, lane) for c in range(vectors)]
                for a in range(first, first + half):
                    value = left(a, block, lane)
                    for c in range(vectors):
                        term = value * rs[c]
                        accs[a, c] = accs[a, c] + term if (a, c) in accs else term
        sums += [jnp.sum(accs[a, c], axis=0, keepdims=True) for a in range(first, first + half) for c in range(vectors)]
    return jnp.concatenate(sums, axis=0)


def tile_of(ref, v, block, lane):
    return ref[v, block * TILE : (block + 1) * TILE, lane : lane + 128]


def last_kernel(
    drift_ref, k_ref, mid_ref, lo_ref, hi_ref, rim_mid_ref, rim_hi_ref, upper_ref, product_any, gram_ref, product_ref, sems
):
    vectors, rows, cols = k_ref.shape
    total = DRIFT + rows
    by = lax.rem(drift_ref[0] + (total - DRIFT), total)
    copies = [pltpu.make_async_copy(product_ref.at[b], product_any.at[b], sems.at[b]) for b in range(vectors)]
    for b in range(vectors):
        joined = jnp.concatenate(
            [
                rim_mid_ref[b] + upper_ref[b, :TILE],
                rim_hi_ref[b] + upper_ref[b, TILE:],
                lo_ref[b],
                mid_ref[b],
                hi_ref[b],
            ],
            axis=0,
        )
        product_ref[b] = k_ref[b] - pltpu.roll(joined, by, 0)[:rows]
        copies[b].start()
    table = pair_sums(
        functools.partial(tile_of, k_ref), functools.partial(tile_of, product_ref), rows // TILE, vectors, cols
    )
    ones = jnp.ones((gram_ref.shape[0], 128), jnp.float32)
    gram_ref[...] = lax.dot_general(
        ones, table, (((1,), (1,)), ((), ())),
        precision=lax.Precision.HIGHEST, preferred_element_type=jnp.float32,
    )
    for copy in copies:
        copy.wait()


def buffer(*shape):
    return pltpu.VMEM(shape, jnp.float32)


def call(kernel, outs, ins, scratch, cost, limit=LIMIT, places=None):
    return pl.pallas_call(
        kernel,
        out_shape=[jax.ShapeDtypeStruct(o, jnp.float32) for o in outs],
        in_specs=ins,
        out_specs=places or [VMEM] * len(outs),
        scratch_shapes=scratch,
        compiler_params=pltpu.CompilerParams(vmem_limit_bytes=limit),
        cost_estimate=pl.CostEstimate(flops=cost << 30, bytes_accessed=4 << 20, transcendentals=0),
    )


def rim_pairs(segs, strips, direct):
    pairs = []
    for s in range(segs):
        for g in range(strips):
            busy = (s + 1) % (segs // 2) == 0 and g % 2 == 1
            if busy == direct:
                pairs.append(((s - direct) * strips + g, s * strips + (g + 1) % strips))
    return pairs


def body(krylov, advect_x, advect_y, step_counts, drifts):
    k, ax, ay = krylov[0], advect_x[0], advect_y[0]
    vectors, rows, cols = k.shape
    segs, strips = lax.axis_size("seg"), lax.axis_size("gx")
    world, pairs = segs * strips, vectors * vectors
    fields = vectors + 2
    onward = functools.partial(lax.ppermute, axis_name="seg", perm=shift_pairs(segs, 1))
    sideways = functools.partial(lax.ppermute, axis_name=("seg", "gx"), perm=rim_pairs(segs, strips, False))
    ahead = functools.partial(lax.ppermute, axis_name=("seg", "gx"), perm=rim_pairs(segs, strips, True))

    head, tail = call(
        pack_kernel,
        [(fields, STEPS, cols)] * 2,
        [ANY] * 3,
        [buffer(fields, TILE, cols), buffer(fields, TILE, cols), pltpu.SemaphoreType.DMA((2, 3))],
        1,
        limit=FULL,
    )(k, ax, ay)
    right = lax.ppermute(head, "gx", shift_pairs(strips, -1))
    left = lax.ppermute(tail, "gx", shift_pairs(strips, 1))
    drift = onward(drifts)
    (mid,) = call(
        inner_kernel,
        [(vectors, rows - 2 * TILE, cols)],
        [SMEM, VMEM, VMEM, VMEM],
        [buffer(vectors, rows, cols), buffer(4, rows, cols)],
        64,
    )(step_counts, k, ax, ay)
    lo, hi, upper = call(
        outer_kernel,
        [(vectors, TILE, cols), (vectors, TILE, cols), (vectors, 2 * TILE, cols)],
        [SMEM] + [VMEM] * 6,
        [buffer(vectors, 5 * TILE, cols), buffer(4, 5 * TILE, cols)],
        1,
    )(step_counts, k, ax, ay, left, right, mid)
    mid = onward(mid)
    hi = onward(hi)
    lo = onward(lo)
    upper = ahead(upper)
    near = mid[:, -(DRIFT - TILE) :]
    rim_mid = sideways(near)
    rim_hi = sideways(lax.optimization_barrier((hi, near))[0])
    product, gram = call(
        last_kernel,
        [k.shape, (world, pairs)],
        [SMEM] + [VMEM] * 7,
        [buffer(*k.shape), pltpu.SemaphoreType.DMA((vectors,))],
        1,
        places=[ANY, VMEM],
    )(drift, k, mid, lo, hi, rim_mid, rim_hi, upper)
    gram = lax.all_to_all(gram, ("seg", "gx"), 0, 0)
    cells = world * rows * cols
    gram = jnp.sum(gram, axis=0).reshape(vectors, vectors) / jnp.float32(cells)
    return product[None], gram


def solution(mesh):
    return jax.shard_map(
        body,
        mesh=mesh,
        in_specs=(
            P("seg", None, "gx", None),
            P("seg", "gx", None),
            P("seg", "gx", None),
            P("seg"),
            P("seg"),
        ),
        out_specs=(P("seg", None, "gx", None), P()),
        check_vma=False,
    )
```

time: 71 us -> 77.3 us (1.089); the launches traced: 69.9 us -> 77.1 us
  blocking collectives: 0 us -> 25.9 us
  waiting for transfers between devices: 28.5 us -> 21.1 us
  starting transfers between devices: 26.2 us -> 20.6 us
  Pallas kernels: 10.1 us -> 7.1 us
  local copies, waits for them, and re-layouts: 3.46 us -> 0.71 us
    all_to_all x0 -> x1, blocking collectives: none -> 25.9 us  [body(): gram = lax.all_to_all(gram, ('seg', 'gx'), 0, 0)]
    all_to_all x1 -> x0, waiting for transfers between devices: 11 us -> none  [body(): gram = lax.all_to_all(gram, ('seg', 'gx'), 0, 0)]
    all_to_all x1 -> x0, starting transfers between devices: 7.06 us -> none  [body(): gram = lax.all_to_all(gram, ('seg', 'gx'), 0, 0)]
    ppermute x1, waiting for transfers between devices: 0.01 us -> 6.68 us  [body(): drift = onward(drifts)]
    ppermute x8, waiting for transfers between devices: 17.5 us -> 14.4 us  [the longest x1 9.54 us: body(): mid = onward(mid)]
    pallas_call x5 -> x4, Pallas kernels: 10.1 us -> 7.1 us  [the longest x1 1.96 us: body(): call(pack_kernel, [(fields, STEPS, cols)] * 2, [ANY] * 3, [buffer(fields,...]
    slice x5 -> x1, local copies, waits for them, and re-layouts: 2.77 us -> 0.02 us  [body(): near = mid[:, -(DRIFT - TILE):]]
    ppermute x8, starting transfers between devices: 17.9 us -> 20.5 us  [the longest x1 6.31 us: body(): rim_mid = sideways(near)]
  transfers between devices with their start and end apart: 10 -> 9, of which waited for: 6 -> 3; matrix products, arithmetic and copies ran while one was open for 0% -> 0% of each run, Pallas kernels for 14% -> 4%
where the time goes in v5:
time: 77.3 us; the launch traced here: 77.1 us
  blocking collectives  25.9 us (34%)
  waiting for transfers between devices  21.1 us (27%)
  starting transfers between devices  20.6 us (27%)
  Pallas kernels  7.1 us (9%)
  between operations  1.42 us (2%)
    all_to_all x1, blocking collectives, body(): gram = lax.all_to_all(gram, ('seg', 'gx'), 0, 0)  25.9 us
    ppermute x1, waiting for transfers between devices, body(): mid = onward(mid)  9.54 us
    ppermute x1, waiting for transfers between devices, body(): drift = onward(drifts)  6.68 us
    ppermute x1, starting transfers between devices, body(): rim_mid = sideways(near)  6.31 us
    ppermute x1, starting transfers between devices, body(): rim_hi = sideways(lax.optimization_barrier((hi, near))[0])  5.57 us
    ppermute x1, waiting for transfers between devices, body(): right = lax.ppermute(head, 'gx', shift_pairs(strips, -1))  4.82 us
    ppermute x1, starting transfers between devices, body(): left = lax.ppermute(tail, 'gx', shift_pairs(strips, 1))  4.46 us
    ppermute x1, starting transfers between devices, body(): lo = onward(lo)  2.18 us
  transfers between devices with their start and end apart: 9, of which 3 were waited for; matrix products, arithmetic and copies ran while one was open for 0% of the time, Pallas kernels for 4%

profile of v5, /device:TPU:1, one launch (start us, length us, event | category | flops | bytes accessed | tf_op | source)
XLA Modules:
  0.0 77.1 jit_solution(18406530624864964850)
XLA Ops:
  0.7 2.0 %shard_map.69 = (f32[10,4,1024]{2,1,0:T(4,128)}, f32[10,4,1024]{2,1,0:T(4,128)}) custom-call(f32[8,32,1024]{2,1,0:T(8,128)} %bitcast.8, f32[32,1024]{1,0:T(8,128)} %bitcast.12, f32[32,1024]{1,0:T(8,128)} %bitcast.15), custom_call_target="tpu_custom_call" | custom-call | flops 1073741824 | bytes 4194304 | tf_op jit(solution)/shard_map/pallas_call | solution.py:191
  2.6 4.5 %collective-permute-start.2 = (f32[10,4,1024]{2,1,0:T(4,128)}, f32[10,4,1024]{2,1,0:T(4,128)S(1)}, u32[]{:S(2)}, u32[]{:S(2)}) collective-permute-start(f32[10,4,1024]{2,1,0:T(4,128)} %get-tuple-element.10), channel_id=1, source_target_pairs={{0,1},{1,2},{2,3},{3,4},{4,5},{5,6},{6,7},{7,0},{8,9},{9,10},{10,1... | collective-permute-start | bytes 491528 | tf_op jit(solution)/shard_map/ppermute | solution.py:200
  7.1 0.0 collective-permute-start.3
  7.8 1.4 %shard_map.68.mid_ref = f32[8,16,1024]{2,1,0:T(8,128)S(1)} custom-call(s32[1]{0:T(128)S(6)} %copy.8.count_ref, f32[8,32,1024]{2,1,0:T(8,128)S(1)} %bitcast.9, f32[32,1024]{1,0:T(8,128)S(1)} %bitcast.13, f32[32,1024]{1,0:T(8,128)S(1)} %bitcast.16), custom_call_target="tpu_custom_call" | custom-call | flops 68719476736 | bytes 4194304 | tf_op jit(solution)/shard_map/pallas_call | solution.py:202
  9.2 0.8 collective-permute-start.1
  9.9 0.0 collective-permute-done.2.left_ref
  9.9 4.8 %collective-permute-done.3.right_ref = f32[10,4,1024]{2,1,0:T(4,128)S(1)} collective-permute-done((f32[10,4,1024]{2,1,0:T(4,128)}, f32[10,4,1024]{2,1,0:T(4,128)S(1)}, u32[]{:S(2)}, u32[]{:S(2)}) %collective-permute-start.3) | collective-permute-done | bytes 163872 | tf_op jit(solution)/shard_map/ppermute | solution.py:199
  14.7 1.8 %shard_map.70 = (f32[8,8,1024]{2,1,0:T(8,128)S(1)}, f32[8,8,1024]{2,1,0:T(8,128)S(1)}, f32[8,16,1024]{2,1,0:T(8,128)S(1)}) custom-call(s32[1]{0:T(128)S(6)} %copy.8.count_ref, f32[8,32,1024]{2,1,0:T(8,128)S(1)} %bitcast.10, f32[32,1024]{1,0:T(8,128)S(1)} %bitcast.14, f32[32,1024]{1,0:T(8,128)S(1)} %bitcast.17, ...), custom_call_target="tpu_custom_call" | custom-call | flops 1073741824 | bytes 4194304 | tf_op jit(solution)/shard_map/pallas_call | solution.py:209
  16.6 0.6 collective-permute-start.5
  17.1 0.7 collective-permute-start.8
  17.8 2.2 %collective-permute-start.4 = (f32[8,8,1024]{2,1,0:T(8,128)S(1)}, f32[8,8,1024]{2,1,0:T(8,128)S(1)}, u32[]{:S(2)}, u32[]{:S(2)}) collective-permute-start(f32[8,8,1024]{2,1,0:T(8,128)S(1)} %get-tuple-element.12), channel_id=1, source_target_pairs={{0,8},{8,16},{16,24},{24,32},{32,40},{40,48},{48,56},{56,64},{64,7... | collective-permute-start | bytes 786440 | tf_op jit(solution)/shard_map/ppermute | solution.py:218
  20.0 9.5 %collective-permute-done.1.mid_ref = f32[8,16,1024]{2,1,0:T(8,128)S(1)} collective-permute-done((f32[8,16,1024]{2,1,0:T(8,128)S(1)}, f32[8,16,1024]{2,1,0:T(8,128)S(1)}, u32[]{:S(2)}, u32[]{:S(2)}) %collective-permute-start.1) | collective-permute-done | bytes 524320 | tf_op jit(solution)/shard_map/ppermute | solution.py:216
  29.6 6.3 %collective-permute-start.6 = (f32[8,8,1024]{2,1,0:T(8,128)S(1)}, f32[8,8,1024]{2,1,0:T(8,128)S(1)}, u32[]{:S(2)}, u32[]{:S(2)}) collective-permute-start(f32[8,8,1024]{2,1,0:T(8,128)S(1)} %slice.4), channel_id=1, source_target_pairs={{0,1},{1,2},{2,3},{3,4},{4,5},{5,6},{6,7},{7,0},{8,9},{9,10},{10,1... | collective-permute-start | bytes 786440 | tf_op jit(solution)/shard_map/ppermute | solution.py:221
  35.9 0.0 collective-permute-done.5.hi_ref
  35.9 5.6 %collective-permute-start.7 = (f32[8,8,1024]{2,1,0:T(8,128)S(1)}, f32[8,8,1024]{2,1,0:T(8,128)S(1)}, u32[]{:S(2)}, u32[]{:S(2)}) collective-permute-start(f32[8,8,1024]{2,1,0:T(8,128)S(1)} %collective-permute-done.5.hi_ref), channel_id=1, source_target_pairs={{0,1},{1,2},{2,3},{3,4},{4,5},{5,6},{6,7},{7,0},{8,9},{9,10},{10,1... | collective-permute-start | bytes 786440 | tf_op jit(solution)/shard_map/ppermute | solution.py:222
  41.5 0.1 collective-permute-start
  41.6 6.7 %collective-permute-done.drift_ref = s32[1]{0:T(128)} collective-permute-done((s32[1]{0:T(128)}, s32[1]{0:T(128)}, u32[]{:S(2)}, u32[]{:S(2)}) %collective-permute-start) | collective-permute-done | bytes 36 | tf_op jit(solution)/shard_map/ppermute | solution.py:201
  48.2 0.0 collective-permute-done.4.lo_ref
  48.3 0.0 collective-permute-done.8.upper_ref
  48.3 0.0 collective-permute-done.6.rim_mid_ref
  48.3 1.9 %shard_map.71 = (f32[8,32,1024]{2,1,0:T(8,128)}, f32[256,64]{1,0:T(8,128)S(1)}) custom-call(s32[1]{0:T(128)} %collective-permute-done.drift_ref, f32[8,32,1024]{2,1,0:T(8,128)S(1)} %bitcast.11, f32[8,16,1024]{2,1,0:T(8,128)S(1)} %collective-permute-done.1.mid_ref, f32[8,8,1024]{2,1,0:T(8,128)S(1)} %collective-permute-done.4.lo_ref, ...), custom_call_target="tpu_custom_call" | custom-call | flops 1073741824 | bytes 4194304 | tf_op jit(solution)/shard_map/pallas_call | solution.py:223
  50.2 25.9 %all_to_all.9 = f32[256,1,64]{2,1,0:T(1,128)S(1)} all-to-all(f32[256,1,64]{2,1,0:T(1,128)S(1)} %bitcast.7), channel_id=1, replica_groups=mesh['seg'=32,'gx'=8] {'seg','gx'}, dimensions={0} | all-to-all | bytes 131072 | tf_op jit(solution)/shard_map/all_to_all | solution.py:231
  76.1 0.3 reduce_sum.9
  76.4 0.7 div.10
  (9 shorter events, 0.0 us)
Async XLA Ops:
  0.6 7.1 %copy-start = (f32[1,8,32,1024]{3,2,1,0:T(8,128)S(1)}, f32[1,8,32,1024]{3,2,1,0:T(8,128)}, u32[]{:S(2)}) copy-start(f32[1,8,32,1024]{3,2,1,0:T(8,128)} %param.5) | copy-start | bytes 3145732
  0.6 7.1 %copy-start.1 = (f32[1,32,1024]{2,1,0:T(8,128)S(1)}, f32[1,32,1024]{2,1,0:T(8,128)}, u32[]{:S(2)}) copy-start(f32[1,32,1024]{2,1,0:T(8,128)} %param.6) | copy-start | bytes 393220
  0.6 7.1 %copy-start.2 = (f32[1,32,1024]{2,1,0:T(8,128)S(1)}, f32[1,32,1024]{2,1,0:T(8,128)}, u32[]{:S(2)}) copy-start(f32[1,32,1024]{2,1,0:T(8,128)} %param.7) | copy-start | bytes 393220
  2.6 7.3 %collective-permute-start.2 = (f32[10,4,1024]{2,1,0:T(4,128)}, f32[10,4,1024]{2,1,0:T(4,128)S(1)}, u32[]{:S(2)}, u32[]{:S(2)}) collective-permute-start(f32[10,4,1024]{2,1,0:T(4,128)} %get-tuple-element.10), channel_id=1, source_target_pairs={{0,1},{1,2},{2,3},{3,4},{4,5},{5,6},{6,7},{7,0},{8,9},{9,10},{10,1... | collective-permute-start | bytes 491528 | tf_op jit(solution)/shard_map/ppermute | solution.py:200
  7.1 7.7 %collective-permute-start.3 = (f32[10,4,1024]{2,1,0:T(4,128)}, f32[10,4,1024]{2,1,0:T(4,128)S(1)}, u32[]{:S(2)}, u32[]{:S(2)}) collective-permute-start(f32[10,4,1024]{2,1,0:T(4,128)} %get-tuple-element.11), channel_id=1, source_target_pairs={{0,7},{1,0},{2,1},{3,2},{4,3},{5,4},{6,5},{7,6},{8,15},{9,8},{10,9... | collective-permute-start | bytes 491528 | tf_op jit(solution)/shard_map/ppermute | solution.py:199
  9.2 20.4 %collective-permute-start.1 = (f32[8,16,1024]{2,1,0:T(8,128)S(1)}, f32[8,16,1024]{2,1,0:T(8,128)S(1)}, u32[]{:S(2)}, u32[]{:S(2)}) collective-permute-start(f32[8,16,1024]{2,1,0:T(8,128)S(1)} %shard_map.68.mid_ref), channel_id=1, source_target_pairs={{0,8},{8,16},{16,24},{24,32},{32,40},{40,48},{48,56},{56,64},{64,7... | collective-permute-start | bytes 1572872 | tf_op jit(solution)/shard_map/ppermute | solution.py:216
  16.6 19.3 %collective-permute-start.5 = (f32[8,8,1024]{2,1,0:T(8,128)S(1)}, f32[8,8,1024]{2,1,0:T(8,128)S(1)}, u32[]{:S(2)}, u32[]{:S(2)}) collective-permute-start(f32[8,8,1024]{2,1,0:T(8,128)S(1)} %get-tuple-element.13), channel_id=1, source_target_pairs={{0,8},{8,16},{16,24},{24,32},{32,40},{40,48},{48,56},{56,64},{64,7... | collective-permute-start | bytes 786440 | tf_op jit(solution)/shard_map/ppermute | solution.py:217
  17.1 31.1 %collective-permute-start.8 = (f32[8,16,1024]{2,1,0:T(8,128)S(1)}, f32[8,16,1024]{2,1,0:T(8,128)S(1)}, u32[]{:S(2)}, u32[]{:S(2)}) collective-permute-start(f32[8,16,1024]{2,1,0:T(8,128)S(1)} %get-tuple-element.15), channel_id=1, source_target_pairs={{113,122},{115,124},{117,126},{119,120},{241,250},{243,252},{245,2... | collective-permute-start | bytes 1572872 | tf_op jit(solution)/shard_map/ppermute | solution.py:219
  17.8 30.4 %collective-permute-start.4 = (f32[8,8,1024]{2,1,0:T(8,128)S(1)}, f32[8,8,1024]{2,1,0:T(8,128)S(1)}, u32[]{:S(2)}, u32[]{:S(2)}) collective-permute-start(f32[8,8,1024]{2,1,0:T(8,128)S(1)} %get-tuple-element.12), channel_id=1, source_target_pairs={{0,8},{8,16},{16,24},{24,32},{32,40},{40,48},{48,56},{56,64},{64,7... | collective-permute-start | bytes 786440 | tf_op jit(solution)/shard_map/ppermute | solution.py:218
  29.6 18.7 %collective-permute-start.6 = (f32[8,8,1024]{2,1,0:T(8,128)S(1)}, f32[8,8,1024]{2,1,0:T(8,128)S(1)}, u32[]{:S(2)}, u32[]{:S(2)}) collective-permute-start(f32[8,8,1024]{2,1,0:T(8,128)S(1)} %slice.4), channel_id=1, source_target_pairs={{0,1},{1,2},{2,3},{3,4},{4,5},{5,6},{6,7},{7,0},{8,9},{9,10},{10,1... | collective-permute-start | bytes 786440 | tf_op jit(solution)/shard_map/ppermute | solution.py:221
  35.9 12.4 %collective-permute-start.7 = (f32[8,8,1024]{2,1,0:T(8,128)S(1)}, f32[8,8,1024]{2,1,0:T(8,128)S(1)}, u32[]{:S(2)}, u32[]{:S(2)}) collective-permute-start(f32[8,8,1024]{2,1,0:T(8,128)S(1)} %collective-permute-done.5.hi_ref), channel_id=1, source_target_pairs={{0,1},{1,2},{2,3},{3,4},{4,5},{5,6},{6,7},{7,0},{8,9},{9,10},{10,1... | collective-permute-start | bytes 786440 | tf_op jit(solution)/shard_map/ppermute | solution.py:222
  41.5 6.8 %collective-permute-start = (s32[1]{0:T(128)}, s32[1]{0:T(128)}, u32[]{:S(2)}, u32[]{:S(2)}) collective-permute-start(s32[1]{0:T(128)} %param.9), channel_id=1, source_target_pairs={{0,8},{8,16},{16,24},{24,32},{32,40},{40,48},{48,56},{56,64},{64,7... | collective-permute-start | bytes 20 | tf_op jit(solution)/shard_map/ppermute | solution.py:201

commit v6 on v5

v6 whole, which is shorter than its diff:
```python
import functools
import jax
import jax.numpy as jnp
from jax import lax
from jax.experimental import pallas as pl
from jax.experimental.pallas import tpu as pltpu
from jax.sharding import PartitionSpec as P

STEPS = 4
DRIFT = 16
TILE = 8

ANY = pl.BlockSpec(memory_space=pl.ANY)
VMEM = pl.BlockSpec(memory_space=pltpu.VMEM)
SMEM = pl.BlockSpec(memory_space=pltpu.SMEM)
LIMIT = 12 * 1024 * 1024
FULL = 60 * 1024 * 1024


def shift_pairs(count, by):
    return [(i, (i + by) % count) for i in range(count)]


def weights(ax, ay):
    col = lax.broadcasted_iota(jnp.int32, ax.shape, 1)
    last = ax.shape[1] - 1
    return (
        0.2 - ax,
        0.2 + ax,
        jnp.where(col == last, 0.0, 0.2 - ay),
        jnp.where(col == 0, 0.0, 0.2 + ay),
    )


def step(q, we, ww, wn, ws):
    rows, cols = q.shape
    return (
        0.2 * q
        + we * pltpu.roll(q, rows - 1, 0)
        + ww * pltpu.roll(q, 1, 0)
        + wn * pltpu.roll(q, cols - 1, 1)
        + ws * pltpu.roll(q, 1, 1)
    )


def inner_kernel(
    count_ref, k_any, ax_any, ay_any, mid_any, beyond_any, head_ref, tail_ref, k_ref, a_ref, q_ref, w_ref, sems, out_sems
):
    vectors, rows, _ = k_ref.shape
    half = vectors // 2
    groups = [pl.ds(0, half), pl.ds(half, vectors - half)]
    copies = [
        pltpu.make_async_copy(ax_any, a_ref.at[0], sems.at[0]),
        pltpu.make_async_copy(ay_any, a_ref.at[1], sems.at[1]),
    ] + [pltpu.make_async_copy(k_any.at[group], k_ref.at[group], sems.at[2 + i]) for i, group in enumerate(groups)]
    beyond = pltpu.make_async_copy(k_any.at[:, pl.ds(0, DRIFT)], beyond_any, out_sems.at[2])
    for copy in copies:
        copy.start()
    beyond.start()
    for i in range(2):
        copies[i].wait()
        head_ref[vectors + i] = a_ref[i, :STEPS]
        tail_ref[vectors + i] = a_ref[i, rows - STEPS :]
    for i, w in enumerate(weights(a_ref[0], a_ref[1])):
        w_ref[i] = w
    outs = []
    for i, group in enumerate(groups):
        copies[2 + i].wait()
        first, size = group.start, group.size
        head_ref[first : first + size] = k_ref[first : first + size, :STEPS]
        tail_ref[first : first + size] = k_ref[first : first + size, rows - STEPS :]
        q_ref[first : first + size] = k_ref[first : first + size]

        @pl.loop(0, count_ref[0])
        def _(_):
            for b in range(first, first + size):
                q_ref[b] = step(q_ref[b], w_ref[0], w_ref[1], w_ref[2], w_ref[3])

        outs.append(
            pltpu.make_async_copy(q_ref.at[group, pl.ds(TILE, rows - 2 * TILE)], mid_any.at[group], out_sems.at[i])
        )
        outs[i].start()
    for copy in outs + [beyond]:
        copy.wait()


def outer_kernel(count_ref, k_ref, ax_ref, ay_ref, left_ref, right_ref, lo_ref, hi_ref, table_ref, q_ref, w_ref):
    vectors, rows, _ = k_ref.shape

    def around(strip, at):
        return jnp.concatenate(
            [strip[rows - 2 * TILE :], right_ref[at], left_ref[at], strip[: 2 * TILE]], axis=0
        )

    for i, w in enumerate(weights(around(ax_ref, vectors), around(ay_ref, vectors + 1))):
        w_ref[i] = w
    for b in range(vectors):
        q_ref[b] = around(k_ref.at[b], b)

    @pl.loop(0, count_ref[0])
    def _(_):
        for b in range(vectors):
            q_ref[b] = step(q_ref[b], w_ref[0], w_ref[1], w_ref[2], w_ref[3])

    hi_ref[...] = q_ref[:, TILE : 2 * TILE]
    lo_ref[...] = q_ref[:, 3 * TILE : 4 * TILE]
    tile = functools.partial(tile_of, k_ref)
    table_ref[...] = pair_sums(tile, tile, rows // TILE, vectors, k_ref.shape[2])


def pair_sums(left, right, blocks, vectors, cols):
    sums = []
    half = vectors // 2
    for first in range(0, vectors, half):
        accs = {}
        for block in range(blocks):
            for lane in range(0, cols, 128):
                rs = [right(c, block, lane) for c in range(vectors)]
                for a in range(first, first + half):
                    value = left(a, block, lane)
                    for c in range(vectors):
                        term = value * rs[c]
                        accs[a, c] = accs[a, c] + term if (a, c) in accs else term
        sums += [jnp.sum(accs[a, c], axis=0, keepdims=True) for a in range(first, first + half) for c in range(vectors)]
    return jnp.concatenate(sums, axis=0)


def tile_of(ref, v, block, lane):
    return ref[v, block * TILE : (block + 1) * TILE, lane : lane + 128]


def gram_kernel(
    drift_ref, k_ref, beyond_ref, lo_ref, mid_ref, hi_ref, upper_ref, own_ref, gram_ref, shifted_ref, before_ref
):
    vectors, rows, cols = k_ref.shape
    drift = drift_ref[0]
    blocks = rows // TILE
    total = rows + DRIFT
    back = lax.rem(total - drift, total)
    row = lax.broadcasted_iota(jnp.int32, (DRIFT, cols), 0)
    for b in range(vectors):
        joined = jnp.concatenate([k_ref[b], beyond_ref[b]], axis=0)
        shifted_ref[b] = pltpu.roll(joined, back, 0)[:rows]
        before_ref[b] = jnp.where(row < drift, pltpu.roll(upper_ref[b], lax.rem(drift, DRIFT), 0), 0.0)

    def left(a, block, lane):
        if block < blocks:
            return tile_of(shifted_ref, a, block, lane)
        return tile_of(k_ref, a, block - blocks, lane)

    def right(c, block, lane):
        if block == 0:
            return tile_of(lo_ref, c, 0, lane)
        if block < blocks - 1:
            return tile_of(mid_ref, c, block - 1, lane)
        if block == blocks - 1:
            return tile_of(hi_ref, c, 0, lane)
        return tile_of(before_ref, c, block - blocks, lane)

    table = own_ref[...] - pair_sums(left, right, blocks + DRIFT // TILE, vectors, cols)
    ones = jnp.ones((gram_ref.shape[0], 128), jnp.float32)
    gram_ref[...] = lax.dot_general(
        ones, table, (((1,), (1,)), ((), ())),
        precision=lax.Precision.HIGHEST, preferred_element_type=jnp.float32,
    )


def last_kernel(drift_ref, k_ref, mid_ref, lo_ref, hi_ref, rim_mid_ref, rim_hi_ref, upper_ref, product_ref):
    vectors, rows, _ = k_ref.shape
    total = DRIFT + rows
    by = lax.rem(drift_ref[0] + (total - DRIFT), total)
    for b in range(vectors):
        joined = jnp.concatenate(
            [
                rim_mid_ref[b] + upper_ref[b, :TILE],
                rim_hi_ref[b] + upper_ref[b, TILE:],
                lo_ref[b],
                mid_ref[b],
                hi_ref[b],
            ],
            axis=0,
        )
        product_ref[b] = k_ref[b] - pltpu.roll(joined, by, 0)[:rows]


def buffer(*shape):
    return pltpu.VMEM(shape, jnp.float32)


def call(kernel, outs, ins, scratch, cost, limit=LIMIT, places=None):
    return pl.pallas_call(
        kernel,
        out_shape=[jax.ShapeDtypeStruct(o, jnp.float32) for o in outs],
        in_specs=ins,
        out_specs=places or [VMEM] * len(outs),
        scratch_shapes=scratch,
        compiler_params=pltpu.CompilerParams(vmem_limit_bytes=limit),
        cost_estimate=pl.CostEstimate(flops=cost << 30, bytes_accessed=cost << 20, transcendentals=0),
    )


def rim_pairs(segs, strips, direct):
    pairs = []
    for s in range(segs):
        for g in range(strips):
            busy = (s + 1) % (segs // 2) == 0 and g % 2 == 1
            if busy == direct:
                pairs.append(((s - direct) * strips + g, s * strips + (g + 1) % strips))
    return pairs


def body(krylov, advect_x, advect_y, step_counts, drifts):
    k, ax, ay = krylov[0], advect_x[0], advect_y[0]
    vectors, rows, cols = k.shape
    segs, strips = lax.axis_size("seg"), lax.axis_size("gx")
    world, pairs = segs * strips, vectors * vectors
    fields = vectors + 2
    onward = functools.partial(lax.ppermute, axis_name="seg", perm=shift_pairs(segs, 1))
    along = rim_pairs(segs, strips, False)
    sideways = functools.partial(lax.ppermute, axis_name=("seg", "gx"), perm=along)
    backward = functools.partial(lax.ppermute, axis_name=("seg", "gx"), perm=[(b, a) for a, b in along])
    ahead = functools.partial(lax.ppermute, axis_name=("seg", "gx"), perm=rim_pairs(segs, strips, True))

    mid, beyond, head, tail = call(
        inner_kernel,
        [(vectors, rows - 2 * TILE, cols), (vectors, DRIFT, cols)] + [(fields, STEPS, cols)] * 2,
        [SMEM, ANY, ANY, ANY],
        [
            buffer(vectors, rows, cols),
            buffer(2, rows, cols),
            buffer(vectors, rows, cols),
            buffer(4, rows, cols),
            pltpu.SemaphoreType.DMA((4,)),
            pltpu.SemaphoreType.DMA((3,)),
        ],
        64,
        limit=FULL,
        places=[ANY, ANY, VMEM, VMEM],
    )(step_counts, k, ax, ay)
    right = lax.ppermute(head, "gx", shift_pairs(strips, -1))
    left = lax.ppermute(tail, "gx", shift_pairs(strips, 1))
    drift = onward(drifts)
    lo, hi, own = call(
        outer_kernel,
        [(vectors, TILE, cols), (vectors, TILE, cols), (pairs, 128)],
        [SMEM] + [VMEM] * 5,
        [buffer(vectors, 5 * TILE, cols), buffer(4, 5 * TILE, cols)],
        0,
    )(step_counts, k, ax, ay, left, right)
    upper = ahead(jnp.concatenate([mid[:, -(DRIFT - TILE) :], hi], axis=1))
    beyond = backward(beyond)
    mid = onward(mid)
    hi = onward(hi)
    lo = onward(lo)
    near = mid[:, -(DRIFT - TILE) :]
    rim_mid = sideways(near)
    rim_hi = sideways(lax.optimization_barrier((hi, near))[0])
    (gram,) = call(
        gram_kernel,
        [(world, pairs)],
        [SMEM] + [VMEM] * 7,
        [buffer(*k.shape), buffer(vectors, DRIFT, cols)],
        1,
    )(drift, k, beyond, lo, mid, hi, upper, own)
    gram = lax.all_to_all(gram, ("seg", "gx"), 0, 0)
    (product,) = call(last_kernel, [k.shape], [SMEM] + [VMEM] * 7, [], 1)(
        drift, k, mid, lo, hi, rim_mid, rim_hi, upper
    )
    product, gram = lax.optimization_barrier((product, gram))
    cells = world * rows * cols
    gram = jnp.sum(gram, axis=0).reshape(vectors, vectors) / jnp.float32(cells)
    return product[None], gram


def solution(mesh):
    return jax.shard_map(
        body,
        mesh=mesh,
        in_specs=(
            P("seg", None, "gx", None),
            P("seg", "gx", None),
            P("seg", "gx", None),
            P("seg"),
            P("seg"),
        ),
        out_specs=(P("seg", None, "gx", None), P()),
        check_vma=False,
    )
```

time: 77.3 us -> 86.2 us (1.12)
  blocking collectives: 25.9 us -> 0 us
  Pallas kernels: 7.1 us -> 26 us
  starting transfers between devices: 20.6 us -> 33.1 us
  waiting for transfers between devices: 21.1 us -> 23.6 us
  local copies, waits for them, and re-layouts: 0.71 us -> 1.68 us
    all_to_all x1 -> x0, blocking collectives: 25.9 us -> none  [body(): gram = lax.all_to_all(gram, ('seg', 'gx'), 0, 0)]
    pallas_call x4, Pallas kernels: 7.1 us -> 26 us  [the longest x1 17.8 us: body(): call(inner_kernel, [(vectors, rows - 2 * TILE, cols), (vectors, DRIFT, co...]
    all_to_all x0 -> x1, waiting for transfers between devices: none -> 11 us  [body(): gram = lax.all_to_all(gram, ('seg', 'gx'), 0, 0)]
    all_to_all x0 -> x1, starting transfers between devices: none -> 7.08 us  [body(): gram = lax.all_to_all(gram, ('seg', 'gx'), 0, 0)]
    ppermute x1, waiting for transfers between devices: 6.68 us -> 0.01 us  [body(): drift = onward(drifts)]
    ppermute x1, waiting for transfers between devices: 0.01 us -> 5.59 us  [body(): hi = onward(hi)]
    ppermute x1 -> x2, starting transfers between devices: 0.68 us -> 5.95 us  [the longest x1 5.26 us: body(): beyond = backward(beyond)]
    ppermute x1, waiting for transfers between devices: 4.82 us -> 0.1 us  [body(): right = lax.ppermute(head, 'gx', shift_pairs(strips, -1))]
  transfers between devices with their start and end apart: 9 -> 11, of which waited for: 3 -> 4; matrix products, arithmetic and copies ran while one was open for 0% -> 1% of each run, Pallas kernels for 4% -> 10%
where the time goes in v6:
time: 86.2 us; the launch traced here: 85.9 us
  starting transfers between devices  33.1 us (38%)
  Pallas kernels  26 us (30%)
  waiting for transfers between devices  23.6 us (27%)
  local copies, waits for them, and re-layouts  1.68 us (2%)
  between operations  1.42 us (2%)
    pallas_call x1, Pallas kernels, body(): call(inner_kernel, [(vectors, rows - 2 * TILE, cols), (vectors, DRIFT, co...  17.8 us
    all_to_all x1, waiting for transfers between devices, body(): gram = lax.all_to_all(gram, ('seg', 'gx'), 0, 0)  11 us
    ppermute x1, starting transfers between devices, body(): rim_hi = sideways(lax.optimization_barrier((hi, near))[0])  9.06 us
    all_to_all x1, starting transfers between devices, body(): gram = lax.all_to_all(gram, ('seg', 'gx'), 0, 0)  7.08 us
    ppermute x1, waiting for transfers between devices, body(): mid = onward(mid)  6.83 us
    ppermute x1, waiting for transfers between devices, body(): hi = onward(hi)  5.59 us
    ppermute x1, starting transfers between devices, body(): beyond = backward(beyond)  5.26 us
    ppermute x1, starting transfers between devices, body(): rim_mid = sideways(near)  5.04 us
  transfers between devices with their start and end apart: 11, of which 4 were waited for; matrix products, arithmetic and copies ran while one was open for 1% of the time, Pallas kernels for 10%

profile of v6, /device:TPU:1, one launch (start us, length us, event | category | flops | bytes accessed | tf_op | source)
XLA Modules:
  0.0 85.9 jit_solution(13670772543348222032)
XLA Ops:
  1.3 17.8 %shard_map.68 = (f32[8,16,1024]{2,1,0:T(8,128)}, f32[8,16,1024]{2,1,0:T(8,128)}, f32[10,4,1024]{2,1,0:T(4,128)}, f32[10,4,1024]{2,1,0:T(4,128)}) custom-call(s32[1]{0:T(128)S(6)} %copy.8.count_ref, f32[8,32,1024]{2,1,0:T(8,128)} %bitcast.8, f32[32,1024]{1,0:T(8,128)} %bitcast.12, f32[32,1024]{1,0:T(8,128)} %bitcast.14), custom_call_target="tpu_custom_call" | custom-call | flops 68719476736 | bytes 67108864 | tf_op jit(solution)/shard_map/pallas_call | solution.py:224
  19.1 4.5 %collective-permute-start.2 = (f32[10,4,1024]{2,1,0:T(4,128)}, f32[10,4,1024]{2,1,0:T(4,128)S(1)}, u32[]{:S(2)}, u32[]{:S(2)}) collective-permute-start(f32[10,4,1024]{2,1,0:T(4,128)} %get-tuple-element.13), channel_id=1, source_target_pairs={{0,1},{1,2},{2,3},{3,4},{4,5},{5,6},{6,7},{7,0},{8,9},{9,10},{10,1... | collective-permute-start | bytes 491528 | tf_op jit(solution)/shard_map/ppermute | solution.py:241
  23.5 0.0 collective-permute-start.3
  23.5 1.3 %collective-permute-start.1 = (f32[8,16,1024]{2,1,0:T(8,128)}, f32[8,16,1024]{2,1,0:T(8,128)S(1)}, u32[]{:S(2)}, u32[]{:S(2)}) collective-permute-start(f32[8,16,1024]{2,1,0:T(8,128)} %get-tuple-element.12), channel_id=1, source_target_pairs={{0,8},{8,16},{16,24},{24,32},{32,40},{40,48},{48,56},{56,64},{64,7... | collective-permute-start | bytes 1572872 | tf_op jit(solution)/shard_map/ppermute | solution.py:252
  24.8 5.3 %collective-permute-start.9 = (f32[8,16,1024]{2,1,0:T(8,128)}, f32[8,16,1024]{2,1,0:T(8,128)S(1)}, u32[]{:S(2)}, u32[]{:S(2)}) collective-permute-start(f32[8,16,1024]{2,1,0:T(8,128)} %get-tuple-element.18), channel_id=1, source_target_pairs={{1,0},{2,1},{3,2},{4,3},{5,4},{6,5},{7,6},{0,7},{9,8},{10,9},{11,1... | collective-permute-start | bytes 1572872 | tf_op jit(solution)/shard_map/ppermute | solution.py:251
  30.1 1.0 %slice.7 = f32[8,8,1024]{2,1,0:T(8,128)S(1)} slice(f32[8,16,1024]{2,1,0:T(8,128)} %get-tuple-element.12), slice={[0:8], [8:16], [0:1024]} | slice | bytes 524288 | tf_op jit(solution)/shard_map/slice | solution.py:250
  31.1 0.1 collective-permute-done.3.right_ref
  31.2 3.8 %shard_map.69 = (f32[8,8,1024]{2,1,0:T(8,128)S(1)}, f32[8,8,1024]{2,1,0:T(8,128)S(1)}, f32[64,128]{1,0:T(8,128)S(1)}) custom-call(s32[1]{0:T(128)S(6)} %copy.8.count_ref, f32[8,32,1024]{2,1,0:T(8,128)S(1)} %bitcast.9, f32[32,1024]{1,0:T(8,128)S(1)} %bitcast.13, f32[32,1024]{1,0:T(8,128)S(1)} %bitcast.15, f32[10,4,1024]{2,1,0:T(4,128)S(1)} %collective-permute-done.2.left_ref, ...), custom_call_target="tpu_custom_call" | custom-call | tf_op jit(solution)/shard_map/pallas_call | solution.py:243
  35.0 0.7 collective-permute-start.8
  35.7 0.1 collective-permute-start.5
  35.8 0.2 collective-permute-start.4
  36.0 6.8 %collective-permute-done.1.mid_ref = f32[8,16,1024]{2,1,0:T(8,128)S(1)} collective-permute-done((f32[8,16,1024]{2,1,0:T(8,128)}, f32[8,16,1024]{2,1,0:T(8,128)S(1)}, u32[]{:S(2)}, u32[]{:S(2)}) %collective-permute-start.1) | collective-permute-done | bytes 524320 | tf_op jit(solution)/shard_map/ppermute | solution.py:252
  42.8 0.0 collective-permute-start
  42.8 5.6 %collective-permute-done.5.hi_ref = f32[8,8,1024]{2,1,0:T(8,128)S(1)} collective-permute-done((f32[8,8,1024]{2,1,0:T(8,128)S(1)}, f32[8,8,1024]{2,1,0:T(8,128)S(1)}, u32[]{:S(2)}, u32[]{:S(2)}) %collective-permute-start.5) | collective-permute-done | bytes 262176 | tf_op jit(solution)/shard_map/ppermute | solution.py:253
  48.4 9.1 %collective-permute-start.7 = (f32[8,8,1024]{2,1,0:T(8,128)S(1)}, f32[8,8,1024]{2,1,0:T(8,128)S(1)}, u32[]{:S(2)}, u32[]{:S(2)}) collective-permute-start(f32[8,8,1024]{2,1,0:T(8,128)S(1)} %collective-permute-done.5.hi_ref), channel_id=1, source_target_pairs={{0,1},{1,2},{2,3},{3,4},{4,5},{5,6},{6,7},{7,0},{8,9},{9,10},{10,1... | collective-permute-start | bytes 786440 | tf_op jit(solution)/shard_map/ppermute | solution.py:257
  57.5 5.0 %collective-permute-start.6 = (f32[8,8,1024]{2,1,0:T(8,128)S(1)}, f32[8,8,1024]{2,1,0:T(8,128)S(1)}, u32[]{:S(2)}, u32[]{:S(2)}) collective-permute-start(f32[8,8,1024]{2,1,0:T(8,128)S(1)} %slice.8), channel_id=1, source_target_pairs={{0,1},{1,2},{2,3},{3,4},{4,5},{5,6},{6,7},{7,0},{8,9},{9,10},{10,1... | collective-permute-start | bytes 786440 | tf_op jit(solution)/shard_map/ppermute | solution.py:256
  62.6 0.0 collective-permute-done.9.beyond_ref
  62.6 0.0 collective-permute-done.8.upper_ref
  62.6 2.7 %shard_map.71 = f32[256,64]{1,0:T(8,128)} custom-call(s32[1]{0:T(128)} %collective-permute-done.drift_ref, f32[8,32,1024]{2,1,0:T(8,128)S(1)} %bitcast.10, f32[8,16,1024]{2,1,0:T(8,128)S(1)} %collective-permute-done.9.beyond_ref, f32[8,8,1024]{2,1,0:T(8,128)S(1)} %collective-permute-done.4.lo_ref, f32[8,16,1024]{2,1,0:T(8,128)S(1)} %collective-permute-done.1.mid_ref, ...), custom_call_target="tpu_custom_call" | custom-call | flops 1073741824 | bytes 1048576 | tf_op jit(solution)/shard_map/pallas_call | solution.py:258
  65.2 7.1 %all-to-all-start = ((f32[256,1,64]{2,1,0:T(1,128)}), f32[256,1,64]{2,1,0:T(1,128)S(1)}, u32[]{:S(2)}, u32[]{:S(2)}) async-start(f32[256,1,64]{2,1,0:T(1,128)} %bitcast.4), calls=%async_computation | async-start | bytes 262144 | tf_op jit(solution)/shard_map/all_to_all | solution.py:265
  72.3 1.8 %shard_map.70 = f32[8,32,1024]{2,1,0:T(8,128)} custom-call(s32[1]{0:T(128)} %collective-permute-done.drift_ref, f32[8,32,1024]{2,1,0:T(8,128)S(1)} %bitcast.11, f32[8,16,1024]{2,1,0:T(8,128)S(1)} %collective-permute-done.1.mid_ref, f32[8,8,1024]{2,1,0:T(8,128)S(1)} %collective-permute-done.4.lo_ref, f32[8,8,1024]{2,1,0:T(8,128)S(1)} %collective-permute-done.5.hi_ref, ...), custom_call_target="tpu_custom_call" | custom-call | flops 1073741824 | bytes 1048576 | tf_op jit(solution)/shard_map/pallas_call | solution.py:266
  74.2 11.0 %all-to-all-done = f32[256,1,64]{2,1,0:T(1,128)S(1)} async-done(((f32[256,1,64]{2,1,0:T(1,128)}), f32[256,1,64]{2,1,0:T(1,128)S(1)}, u32[]{:S(2)}, u32[]{:S(2)}) %all-to-all-start) | async-done | bytes 65568 | tf_op jit(solution)/shard_map/all_to_all | solution.py:265
  85.2 0.1 reduce_sum.9
  85.3 0.7 div.10
  (14 shorter events, 0.1 us)
Async XLA Ops:
  1.3 29.9 %copy-start = (f32[1,8,32,1024]{3,2,1,0:T(8,128)S(1)}, f32[1,8,32,1024]{3,2,1,0:T(8,128)}, u32[]{:S(2)}) copy-start(f32[1,8,32,1024]{3,2,1,0:T(8,128)} %param.5) | copy-start | bytes 3145732
  19.1 12.0 %collective-permute-start.2 = (f32[10,4,1024]{2,1,0:T(4,128)}, f32[10,4,1024]{2,1,0:T(4,128)S(1)}, u32[]{:S(2)}, u32[]{:S(2)}) collective-permute-start(f32[10,4,1024]{2,1,0:T(4,128)} %get-tuple-element.13), channel_id=1, source_target_pairs={{0,1},{1,2},{2,3},{3,4},{4,5},{5,6},{6,7},{7,0},{8,9},{9,10},{10,1... | collective-permute-start | bytes 491528 | tf_op jit(solution)/shard_map/ppermute | solution.py:241
  23.5 7.7 %collective-permute-start.3 = (f32[10,4,1024]{2,1,0:T(4,128)}, f32[10,4,1024]{2,1,0:T(4,128)S(1)}, u32[]{:S(2)}, u32[]{:S(2)}) collective-permute-start(f32[10,4,1024]{2,1,0:T(4,128)} %get-tuple-element.14), channel_id=1, source_target_pairs={{0,7},{1,0},{2,1},{3,2},{4,3},{5,4},{6,5},{7,6},{8,15},{9,8},{10,9... | collective-permute-start | bytes 491528 | tf_op jit(solution)/shard_map/ppermute | solution.py:240
  23.5 19.3 %collective-permute-start.1 = (f32[8,16,1024]{2,1,0:T(8,128)}, f32[8,16,1024]{2,1,0:T(8,128)S(1)}, u32[]{:S(2)}, u32[]{:S(2)}) collective-permute-start(f32[8,16,1024]{2,1,0:T(8,128)} %get-tuple-element.12), channel_id=1, source_target_pairs={{0,8},{8,16},{16,24},{24,32},{32,40},{40,48},{48,56},{56,64},{64,7... | collective-permute-start | bytes 1572872 | tf_op jit(solution)/shard_map/ppermute | solution.py:252
  24.8 6.4 %copy-start.1 = (f32[1,32,1024]{2,1,0:T(8,128)S(1)}, f32[1,32,1024]{2,1,0:T(8,128)}, u32[]{:S(2)}) copy-start(f32[1,32,1024]{2,1,0:T(8,128)} %param.6) | copy-start | bytes 393220
  24.8 6.4 %copy-start.2 = (f32[1,32,1024]{2,1,0:T(8,128)S(1)}, f32[1,32,1024]{2,1,0:T(8,128)}, u32[]{:S(2)}) copy-start(f32[1,32,1024]{2,1,0:T(8,128)} %param.7) | copy-start | bytes 393220
  24.8 37.7 %collective-permute-start.9 = (f32[8,16,1024]{2,1,0:T(8,128)}, f32[8,16,1024]{2,1,0:T(8,128)S(1)}, u32[]{:S(2)}, u32[]{:S(2)}) collective-permute-start(f32[8,16,1024]{2,1,0:T(8,128)} %get-tuple-element.18), channel_id=1, source_target_pairs={{1,0},{2,1},{3,2},{4,3},{5,4},{6,5},{7,6},{0,7},{9,8},{10,9},{11,1... | collective-permute-start | bytes 1572872 | tf_op jit(solution)/shard_map/ppermute | solution.py:251
  35.0 27.5 %collective-permute-start.8 = (f32[8,16,1024]{2,1,0:T(8,128)S(1)}, f32[8,16,1024]{2,1,0:T(8,128)S(1)}, u32[]{:S(2)}, u32[]{:S(2)}) collective-permute-start(f32[8,16,1024]{2,1,0:T(8,128)S(1)} %pad_maximum_fusion), channel_id=1, source_target_pairs={{113,122},{115,124},{117,126},{119,120},{241,250},{243,252},{245,2... | collective-permute-start | bytes 1572872 | tf_op jit(solution)/shard_map/ppermute | solution.py:250
  35.7 12.7 %collective-permute-start.5 = (f32[8,8,1024]{2,1,0:T(8,128)S(1)}, f32[8,8,1024]{2,1,0:T(8,128)S(1)}, u32[]{:S(2)}, u32[]{:S(2)}) collective-permute-start(f32[8,8,1024]{2,1,0:T(8,128)S(1)} %get-tuple-element.16), channel_id=1, source_target_pairs={{0,8},{8,16},{16,24},{24,32},{32,40},{40,48},{48,56},{56,64},{64,7... | collective-permute-start | bytes 786440 | tf_op jit(solution)/shard_map/ppermute | solution.py:253
  35.8 26.7 %collective-permute-start.4 = (f32[8,8,1024]{2,1,0:T(8,128)S(1)}, f32[8,8,1024]{2,1,0:T(8,128)S(1)}, u32[]{:S(2)}, u32[]{:S(2)}) collective-permute-start(f32[8,8,1024]{2,1,0:T(8,128)S(1)} %get-tuple-element.15), channel_id=1, source_target_pairs={{0,8},{8,16},{16,24},{24,32},{32,40},{40,48},{48,56},{56,64},{64,7... | collective-permute-start | bytes 786440 | tf_op jit(solution)/shard_map/ppermute | solution.py:254
  42.8 14.7 %collective-permute-start = (s32[1]{0:T(128)}, s32[1]{0:T(128)}, u32[]{:S(2)}, u32[]{:S(2)}) collective-permute-start(s32[1]{0:T(128)} %param.9), channel_id=1, source_target_pairs={{0,8},{8,16},{16,24},{24,32},{32,40},{40,48},{48,56},{56,64},{64,7... | collective-permute-start | bytes 20 | tf_op jit(solution)/shard_map/ppermute | solution.py:242
  48.4 23.9 %collective-permute-start.7 = (f32[8,8,1024]{2,1,0:T(8,128)S(1)}, f32[8,8,1024]{2,1,0:T(8,128)S(1)}, u32[]{:S(2)}, u32[]{:S(2)}) collective-permute-start(f32[8,8,1024]{2,1,0:T(8,128)S(1)} %collective-permute-done.5.hi_ref), channel_id=1, source_target_pairs={{0,1},{1,2},{2,3},{3,4},{4,5},{5,6},{6,7},{7,0},{8,9},{9,10},{10,1... | collective-permute-start | bytes 786440 | tf_op jit(solution)/shard_map/ppermute | solution.py:257
  57.5 14.8 %collective-permute-start.6 = (f32[8,8,1024]{2,1,0:T(8,128)S(1)}, f32[8,8,1024]{2,1,0:T(8,128)S(1)}, u32[]{:S(2)}, u32[]{:S(2)}) collective-permute-start(f32[8,8,1024]{2,1,0:T(8,128)S(1)} %slice.8), channel_id=1, source_target_pairs={{0,1},{1,2},{2,3},{3,4},{4,5},{5,6},{6,7},{7,0},{8,9},{9,10},{10,1... | collective-permute-start | bytes 786440 | tf_op jit(solution)/shard_map/ppermute | solution.py:256
  65.2 20.0 %all-to-all-start = ((f32[256,1,64]{2,1,0:T(1,128)}), f32[256,1,64]{2,1,0:T(1,128)S(1)}, u32[]{:S(2)}, u32[]{:S(2)}) async-start(f32[256,1,64]{2,1,0:T(1,128)} %bitcast.4), calls=%async_computation | async-start | bytes 262144 | tf_op jit(solution)/shard_map/all_to_all | solution.py:265

commit v7 on v6

--- a/solution.py
+++ b/solution.py
@@ -53,10 +53,8 @@
         pltpu.make_async_copy(ax_any, a_ref.at[0], sems.at[0]),
         pltpu.make_async_copy(ay_any, a_ref.at[1], sems.at[1]),
     ] + [pltpu.make_async_copy(k_any.at[group], k_ref.at[group], sems.at[2 + i]) for i, group in enumerate(groups)]
-    beyond = pltpu.make_async_copy(k_any.at[:, pl.ds(0, DRIFT)], beyond_any, out_sems.at[2])
     for copy in copies:
         copy.start()
-    beyond.start()
     for i in range(2):
         copies[i].wait()
         head_ref[vectors + i] = a_ref[i, :STEPS]
@@ -80,11 +78,13 @@
             pltpu.make_async_copy(q_ref.at[group, pl.ds(TILE, rows - 2 * TILE)], mid_any.at[group], out_sems.at[i])
         )
         outs[i].start()
-    for copy in outs + [beyond]:
+    outs.append(pltpu.make_async_copy(k_ref.at[:, pl.ds(0, DRIFT)], beyond_any, out_sems.at[2]))
+    outs[-1].start()
+    for copy in outs:
         copy.wait()
 
 
-def outer_kernel(count_ref, k_ref, ax_ref, ay_ref, left_ref, right_ref, lo_ref, hi_ref, table_ref, q_ref, w_ref):
+def outer_kernel(count_ref, k_ref, ax_ref, ay_ref, left_ref, right_ref, edge_ref, table_ref, q_ref, w_ref):
     vectors, rows, _ = k_ref.shape
 
     def around(strip, at):
@@ -102,8 +102,8 @@
         for b in range(vectors):
             q_ref[b] = step(q_ref[b], w_ref[0], w_ref[1], w_ref[2], w_ref[3])
 
-    hi_ref[...] = q_ref[:, TILE : 2 * TILE]
-    lo_ref[...] = q_ref[:, 3 * TILE : 4 * TILE]
+    edge_ref[:, :TILE] = q_ref[:, TILE : 2 * TILE]
+    edge_ref[:, TILE:] = q_ref[:, 3 * TILE : 4 * TILE]
     tile = functools.partial(tile_of, k_ref)
     table_ref[...] = pair_sums(tile, tile, rows // TILE, vectors, k_ref.shape[2])
 
@@ -130,7 +130,7 @@
 
 
 def gram_kernel(
-    drift_ref, k_ref, beyond_ref, lo_ref, mid_ref, hi_ref, upper_ref, own_ref, gram_ref, shifted_ref, before_ref
+    drift_ref, k_ref, beyond_ref, mid_ref, edge_ref, upper_ref, own_ref, gram_ref, shifted_ref, before_ref
 ):
     vectors, rows, cols = k_ref.shape
     drift = drift_ref[0]
@@ -150,11 +150,11 @@
 
     def right(c, block, lane):
         if block == 0:
-            return tile_of(lo_ref, c, 0, lane)
+            return tile_of(edge_ref, c, 1, lane)
         if block < blocks - 1:
             return tile_of(mid_ref, c, block - 1, lane)
         if block == blocks - 1:
-            return tile_of(hi_ref, c, 0, lane)
+            return tile_of(edge_ref, c, 0, lane)
         return tile_of(before_ref, c, block - blocks, lane)
 
     table = own_ref[...] - pair_sums(left, right, blocks + DRIFT // TILE, vectors, cols)
@@ -165,20 +165,13 @@
     )
 
 
-def last_kernel(drift_ref, k_ref, mid_ref, lo_ref, hi_ref, rim_mid_ref, rim_hi_ref, upper_ref, product_ref):
+def last_kernel(drift_ref, k_ref, mid_ref, edge_ref, rim_ref, upper_ref, product_ref):
     vectors, rows, _ = k_ref.shape
     total = DRIFT + rows
     by = lax.rem(drift_ref[0] + (total - DRIFT), total)
     for b in range(vectors):
         joined = jnp.concatenate(
-            [
-                rim_mid_ref[b] + upper_ref[b, :TILE],
-                rim_hi_ref[b] + upper_ref[b, TILE:],
-                lo_ref[b],
-                mid_ref[b],
-                hi_ref[b],
-            ],
-            axis=0,
+            [rim_ref[b] + upper_ref[b], edge_ref[b, TILE:], mid_ref[b], edge_ref[b, :TILE]], axis=0
         )
         product_ref[b] = k_ref[b] - pltpu.roll(joined, by, 0)[:rows]
 
@@ -240,31 +233,29 @@
     right = lax.ppermute(head, "gx", shift_pairs(strips, -1))
     left = lax.ppermute(tail, "gx", shift_pairs(strips, 1))
     drift = onward(drifts)
-    lo, hi, own = call(
+    edge, own = call(
         outer_kernel,
-        [(vectors, TILE, cols), (vectors, TILE, cols), (pairs, 128)],
+        [(vectors, 2 * TILE, cols), (pairs, 128)],
         [SMEM] + [VMEM] * 5,
         [buffer(vectors, 5 * TILE, cols), buffer(4, 5 * TILE, cols)],
         0,
     )(step_counts, k, ax, ay, left, right)
-    upper = ahead(jnp.concatenate([mid[:, -(DRIFT - TILE) :], hi], axis=1))
+    upper = ahead(jnp.concatenate([mid[:, -(DRIFT - TILE) :], edge[:, :TILE]], axis=1))
     beyond = backward(beyond)
     mid = onward(mid)
-    hi = onward(hi)
-    lo = onward(lo)
-    near = mid[:, -(DRIFT - TILE) :]
-    rim_mid = sideways(near)
-    rim_hi = sideways(lax.optimization_barrier((hi, near))[0])
+    edge = onward(edge)
     (gram,) = call(
         gram_kernel,
         [(world, pairs)],
-        [SMEM] + [VMEM] * 7,
+        [SMEM] + [VMEM] * 6,
         [buffer(*k.shape), buffer(vectors, DRIFT, cols)],
         1,
-    )(drift, k, beyond, lo, mid, hi, upper, own)
+    )(drift, k, beyond, mid, edge, upper, own)
+    near, gram = lax.optimization_barrier((jnp.concatenate([mid[:, -(DRIFT - TILE) :], edge[:, :TILE]], axis=1), gram))
+    rim = sideways(near)
     gram = lax.all_to_all(gram, ("seg", "gx"), 0, 0)
-    (product,) = call(last_kernel, [k.shape], [SMEM] + [VMEM] * 7, [], 1)(
-        drift, k, mid, lo, hi, rim_mid, rim_hi, upper
+    (product,) = call(last_kernel, [k.shape], [SMEM] + [VMEM] * 5, [], 1)(
+        drift, k, mid, edge, rim, upper
     )
     product, gram = lax.optimization_barrier((product, gram))
     cells = world * rows * cols

time: 86.2 us -> 74.7 us (0.87)
  Pallas kernels: 26 us -> 9.75 us
  starting transfers between devices: 33.1 us -> 34.7 us
  waiting for transfers between devices: 23.6 us -> 24.9 us
    pallas_call x1, Pallas kernels: 17.8 us -> 3.74 us  [body(): call(inner_kernel, [(vectors, rows - 2 * TILE, cols), (vectors, DRIFT, co...]
    ppermute x5 -> x3, waiting for transfers between devices: 5.6 us -> 15.7 us  [the longest x1 10.4 us: body(): edge = onward(edge)]
    ppermute x1, waiting for transfers between devices: 6.83 us -> 0.41 us  [body(): mid = onward(mid)]
    all_to_all x1, waiting for transfers between devices: 11 us -> 5.79 us  [body(): gram = lax.all_to_all(gram, ('seg', 'gx'), 0, 0)]
    ppermute x1, starting transfers between devices: 5.26 us -> 2.41 us  [body(): beyond = backward(beyond)]
    ppermute x1, waiting for transfers between devices: 0.1 us -> 2.47 us  [body(): right = lax.ppermute(head, 'gx', shift_pairs(strips, -1))]
    pallas_call x3, Pallas kernels: 8.26 us -> 6.02 us  [the longest x1 2.74 us: body(): call(gram_kernel, [(world, pairs)], [SMEM] + [VMEM] * 6, [buffer(*k.shape...]
    ppermute x5 -> x3, starting transfers between devices: 15 us -> 17.1 us  [the longest x1 8.76 us: body(): rim = sideways(near)]
  transfers between devices with their start and end apart: 11 -> 9, of which waited for: 4 -> 6; matrix products, arithmetic and copies ran while one was open for 1% -> 1% of each run, Pallas kernels for 10% -> 4%
where the time goes in v7:
time: 74.7 us; the launch traced here: 74.2 us
  starting transfers between devices  34.7 us (46%)
  waiting for transfers between devices  24.9 us (33%)
  Pallas kernels  9.75 us (13%)
  local copies, waits for them, and re-layouts  2.48 us (3%)
  between operations  1.4 us (2%)
  other arithmetic  0.96 us (1%)
    ppermute x1, waiting for transfers between devices, body(): edge = onward(edge)  10.4 us
    ppermute x1, starting transfers between devices, body(): rim = sideways(near)  8.76 us
    ppermute x1, starting transfers between devices, body(): edge = onward(edge)  7.67 us
    all_to_all x1, starting transfers between devices, body(): gram = lax.all_to_all(gram, ('seg', 'gx'), 0, 0)  7.23 us
    all_to_all x1, waiting for transfers between devices, body(): gram = lax.all_to_all(gram, ('seg', 'gx'), 0, 0)  5.79 us
    ppermute x1, waiting for transfers between devices, body(): rim = sideways(near)  5.21 us
    ppermute x1, starting transfers between devices, body(): left = lax.ppermute(tail, 'gx', shift_pairs(strips, 1))  4.46 us
    pallas_call x1, Pallas kernels, body(): call(inner_kernel, [(vectors, rows - 2 * TILE, cols), (vectors, DRIFT, co...  3.74 us
  transfers between devices with their start and end apart: 9, of which 6 were waited for; matrix products, arithmetic and copies ran while one was open for 1% of the time, Pallas kernels for 4%

profile of v7, /device:TPU:1, one launch (start us, length us, event | category | flops | bytes accessed | tf_op | source)
XLA Modules:
  0.0 74.2 jit_solution(7017411385934824811)
XLA Ops:
  1.3 3.7 %shard_map.68 = (f32[8,16,1024]{2,1,0:T(8,128)}, f32[8,16,1024]{2,1,0:T(8,128)}, f32[10,4,1024]{2,1,0:T(4,128)}, f32[10,4,1024]{2,1,0:T(4,128)}) custom-call(s32[1]{0:T(128)S(6)} %copy.8.count_ref, f32[8,32,1024]{2,1,0:T(8,128)} %bitcast.8, f32[32,1024]{1,0:T(8,128)} %bitcast.12, f32[32,1024]{1,0:T(8,128)} %bitcast.14), custom_call_target="tpu_custom_call" | custom-call | flops 68719476736 | bytes 67108864 | tf_op jit(solution)/shard_map/pallas_call | solution.py:217
  5.1 4.5 %collective-permute-start.2 = (f32[10,4,1024]{2,1,0:T(4,128)}, f32[10,4,1024]{2,1,0:T(4,128)S(1)}, u32[]{:S(2)}, u32[]{:S(2)}) collective-permute-start(f32[10,4,1024]{2,1,0:T(4,128)} %get-tuple-element.13), channel_id=1, source_target_pairs={{0,1},{1,2},{2,3},{3,4},{4,5},{5,6},{6,7},{7,0},{8,9},{9,10},{10,1... | collective-permute-start | bytes 491528 | tf_op jit(solution)/shard_map/ppermute | solution.py:234
  9.5 3.4 %collective-permute-start.1 = (f32[8,16,1024]{2,1,0:T(8,128)}, f32[8,16,1024]{2,1,0:T(8,128)S(1)}, u32[]{:S(2)}, u32[]{:S(2)}) collective-permute-start(f32[8,16,1024]{2,1,0:T(8,128)} %get-tuple-element.12), channel_id=1, source_target_pairs={{0,8},{8,16},{16,24},{24,32},{32,40},{40,48},{48,56},{56,64},{64,7... | collective-permute-start | bytes 1572872 | tf_op jit(solution)/shard_map/ppermute | solution.py:245
  12.9 2.5 %collective-permute-done.3.right_ref = f32[10,4,1024]{2,1,0:T(4,128)S(1)} collective-permute-done((f32[10,4,1024]{2,1,0:T(4,128)}, f32[10,4,1024]{2,1,0:T(4,128)S(1)}, u32[]{:S(2)}, u32[]{:S(2)}) %collective-permute-start.3) | collective-permute-done | bytes 163872 | tf_op jit(solution)/shard_map/ppermute | solution.py:233
  15.4 1.4 %shard_map.69 = (f32[8,16,1024]{2,1,0:T(8,128)S(1)}, f32[64,128]{1,0:T(8,128)S(1)}) custom-call(s32[1]{0:T(128)S(6)} %copy.8.count_ref, f32[8,32,1024]{2,1,0:T(8,128)S(1)} %bitcast.9, f32[32,1024]{1,0:T(8,128)S(1)} %bitcast.13, f32[32,1024]{1,0:T(8,128)S(1)} %bitcast.15, f32[10,4,1024]{2,1,0:T(4,128)S(1)} %collective-permute-done.2.left_ref, ...), custom_call_target="tpu_custom_call" | custom-call | tf_op jit(solution)/shard_map/pallas_call | solution.py:236
  16.7 7.7 %collective-permute-start.4 = (f32[8,16,1024]{2,1,0:T(8,128)S(1)}, f32[8,16,1024]{2,1,0:T(8,128)S(1)}, u32[]{:S(2)}, u32[]{:S(2)}) collective-permute-start(f32[8,16,1024]{2,1,0:T(8,128)S(1)} %get-tuple-element.15), channel_id=1, source_target_pairs={{0,8},{8,16},{16,24},{24,32},{32,40},{40,48},{48,56},{56,64},{64,7... | collective-permute-start | bytes 1572872 | tf_op jit(solution)/shard_map/ppermute | solution.py:246
  24.4 2.4 %collective-permute-start.5 = (f32[8,16,1024]{2,1,0:T(8,128)S(1)}, f32[8,16,1024]{2,1,0:T(8,128)S(1)}, u32[]{:S(2)}, u32[]{:S(2)}) collective-permute-start(f32[8,16,1024]{2,1,0:T(8,128)S(1)} %copy-done.6), channel_id=1, source_target_pairs={{1,0},{2,1},{3,2},{4,3},{5,4},{6,5},{7,6},{0,7},{9,8},{10,9},{11,1... | collective-permute-start | bytes 1572872 | tf_op jit(solution)/shard_map/ppermute | solution.py:244
  26.9 0.1 pad_maximum_fusion.1
  27.0 0.7 collective-permute-start.6
  27.7 0.1 collective-permute-start
  27.7 0.4 collective-permute-done.1.mid_ref
  28.2 0.8 %copy-done.1 = f32[8,16,1024]{2,1,0:T(8,128)} copy-done((f32[8,16,1024]{2,1,0:T(8,128)}, f32[8,16,1024]{2,1,0:T(8,128)S(1)}, u32[]{:S(2)}) %copy-start.1) | copy-done | bytes 524312
  29.0 10.4 %collective-permute-done.4.edge_ref = f32[8,16,1024]{2,1,0:T(8,128)S(1)} collective-permute-done((f32[8,16,1024]{2,1,0:T(8,128)S(1)}, f32[8,16,1024]{2,1,0:T(8,128)S(1)}, u32[]{:S(2)}, u32[]{:S(2)}) %collective-permute-start.4) | collective-permute-done | bytes 524320 | tf_op jit(solution)/shard_map/ppermute | solution.py:246
  39.4 0.9 %slice-done = f32[8,8,1024]{2,1,0:T(8,128)S(1)} async-done(((f32[8,16,1024]{2,1,0:T(8,128)}), f32[8,8,1024]{2,1,0:T(8,128)S(1)}, s32[]{:S(2)}) %slice-start) | async-done | bytes 262168 | tf_op jit(solution)/shard_map/slice | solution.py:254
  40.3 0.9 %pad_maximum_fusion = f32[8,16,1024]{2,1,0:T(8,128)} fusion(f32[8,8,1024]{2,1,0:T(8,128)S(1)} %slice.17, f32[8,8,1024]{2,1,0:T(8,128)S(1)} %slice-done), kind=kLoop, calls=%fused_computation | loop fusion | flops 131072 | bytes 1048576 | tf_op jit(solution)/shard_map/concatenate | solution.py:254
  41.2 0.6 collective-permute-done.5.beyond_ref
  41.8 2.7 %shard_map.70 = f32[256,64]{1,0:T(8,128)} custom-call(s32[1]{0:T(128)} %collective-permute-done.drift_ref, f32[8,32,1024]{2,1,0:T(8,128)S(1)} %bitcast.10, f32[8,16,1024]{2,1,0:T(8,128)S(1)} %collective-permute-done.5.beyond_ref, f32[8,16,1024]{2,1,0:T(8,128)S(1)} %copy-done.2, f32[8,16,1024]{2,1,0:T(8,128)S(1)} %collective-permute-done.4.edge_ref, ...), custom_call_target="tpu_custom_call" | custom-call | flops 1073741824 | bytes 1048576 | tf_op jit(solution)/shard_map/pallas_call | solution.py:247
  44.5 8.8 %collective-permute-start.7 = (f32[8,16,1024]{2,1,0:T(8,128)}, f32[8,16,1024]{2,1,0:T(8,128)S(1)}, u32[]{:S(2)}, u32[]{:S(2)}) collective-permute-start(f32[8,16,1024]{2,1,0:T(8,128)} %pad_maximum_fusion), channel_id=1, source_target_pairs={{0,1},{1,2},{2,3},{3,4},{4,5},{5,6},{6,7},{7,0},{8,9},{9,10},{10,1... | collective-permute-start | bytes 1572872 | tf_op jit(solution)/shard_map/ppermute | solution.py:255
  53.3 7.2 %all-to-all-start = ((f32[256,1,64]{2,1,0:T(1,128)}), f32[256,1,64]{2,1,0:T(1,128)S(1)}, u32[]{:S(2)}, u32[]{:S(2)}) async-start(f32[256,1,64]{2,1,0:T(1,128)} %bitcast.4), calls=%async_computation | async-start | bytes 262144 | tf_op jit(solution)/shard_map/all_to_all | solution.py:256
  60.5 5.2 %collective-permute-done.7.rim_ref = f32[8,16,1024]{2,1,0:T(8,128)S(1)} collective-permute-done((f32[8,16,1024]{2,1,0:T(8,128)}, f32[8,16,1024]{2,1,0:T(8,128)S(1)}, u32[]{:S(2)}, u32[]{:S(2)}) %collective-permute-start.7) | collective-permute-done | bytes 524320 | tf_op jit(solution)/shard_map/ppermute | solution.py:255
  65.7 1.9 %shard_map.71 = f32[8,32,1024]{2,1,0:T(8,128)} custom-call(s32[1]{0:T(128)} %collective-permute-done.drift_ref, f32[8,32,1024]{2,1,0:T(8,128)S(1)} %bitcast.11, f32[8,16,1024]{2,1,0:T(8,128)S(1)} %copy-done.2, f32[8,16,1024]{2,1,0:T(8,128)S(1)} %collective-permute-done.4.edge_ref, f32[8,16,1024]{2,1,0:T(8,128)S(1)} %collective-permute-done.7.rim_ref, ...), custom_call_target="tpu_custom_call" | custom-call | flops 1073741824 | bytes 1048576 | tf_op jit(solution)/shard_map/pallas_call | solution.py:257
  67.7 5.8 %all-to-all-done = f32[256,1,64]{2,1,0:T(1,128)S(1)} async-done(((f32[256,1,64]{2,1,0:T(1,128)}), f32[256,1,64]{2,1,0:T(1,128)S(1)}, u32[]{:S(2)}, u32[]{:S(2)}) %all-to-all-start) | async-done | bytes 65568 | tf_op jit(solution)/shard_map/all_to_all | solution.py:256
  73.4 0.1 reduce_sum.9
  73.5 0.7 div.10
  (22 shorter events, 0.1 us)
Async XLA Ops:
  1.3 14.1 %copy-start = (f32[1,8,32,1024]{3,2,1,0:T(8,128)S(1)}, f32[1,8,32,1024]{3,2,1,0:T(8,128)}, u32[]{:S(2)}) copy-start(f32[1,8,32,1024]{3,2,1,0:T(8,128)} %param.5) | copy-start | bytes 3145732
  1.3 14.1 %copy-start.3 = (f32[1,32,1024]{2,1,0:T(8,128)S(1)}, f32[1,32,1024]{2,1,0:T(8,128)}, u32[]{:S(2)}) copy-start(f32[1,32,1024]{2,1,0:T(8,128)} %param.6) | copy-start | bytes 393220
  1.3 14.1 %copy-start.4 = (f32[1,32,1024]{2,1,0:T(8,128)S(1)}, f32[1,32,1024]{2,1,0:T(8,128)}, u32[]{:S(2)}) copy-start(f32[1,32,1024]{2,1,0:T(8,128)} %param.7) | copy-start | bytes 393220
  5.1 7.9 %collective-permute-start.2 = (f32[10,4,1024]{2,1,0:T(4,128)}, f32[10,4,1024]{2,1,0:T(4,128)S(1)}, u32[]{:S(2)}, u32[]{:S(2)}) collective-permute-start(f32[10,4,1024]{2,1,0:T(4,128)} %get-tuple-element.13), channel_id=1, source_target_pairs={{0,1},{1,2},{2,3},{3,4},{4,5},{5,6},{6,7},{7,0},{8,9},{9,10},{10,1... | collective-permute-start | bytes 491528 | tf_op jit(solution)/shard_map/ppermute | solution.py:234
  9.5 5.9 %collective-permute-start.3 = (f32[10,4,1024]{2,1,0:T(4,128)}, f32[10,4,1024]{2,1,0:T(4,128)S(1)}, u32[]{:S(2)}, u32[]{:S(2)}) collective-permute-start(f32[10,4,1024]{2,1,0:T(4,128)} %get-tuple-element.14), channel_id=1, source_target_pairs={{0,7},{1,0},{2,1},{3,2},{4,3},{5,4},{6,5},{7,6},{8,15},{9,8},{10,9... | collective-permute-start | bytes 491528 | tf_op jit(solution)/shard_map/ppermute | solution.py:233
  9.5 14.9 %copy-start.6 = (f32[8,16,1024]{2,1,0:T(8,128)S(1)}, f32[8,16,1024]{2,1,0:T(8,128)}, u32[]{:S(2)}) copy-start(f32[8,16,1024]{2,1,0:T(8,128)} %get-tuple-element.16) | copy-start | bytes 1572868
  9.5 17.3 %copy-start.5 = (f32[8,16,1024]{2,1,0:T(8,128)S(1)}, f32[8,16,1024]{2,1,0:T(8,128)}, u32[]{:S(2)}) copy-start(f32[8,16,1024]{2,1,0:T(8,128)} %get-tuple-element.12) | copy-start | bytes 1572868
  9.5 18.6 %collective-permute-start.1 = (f32[8,16,1024]{2,1,0:T(8,128)}, f32[8,16,1024]{2,1,0:T(8,128)S(1)}, u32[]{:S(2)}, u32[]{:S(2)}) collective-permute-start(f32[8,16,1024]{2,1,0:T(8,128)} %get-tuple-element.12), channel_id=1, source_target_pairs={{0,8},{8,16},{16,24},{24,32},{32,40},{40,48},{48,56},{56,64},{64,7... | collective-permute-start | bytes 1572872 | tf_op jit(solution)/shard_map/ppermute | solution.py:245
  16.7 22.7 %collective-permute-start.4 = (f32[8,16,1024]{2,1,0:T(8,128)S(1)}, f32[8,16,1024]{2,1,0:T(8,128)S(1)}, u32[]{:S(2)}, u32[]{:S(2)}) collective-permute-start(f32[8,16,1024]{2,1,0:T(8,128)S(1)} %get-tuple-element.15), channel_id=1, source_target_pairs={{0,8},{8,16},{16,24},{24,32},{32,40},{40,48},{48,56},{56,64},{64,7... | collective-permute-start | bytes 1572872 | tf_op jit(solution)/shard_map/ppermute | solution.py:246
  24.4 17.3 %collective-permute-start.5 = (f32[8,16,1024]{2,1,0:T(8,128)S(1)}, f32[8,16,1024]{2,1,0:T(8,128)S(1)}, u32[]{:S(2)}, u32[]{:S(2)}) collective-permute-start(f32[8,16,1024]{2,1,0:T(8,128)S(1)} %copy-done.6), channel_id=1, source_target_pairs={{1,0},{2,1},{3,2},{4,3},{5,4},{6,5},{7,6},{0,7},{9,8},{10,9},{11,1... | collective-permute-start | bytes 1572872 | tf_op jit(solution)/shard_map/ppermute | solution.py:244
  27.0 14.8 %collective-permute-start.6 = (f32[8,16,1024]{2,1,0:T(8,128)S(1)}, f32[8,16,1024]{2,1,0:T(8,128)S(1)}, u32[]{:S(2)}, u32[]{:S(2)}) collective-permute-start(f32[8,16,1024]{2,1,0:T(8,128)S(1)} %pad_maximum_fusion.1), channel_id=1, source_target_pairs={{113,122},{115,124},{117,126},{119,120},{241,250},{243,252},{245,2... | collective-permute-start | bytes 1572872 | tf_op jit(solution)/shard_map/ppermute | solution.py:243
  27.7 13.6 %collective-permute-start = (s32[1]{0:T(128)}, s32[1]{0:T(128)}, u32[]{:S(2)}, u32[]{:S(2)}) collective-permute-start(s32[1]{0:T(128)} %param.9), channel_id=1, source_target_pairs={{0,8},{8,16},{16,24},{24,32},{32,40},{40,48},{48,56},{56,64},{64,7... | collective-permute-start | bytes 20 | tf_op jit(solution)/shard_map/ppermute | solution.py:235
  28.2 0.8 %copy-start.1 = (f32[8,16,1024]{2,1,0:T(8,128)}, f32[8,16,1024]{2,1,0:T(8,128)S(1)}, u32[]{:S(2)}) copy-start(f32[8,16,1024]{2,1,0:T(8,128)S(1)} %collective-permute-done.1.mid_ref) | copy-start | bytes 1572868
  39.4 1.0 %slice-start = ((f32[8,16,1024]{2,1,0:T(8,128)}), f32[8,8,1024]{2,1,0:T(8,128)S(1)}, s32[]{:S(2)}) async-start(f32[8,16,1024]{2,1,0:T(8,128)} %copy-done.1), calls=%async_computation.1 | async-start | bytes 524288 | tf_op jit(solution)/shard_map/slice | solution.py:254
  40.3 1.4 %copy-start.2 = (f32[8,16,1024]{2,1,0:T(8,128)S(1)}, f32[8,16,1024]{2,1,0:T(8,128)}, u32[]{:S(2)}) copy-start(f32[8,16,1024]{2,1,0:T(8,128)} %copy-done.1) | copy-start | bytes 1572868
  44.5 21.2 %collective-permute-start.7 = (f32[8,16,1024]{2,1,0:T(8,128)}, f32[8,16,1024]{2,1,0:T(8,128)S(1)}, u32[]{:S(2)}, u32[]{:S(2)}) collective-permute-start(f32[8,16,1024]{2,1,0:T(8,128)} %pad_maximum_fusion), channel_id=1, source_target_pairs={{0,1},{1,2},{2,3},{3,4},{4,5},{5,6},{6,7},{7,0},{8,9},{9,10},{10,1... | collective-permute-start | bytes 1572872 | tf_op jit(solution)/shard_map/ppermute | solution.py:255
  53.3 20.2 %all-to-all-start = ((f32[256,1,64]{2,1,0:T(1,128)}), f32[256,1,64]{2,1,0:T(1,128)S(1)}, u32[]{:S(2)}, u32[]{:S(2)}) async-start(f32[256,1,64]{2,1,0:T(1,128)} %bitcast.4), calls=%async_computation | async-start | bytes 262144 | tf_op jit(solution)/shard_map/all_to_all | solution.py:256

commit v8 on v7

--- a/solution.py
+++ b/solution.py
@@ -130,11 +130,13 @@
 
 
 def gram_kernel(
-    drift_ref, k_ref, beyond_ref, mid_ref, edge_ref, upper_ref, own_ref, gram_ref, shifted_ref, before_ref
+    drift_ref, k_ref, beyond_ref, mid_ref, edge_ref, upper_ref, own_ref, gram_ref, near_ref, shifted_ref, before_ref
 ):
     vectors, rows, cols = k_ref.shape
     drift = drift_ref[0]
     blocks = rows // TILE
+    near_ref[:, : DRIFT - TILE] = mid_ref[:, -(DRIFT - TILE) :]
+    near_ref[:, DRIFT - TILE :] = edge_ref[:, :TILE]
     total = rows + DRIFT
     back = lax.rem(total - drift, total)
     row = lax.broadcasted_iota(jnp.int32, (DRIFT, cols), 0)
@@ -196,9 +198,9 @@
     pairs = []
     for s in range(segs):
         for g in range(strips):
-            busy = (s + 1) % (segs // 2) == 0 and g % 2 == 1
-            if busy == direct:
-                pairs.append(((s - direct) * strips + g, s * strips + (g + 1) % strips))
+            crosses = g % 2 == 1 and s != segs // 2
+            if crosses == direct:
+                pairs.append((((s - direct) % segs) * strips + g, s * strips + (g + 1) % strips))
     return pairs
 
 
@@ -244,14 +246,13 @@
     beyond = backward(beyond)
     mid = onward(mid)
     edge = onward(edge)
-    (gram,) = call(
+    gram, near = call(
         gram_kernel,
-        [(world, pairs)],
+        [(world, pairs), (vectors, DRIFT, cols)],
         [SMEM] + [VMEM] * 6,
         [buffer(*k.shape), buffer(vectors, DRIFT, cols)],
         1,
     )(drift, k, beyond, mid, edge, upper, own)
-    near, gram = lax.optimization_barrier((jnp.concatenate([mid[:, -(DRIFT - TILE) :], edge[:, :TILE]], axis=1), gram))
     rim = sideways(near)
     gram = lax.all_to_all(gram, ("seg", "gx"), 0, 0)
     (product,) = call(last_kernel, [k.shape], [SMEM] + [VMEM] * 5, [], 1)(

time: 74.7 us -> 78.3 us (1.048)
  waiting for transfers between devices: 24.9 us -> 36 us
  starting transfers between devices: 34.7 us -> 24.3 us
  Pallas kernels: 9.75 us -> 14.4 us
  other arithmetic: 0.96 us -> 0.11 us
    ppermute x1, waiting for transfers between devices: 0.01 us -> 22.8 us  [body(): drift = onward(drifts)]
    ppermute x1, waiting for transfers between devices: 10.4 us -> 0.01 us  [body(): edge = onward(edge)]
    ppermute x1, starting transfers between devices: 7.67 us -> 0.08 us  [body(): edge = onward(edge)]
    ppermute x1, starting transfers between devices: 8.76 us -> 1.28 us  [body(): rim = sideways(near)]
    ppermute x1, waiting for transfers between devices: 5.21 us -> 0.01 us  [body(): rim = sideways(near)]
    all_to_all x1, waiting for transfers between devices: 5.79 us -> 10.9 us  [body(): gram = lax.all_to_all(gram, ('seg', 'gx'), 0, 0)]
    all_to_all x1, starting transfers between devices: 7.23 us -> 10.5 us  [body(): gram = lax.all_to_all(gram, ('seg', 'gx'), 0, 0)]
    ppermute x1, starting transfers between devices: 2.41 us -> 4.88 us  [body(): beyond = backward(beyond)]
  transfers between devices with their start and end apart: 9 -> 9, of which waited for: 6 -> 3; matrix products, arithmetic and copies ran while one was open for 1% -> 1% of each run, Pallas kernels for 4% -> 7%
where the time goes in v8:
time: 78.3 us; the launch traced here: 77.9 us
  waiting for transfers between devices  36 us (46%)
  starting transfers between devices  24.3 us (31%)
  Pallas kernels  14.4 us (18%)
  local copies, waits for them, and re-layouts  1.71 us (2%)
  between operations  1.4 us (2%)
    ppermute x1, waiting for transfers between devices, body(): drift = onward(drifts)  22.8 us
    all_to_all x1, waiting for transfers between devices, body(): gram = lax.all_to_all(gram, ('seg', 'gx'), 0, 0)  10.9 us
    all_to_all x1, starting transfers between devices, body(): gram = lax.all_to_all(gram, ('seg', 'gx'), 0, 0)  10.5 us
    pallas_call x1, Pallas kernels, body(): call(inner_kernel, [(vectors, rows - 2 * TILE, cols), (vectors, DRIFT, co...  5.79 us
    ppermute x1, starting transfers between devices, body(): beyond = backward(beyond)  4.88 us
    ppermute x1, starting transfers between devices, body(): left = lax.ppermute(tail, 'gx', shift_pairs(strips, 1))  4.46 us
    pallas_call x1, Pallas kernels, body(): call(outer_kernel, [(vectors, 2 * TILE, cols), (pairs, 128)], [SMEM] + [V...  3.78 us
    pallas_call x1, Pallas kernels, body(): call(gram_kernel, [(world, pairs), (vectors, DRIFT, cols)], [SMEM] + [VME...  2.85 us
  transfers between devices with their start and end apart: 9, of which 3 were waited for; matrix products, arithmetic and copies ran while one was open for 1% of the time, Pallas kernels for 7%

profile of v8, /device:TPU:1, one launch (start us, length us, event | category | flops | bytes accessed | tf_op | source)
XLA Modules:
  0.0 77.9 jit_solution(5362412275300073328)
XLA Ops:
  1.3 5.8 %shard_map.68 = (f32[8,16,1024]{2,1,0:T(8,128)}, f32[8,16,1024]{2,1,0:T(8,128)}, f32[10,4,1024]{2,1,0:T(4,128)}, f32[10,4,1024]{2,1,0:T(4,128)}) custom-call(s32[1]{0:T(128)S(6)} %copy.8.count_ref, f32[8,32,1024]{2,1,0:T(8,128)} %bitcast.8, f32[32,1024]{1,0:T(8,128)} %bitcast.12, f32[32,1024]{1,0:T(8,128)} %bitcast.14), custom_call_target="tpu_custom_call" | custom-call | flops 68719476736 | bytes 67108864 | tf_op jit(solution)/shard_map/pallas_call | solution.py:219
  7.1 4.5 %collective-permute-start.2 = (f32[10,4,1024]{2,1,0:T(4,128)}, f32[10,4,1024]{2,1,0:T(4,128)S(1)}, u32[]{:S(2)}, u32[]{:S(2)}) collective-permute-start(f32[10,4,1024]{2,1,0:T(4,128)} %get-tuple-element.13), channel_id=1, source_target_pairs={{0,1},{1,2},{2,3},{3,4},{4,5},{5,6},{6,7},{7,0},{8,9},{9,10},{10,1... | collective-permute-start | bytes 491528 | tf_op jit(solution)/shard_map/ppermute | solution.py:236
  11.5 0.0 collective-permute-start.3
  11.5 4.9 %collective-permute-start.5 = (f32[8,16,1024]{2,1,0:T(8,128)}, f32[8,16,1024]{2,1,0:T(8,128)S(1)}, u32[]{:S(2)}, u32[]{:S(2)}) collective-permute-start(f32[8,16,1024]{2,1,0:T(8,128)} %get-tuple-element.16), channel_id=1, source_target_pairs={{1,0},{3,2},{5,4},{7,6},{9,8},{11,10},{13,12},{15,14},{17,16},{19,... | collective-permute-start | bytes 1572872 | tf_op jit(solution)/shard_map/ppermute | solution.py:246
  16.4 0.0 copy-start.1
  16.4 0.0 copy-start.2
  16.5 1.4 %collective-permute-start.1 = (f32[8,16,1024]{2,1,0:T(8,128)}, f32[8,16,1024]{2,1,0:T(8,128)S(1)}, u32[]{:S(2)}, u32[]{:S(2)}) collective-permute-start(f32[8,16,1024]{2,1,0:T(8,128)} %get-tuple-element.12), channel_id=1, source_target_pairs={{0,8},{8,16},{16,24},{24,32},{32,40},{40,48},{48,56},{56,64},{64,7... | collective-permute-start | bytes 1572872 | tf_op jit(solution)/shard_map/ppermute | solution.py:247
  17.8 1.0 %slice.6 = f32[8,8,1024]{2,1,0:T(8,128)S(1)} slice(f32[8,16,1024]{2,1,0:T(8,128)} %get-tuple-element.12), slice={[0:8], [8:16], [0:1024]} | slice | bytes 524288 | tf_op jit(solution)/shard_map/slice | solution.py:245
  18.8 2.3 %collective-permute-done.3.right_ref = f32[10,4,1024]{2,1,0:T(4,128)S(1)} collective-permute-done((f32[10,4,1024]{2,1,0:T(4,128)}, f32[10,4,1024]{2,1,0:T(4,128)S(1)}, u32[]{:S(2)}, u32[]{:S(2)}) %collective-permute-start.3) | collective-permute-done | bytes 163872 | tf_op jit(solution)/shard_map/ppermute | solution.py:235
  21.2 3.8 %shard_map.69 = (f32[8,16,1024]{2,1,0:T(8,128)S(1)}, f32[64,128]{1,0:T(8,128)S(1)}) custom-call(s32[1]{0:T(128)S(6)} %copy.8.count_ref, f32[8,32,1024]{2,1,0:T(8,128)S(1)} %bitcast.9, f32[32,1024]{1,0:T(8,128)S(1)} %bitcast.13, f32[32,1024]{1,0:T(8,128)S(1)} %bitcast.15, f32[10,4,1024]{2,1,0:T(4,128)S(1)} %collective-permute-done.2.left_ref, ...), custom_call_target="tpu_custom_call" | custom-call | tf_op jit(solution)/shard_map/pallas_call | solution.py:238
  25.0 0.1 pad_maximum_fusion
  25.0 1.3 %collective-permute-start.6 = (f32[8,16,1024]{2,1,0:T(8,128)S(1)}, f32[8,16,1024]{2,1,0:T(8,128)S(1)}, u32[]{:S(2)}, u32[]{:S(2)}) collective-permute-start(f32[8,16,1024]{2,1,0:T(8,128)S(1)} %pad_maximum_fusion), channel_id=1, source_target_pairs={{249,2},{251,4},{253,6},{255,0},{1,10},{3,12},{5,14},{7,8},{9,18},... | collective-permute-start | bytes 1572872 | tf_op jit(solution)/shard_map/ppermute | solution.py:245
  26.3 0.1 collective-permute-start.4
  26.4 0.4 collective-permute-start
  26.9 22.8 %collective-permute-done.drift_ref = s32[1]{0:T(128)} collective-permute-done((s32[1]{0:T(128)}, s32[1]{0:T(128)}, u32[]{:S(2)}, u32[]{:S(2)}) %collective-permute-start) | collective-permute-done | bytes 36 | tf_op jit(solution)/shard_map/ppermute | solution.py:237
  49.6 0.0 collective-permute-done.6.upper_ref
  49.6 0.0 collective-permute-done.4.edge_ref
  49.6 2.8 %shard_map.70 = (f32[256,64]{1,0:T(8,128)}, f32[8,16,1024]{2,1,0:T(8,128)}) custom-call(s32[1]{0:T(128)} %collective-permute-done.drift_ref, f32[8,32,1024]{2,1,0:T(8,128)S(1)} %bitcast.10, f32[8,16,1024]{2,1,0:T(8,128)S(1)} %collective-permute-done.5.beyond_ref, f32[8,16,1024]{2,1,0:T(8,128)S(1)} %collective-permute-done.1.mid_ref, ...), custom_call_target="tpu_custom_call" | custom-call | flops 1073741824 | bytes 1048576 | tf_op jit(solution)/shard_map/pallas_call | solution.py:249
  52.5 1.3 %collective-permute-start.7 = (f32[8,16,1024]{2,1,0:T(8,128)}, f32[8,16,1024]{2,1,0:T(8,128)S(1)}, u32[]{:S(2)}, u32[]{:S(2)}) collective-permute-start(f32[8,16,1024]{2,1,0:T(8,128)} %get-tuple-element.18), channel_id=1, source_target_pairs={{0,1},{2,3},{4,5},{6,7},{8,9},{10,11},{12,13},{14,15},{16,17},{18,... | collective-permute-start | bytes 1572872 | tf_op jit(solution)/shard_map/ppermute | solution.py:256
  53.8 10.5 %all-to-all-start = ((f32[256,1,64]{2,1,0:T(1,128)}), f32[256,1,64]{2,1,0:T(1,128)S(1)}, u32[]{:S(2)}, u32[]{:S(2)}) async-start(f32[256,1,64]{2,1,0:T(1,128)} %bitcast.4), calls=%async_computation | async-start | bytes 262144 | tf_op jit(solution)/shard_map/all_to_all | solution.py:257
  64.3 2.0 %shard_map.71 = f32[8,32,1024]{2,1,0:T(8,128)} custom-call(s32[1]{0:T(128)} %collective-permute-done.drift_ref, f32[8,32,1024]{2,1,0:T(8,128)S(1)} %bitcast.11, f32[8,16,1024]{2,1,0:T(8,128)S(1)} %collective-permute-done.1.mid_ref, f32[8,16,1024]{2,1,0:T(8,128)S(1)} %collective-permute-done.4.edge_ref, f32[8,16,1024]{2,1,0:T(8,128)S(1)} %collective-permute-done.7.rim_ref, ...), custom_call_target="tpu_custom_call" | custom-call | flops 1073741824 | bytes 1048576 | tf_op jit(solution)/shard_map/pallas_call | solution.py:258
  66.3 10.9 %all-to-all-done = f32[256,1,64]{2,1,0:T(1,128)S(1)} async-done(((f32[256,1,64]{2,1,0:T(1,128)}), f32[256,1,64]{2,1,0:T(1,128)S(1)}, u32[]{:S(2)}, u32[]{:S(2)}) %all-to-all-start) | async-done | bytes 65568 | tf_op jit(solution)/shard_map/all_to_all | solution.py:257
  77.2 0.1 reduce_sum.9
  77.3 0.7 div.10
  (10 shorter events, 0.0 us)
Async XLA Ops:
  1.3 19.9 %copy-start = (f32[1,8,32,1024]{3,2,1,0:T(8,128)S(1)}, f32[1,8,32,1024]{3,2,1,0:T(8,128)}, u32[]{:S(2)}) copy-start(f32[1,8,32,1024]{3,2,1,0:T(8,128)} %param.5) | copy-start | bytes 3145732
  7.1 11.8 %collective-permute-start.2 = (f32[10,4,1024]{2,1,0:T(4,128)}, f32[10,4,1024]{2,1,0:T(4,128)S(1)}, u32[]{:S(2)}, u32[]{:S(2)}) collective-permute-start(f32[10,4,1024]{2,1,0:T(4,128)} %get-tuple-element.13), channel_id=1, source_target_pairs={{0,1},{1,2},{2,3},{3,4},{4,5},{5,6},{6,7},{7,0},{8,9},{9,10},{10,1... | collective-permute-start | bytes 491528 | tf_op jit(solution)/shard_map/ppermute | solution.py:236
  11.5 9.6 %collective-permute-start.3 = (f32[10,4,1024]{2,1,0:T(4,128)}, f32[10,4,1024]{2,1,0:T(4,128)S(1)}, u32[]{:S(2)}, u32[]{:S(2)}) collective-permute-start(f32[10,4,1024]{2,1,0:T(4,128)} %get-tuple-element.14), channel_id=1, source_target_pairs={{0,7},{1,0},{2,1},{3,2},{4,3},{5,4},{6,5},{7,6},{8,15},{9,8},{10,9... | collective-permute-start | bytes 491528 | tf_op jit(solution)/shard_map/ppermute | solution.py:235
  11.5 38.1 %collective-permute-start.5 = (f32[8,16,1024]{2,1,0:T(8,128)}, f32[8,16,1024]{2,1,0:T(8,128)S(1)}, u32[]{:S(2)}, u32[]{:S(2)}) collective-permute-start(f32[8,16,1024]{2,1,0:T(8,128)} %get-tuple-element.16), channel_id=1, source_target_pairs={{1,0},{3,2},{5,4},{7,6},{9,8},{11,10},{13,12},{15,14},{17,16},{19,... | collective-permute-start | bytes 1572872 | tf_op jit(solution)/shard_map/ppermute | solution.py:246
  16.4 4.7 %copy-start.1 = (f32[1,32,1024]{2,1,0:T(8,128)S(1)}, f32[1,32,1024]{2,1,0:T(8,128)}, u32[]{:S(2)}) copy-start(f32[1,32,1024]{2,1,0:T(8,128)} %param.6) | copy-start | bytes 393220
  16.4 4.7 %copy-start.2 = (f32[1,32,1024]{2,1,0:T(8,128)S(1)}, f32[1,32,1024]{2,1,0:T(8,128)}, u32[]{:S(2)}) copy-start(f32[1,32,1024]{2,1,0:T(8,128)} %param.7) | copy-start | bytes 393220
  16.5 33.2 %collective-permute-start.1 = (f32[8,16,1024]{2,1,0:T(8,128)}, f32[8,16,1024]{2,1,0:T(8,128)S(1)}, u32[]{:S(2)}, u32[]{:S(2)}) collective-permute-start(f32[8,16,1024]{2,1,0:T(8,128)} %get-tuple-element.12), channel_id=1, source_target_pairs={{0,8},{8,16},{16,24},{24,32},{32,40},{40,48},{48,56},{56,64},{64,7... | collective-permute-start | bytes 1572872 | tf_op jit(solution)/shard_map/ppermute | solution.py:247
  25.0 24.6 %collective-permute-start.6 = (f32[8,16,1024]{2,1,0:T(8,128)S(1)}, f32[8,16,1024]{2,1,0:T(8,128)S(1)}, u32[]{:S(2)}, u32[]{:S(2)}) collective-permute-start(f32[8,16,1024]{2,1,0:T(8,128)S(1)} %pad_maximum_fusion), channel_id=1, source_target_pairs={{249,2},{251,4},{253,6},{255,0},{1,10},{3,12},{5,14},{7,8},{9,18},... | collective-permute-start | bytes 1572872 | tf_op jit(solution)/shard_map/ppermute | solution.py:245
  26.3 23.3 %collective-permute-start.4 = (f32[8,16,1024]{2,1,0:T(8,128)S(1)}, f32[8,16,1024]{2,1,0:T(8,128)S(1)}, u32[]{:S(2)}, u32[]{:S(2)}) collective-permute-start(f32[8,16,1024]{2,1,0:T(8,128)S(1)} %get-tuple-element.15), channel_id=1, source_target_pairs={{0,8},{8,16},{16,24},{24,32},{32,40},{40,48},{48,56},{56,64},{64,7... | collective-permute-start | bytes 1572872 | tf_op jit(solution)/shard_map/ppermute | solution.py:248
  26.4 23.2 %collective-permute-start = (s32[1]{0:T(128)}, s32[1]{0:T(128)}, u32[]{:S(2)}, u32[]{:S(2)}) collective-permute-start(s32[1]{0:T(128)} %param.9), channel_id=1, source_target_pairs={{0,8},{8,16},{16,24},{24,32},{32,40},{40,48},{48,56},{56,64},{64,7... | collective-permute-start | bytes 20 | tf_op jit(solution)/shard_map/ppermute | solution.py:237
  52.5 11.8 %collective-permute-start.7 = (f32[8,16,1024]{2,1,0:T(8,128)}, f32[8,16,1024]{2,1,0:T(8,128)S(1)}, u32[]{:S(2)}, u32[]{:S(2)}) collective-permute-start(f32[8,16,1024]{2,1,0:T(8,128)} %get-tuple-element.18), channel_id=1, source_target_pairs={{0,1},{2,3},{4,5},{6,7},{8,9},{10,11},{12,13},{14,15},{16,17},{18,... | collective-permute-start | bytes 1572872 | tf_op jit(solution)/shard_map/ppermute | solution.py:256
  53.8 23.4 %all-to-all-start = ((f32[256,1,64]{2,1,0:T(1,128)}), f32[256,1,64]{2,1,0:T(1,128)S(1)}, u32[]{:S(2)}, u32[]{:S(2)}) async-start(f32[256,1,64]{2,1,0:T(1,128)} %bitcast.4), calls=%async_computation | async-start | bytes 262144 | tf_op jit(solution)/shard_map/all_to_all | solution.py:257

commit v9 on v8

--- a/solution.py
+++ b/solution.py
@@ -43,45 +43,37 @@
     )
 
 
-def inner_kernel(
-    count_ref, k_any, ax_any, ay_any, mid_any, beyond_any, head_ref, tail_ref, k_ref, a_ref, q_ref, w_ref, sems, out_sems
-):
-    vectors, rows, _ = k_ref.shape
-    half = vectors // 2
-    groups = [pl.ds(0, half), pl.ds(half, vectors - half)]
-    copies = [
-        pltpu.make_async_copy(ax_any, a_ref.at[0], sems.at[0]),
-        pltpu.make_async_copy(ay_any, a_ref.at[1], sems.at[1]),
-    ] + [pltpu.make_async_copy(k_any.at[group], k_ref.at[group], sems.at[2 + i]) for i, group in enumerate(groups)]
+def pack_kernel(k_any, ax_any, ay_any, head_ref, tail_ref, low_ref, high_ref, sems):
+    rows = k_any.shape[1]
+    vectors = k_any.shape[0]
+    copies = []
+    for i, (at, target) in enumerate(((0, low_ref), (rows - TILE, high_ref))):
+        copies += [
+            pltpu.make_async_copy(k_any.at[:, pl.ds(at, TILE)], target.at[pl.ds(0, vectors)], sems.at[i, 0]),
+            pltpu.make_async_copy(ax_any.at[pl.ds(at, TILE)], target.at[vectors], sems.at[i, 1]),
+            pltpu.make_async_copy(ay_any.at[pl.ds(at, TILE)], target.at[vectors + 1], sems.at[i, 2]),
+        ]
     for copy in copies:
         copy.start()
-    for i in range(2):
-        copies[i].wait()
-        head_ref[vectors + i] = a_ref[i, :STEPS]
-        tail_ref[vectors + i] = a_ref[i, rows - STEPS :]
-    for i, w in enumerate(weights(a_ref[0], a_ref[1])):
+    for copy in copies:
+        copy.wait()
+    head_ref[...] = low_ref[:, :STEPS]
+    tail_ref[...] = high_ref[:, TILE - STEPS :]
+
+
+def inner_kernel(count_ref, k_ref, ax_ref, ay_ref, mid_ref, beyond_ref, q_ref, w_ref):
+    vectors, rows, _ = k_ref.shape
+    for i, w in enumerate(weights(ax_ref[...], ay_ref[...])):
         w_ref[i] = w
-    outs = []
-    for i, group in enumerate(groups):
-        copies[2 + i].wait()
-        first, size = group.start, group.size
-        head_ref[first : first + size] = k_ref[first : first + size, :STEPS]
-        tail_ref[first : first + size] = k_ref[first : first + size, rows - STEPS :]
-        q_ref[first : first + size] = k_ref[first : first + size]
-
-        @pl.loop(0, count_ref[0])
-        def _(_):
-            for b in range(first, first + size):
-                q_ref[b] = step(q_ref[b], w_ref[0], w_ref[1], w_ref[2], w_ref[3])
-
-        outs.append(
-            pltpu.make_async_copy(q_ref.at[group, pl.ds(TILE, rows - 2 * TILE)], mid_any.at[group], out_sems.at[i])
-        )
-        outs[i].start()
-    outs.append(pltpu.make_async_copy(k_ref.at[:, pl.ds(0, DRIFT)], beyond_any, out_sems.at[2]))
-    outs[-1].start()
-    for copy in outs:
-        copy.wait()
+    q_ref[...] = k_ref[...]
+
+    @pl.loop(0, count_ref[0])
+    def _(_):
+        for b in range(vectors):
+            q_ref[b] = step(q_ref[b], w_ref[0], w_ref[1], w_ref[2], w_ref[3])
+
+    mid_ref[...] = q_ref[:, TILE : rows - TILE]
+    beyond_ref[...] = k_ref[:, :DRIFT]
 
 
 def outer_kernel(count_ref, k_ref, ax_ref, ay_ref, left_ref, right_ref, edge_ref, table_ref, q_ref, w_ref):
@@ -182,12 +174,12 @@
     return pltpu.VMEM(shape, jnp.float32)
 
 
-def call(kernel, outs, ins, scratch, cost, limit=LIMIT, places=None):
+def call(kernel, outs, ins, scratch, cost, limit=LIMIT):
     return pl.pallas_call(
         kernel,
         out_shape=[jax.ShapeDtypeStruct(o, jnp.float32) for o in outs],
         in_specs=ins,
-        out_specs=places or [VMEM] * len(outs),
+        out_specs=[VMEM] * len(outs),
         scratch_shapes=scratch,
         compiler_params=pltpu.CompilerParams(vmem_limit_bytes=limit),
         cost_estimate=pl.CostEstimate(flops=cost << 30, bytes_accessed=cost << 20, transcendentals=0),
@@ -216,24 +208,23 @@
     backward = functools.partial(lax.ppermute, axis_name=("seg", "gx"), perm=[(b, a) for a, b in along])
     ahead = functools.partial(lax.ppermute, axis_name=("seg", "gx"), perm=rim_pairs(segs, strips, True))
 
-    mid, beyond, head, tail = call(
-        inner_kernel,
-        [(vectors, rows - 2 * TILE, cols), (vectors, DRIFT, cols)] + [(fields, STEPS, cols)] * 2,
-        [SMEM, ANY, ANY, ANY],
-        [
-            buffer(vectors, rows, cols),
-            buffer(2, rows, cols),
-            buffer(vectors, rows, cols),
-            buffer(4, rows, cols),
-            pltpu.SemaphoreType.DMA((4,)),
-            pltpu.SemaphoreType.DMA((3,)),
-        ],
-        64,
+    head, tail = call(
+        pack_kernel,
+        [(fields, STEPS, cols)] * 2,
+        [ANY] * 3,
+        [buffer(fields, TILE, cols), buffer(fields, TILE, cols), pltpu.SemaphoreType.DMA((2, 3))],
+        1,
         limit=FULL,
-        places=[ANY, ANY, VMEM, VMEM],
-    )(step_counts, k, ax, ay)
+    )(k, ax, ay)
     right = lax.ppermute(head, "gx", shift_pairs(strips, -1))
     left = lax.ppermute(tail, "gx", shift_pairs(strips, 1))
+    mid, beyond = call(
+        inner_kernel,
+        [(vectors, rows - 2 * TILE, cols), (vectors, DRIFT, cols)],
+        [SMEM, VMEM, VMEM, VMEM],
+        [buffer(vectors, rows, cols), buffer(4, rows, cols)],
+        64,
+    )(step_counts, k, ax, ay)
     drift = onward(drifts)
     edge, own = call(
         outer_kernel,
@@ -243,6 +234,7 @@
         0,
     )(step_counts, k, ax, ay, left, right)
     upper = ahead(jnp.concatenate([mid[:, -(DRIFT - TILE) :], edge[:, :TILE]], axis=1))
+    beyond, _ = lax.optimization_barrier((beyond, edge))
     beyond = backward(beyond)
     mid = onward(mid)
     edge = onward(edge)

time: 78.3 us -> 73.5 us (0.939)
  Pallas kernels: 14.4 us -> 10.2 us
  local copies, waits for them, and re-layouts: 1.71 us -> 0.72 us
    pallas_call x1, Pallas kernels: 5.79 us -> 1.42 us  [body(): call(inner_kernel, [(vectors, rows - 2 * TILE, cols), (vectors, DRIFT, co...]
    ppermute x1, starting transfers between devices: 4.88 us -> 1.32 us  [body(): beyond = backward(beyond)]
    ppermute x1, starting transfers between devices: 1.32 us -> 3.97 us  [body(): ahead(jnp.concatenate([mid[:, -(DRIFT - TILE):], edge[:, :TILE]], axis=1))]
    ppermute x1, waiting for transfers between devices: 2.3 us -> 4.76 us  [body(): right = lax.ppermute(head, 'gx', shift_pairs(strips, -1))]
    ppermute x1, starting transfers between devices: 0.43 us -> 2.7 us  [body(): drift = onward(drifts)]
    pallas_call x0 -> x1, Pallas kernels: none -> 1.96 us  [body(): call(pack_kernel, [(fields, STEPS, cols)] * 2, [ANY] * 3, [buffer(fields,...]
    ppermute x1, waiting for transfers between devices: 22.8 us -> 20.8 us  [body(): drift = onward(drifts)]
    pallas_call x1, Pallas kernels: 3.78 us -> 2.16 us  [body(): call(outer_kernel, [(vectors, 2 * TILE, cols), (pairs, 128)], [SMEM] + [V...]
  transfers between devices with their start and end apart: 9 -> 9, of which waited for: 3 -> 3; matrix products, arithmetic and copies ran while one was open for 1% -> 0% of each run, Pallas kernels for 7% -> 7%
where the time goes in v9:
time: 73.5 us; the launch traced here: 73.3 us
  waiting for transfers between devices  36.6 us (50%)
  starting transfers between devices  24.2 us (33%)
  Pallas kernels  10.2 us (14%)
  between operations  1.43 us (2%)
    ppermute x1, waiting for transfers between devices, body(): drift = onward(drifts)  20.8 us
    all_to_all x1, waiting for transfers between devices, body(): gram = lax.all_to_all(gram, ('seg', 'gx'), 0, 0)  11 us
    all_to_all x1, starting transfers between devices, body(): gram = lax.all_to_all(gram, ('seg', 'gx'), 0, 0)  9.16 us
    ppermute x1, waiting for transfers between devices, body(): right = lax.ppermute(head, 'gx', shift_pairs(strips, -1))  4.76 us
    ppermute x1, starting transfers between devices, body(): left = lax.ppermute(tail, 'gx', shift_pairs(strips, 1))  4.46 us
    ppermute x1, starting transfers between devices, body(): ahead(jnp.concatenate([mid[:, -(DRIFT - TILE):], edge[:, :TILE]], axis=1))  3.97 us
    pallas_call x1, Pallas kernels, body(): call(gram_kernel, [(world, pairs), (vectors, DRIFT, cols)], [SMEM] + [VME...  2.8 us
    ppermute x1, starting transfers between devices, body(): drift = onward(drifts)  2.7 us
  transfers between devices with their start and end apart: 9, of which 3 were waited for; matrix products, arithmetic and copies ran while one was open for 0% of the time, Pallas kernels for 7%

profile of v9, /device:TPU:1, one launch (start us, length us, event | category | flops | bytes accessed | tf_op | source)
XLA Modules:
  0.0 73.3 jit_solution(2550633992085677157)
XLA Ops:
  0.7 2.0 %shard_map.69 = (f32[10,4,1024]{2,1,0:T(4,128)}, f32[10,4,1024]{2,1,0:T(4,128)}) custom-call(f32[8,32,1024]{2,1,0:T(8,128)} %bitcast.8, f32[32,1024]{1,0:T(8,128)} %bitcast.13, f32[32,1024]{1,0:T(8,128)} %bitcast.16), custom_call_target="tpu_custom_call" | custom-call | flops 1073741824 | bytes 1048576 | tf_op jit(solution)/shard_map/pallas_call | solution.py:211
  2.6 4.5 %collective-permute-start.2 = (f32[10,4,1024]{2,1,0:T(4,128)}, f32[10,4,1024]{2,1,0:T(4,128)S(1)}, u32[]{:S(2)}, u32[]{:S(2)}) collective-permute-start(f32[10,4,1024]{2,1,0:T(4,128)} %get-tuple-element.14), channel_id=1, source_target_pairs={{0,1},{1,2},{2,3},{3,4},{4,5},{5,6},{6,7},{7,0},{8,9},{9,10},{10,1... | collective-permute-start | bytes 491528 | tf_op jit(solution)/shard_map/ppermute | solution.py:220
  7.1 0.0 collective-permute-start.3
  7.8 1.4 %shard_map.68 = (f32[8,16,1024]{2,1,0:T(8,128)S(1)}, f32[8,16,1024]{2,1,0:T(8,128)S(1)}) custom-call(s32[1]{0:T(128)S(6)} %copy.8.count_ref, f32[8,32,1024]{2,1,0:T(8,128)S(1)} %bitcast.9, f32[32,1024]{1,0:T(8,128)S(1)} %bitcast.14, f32[32,1024]{1,0:T(8,128)S(1)} %bitcast.17), custom_call_target="tpu_custom_call" | custom-call | flops 68719476736 | bytes 67108864 | tf_op jit(solution)/shard_map/pallas_call | solution.py:221
  9.2 0.8 %collective-permute-start.1 = (f32[8,16,1024]{2,1,0:T(8,128)S(1)}, f32[8,16,1024]{2,1,0:T(8,128)S(1)}, u32[]{:S(2)}, u32[]{:S(2)}) collective-permute-start(f32[8,16,1024]{2,1,0:T(8,128)S(1)} %get-tuple-element.13), channel_id=1, source_target_pairs={{0,8},{8,16},{16,24},{24,32},{32,40},{40,48},{48,56},{56,64},{64,7... | collective-permute-start | bytes 1572872 | tf_op jit(solution)/shard_map/ppermute | solution.py:239
  10.0 0.0 collective-permute-done.2.left_ref
  10.0 4.8 %collective-permute-done.3.right_ref = f32[10,4,1024]{2,1,0:T(4,128)S(1)} collective-permute-done((f32[10,4,1024]{2,1,0:T(4,128)}, f32[10,4,1024]{2,1,0:T(4,128)S(1)}, u32[]{:S(2)}, u32[]{:S(2)}) %collective-permute-start.3) | collective-permute-done | bytes 163872 | tf_op jit(solution)/shard_map/ppermute | solution.py:219
  14.7 2.2 %shard_map.70 = (f32[8,16,1024]{2,1,0:T(8,128)S(1)}, f32[64,128]{1,0:T(8,128)S(1)}) custom-call(s32[1]{0:T(128)S(6)} %copy.8.count_ref, f32[8,32,1024]{2,1,0:T(8,128)S(1)} %bitcast.10, f32[32,1024]{1,0:T(8,128)S(1)} %bitcast.15, f32[32,1024]{1,0:T(8,128)S(1)} %bitcast.18, f32[10,4,1024]{2,1,0:T(4,128)S(1)} %collective-permute-done.2.left_ref, ...), custom_call_target="tpu_custom_call" | custom-call | tf_op jit(solution)/shard_map/pallas_call | solution.py:229
  16.9 0.6 collective-permute-start.4
  17.5 4.0 %collective-permute-start.6 = (f32[8,16,1024]{2,1,0:T(8,128)S(1)}, f32[8,16,1024]{2,1,0:T(8,128)S(1)}, u32[]{:S(2)}, u32[]{:S(2)}) collective-permute-start(f32[8,16,1024]{2,1,0:T(8,128)S(1)} %pad_maximum_fusion), channel_id=1, source_target_pairs={{249,2},{251,4},{253,6},{255,0},{1,10},{3,12},{5,14},{7,8},{9,18},... | collective-permute-start | bytes 1572872 | tf_op jit(solution)/shard_map/ppermute | solution.py:236
  21.5 1.3 %collective-permute-start.5 = (f32[8,16,1024]{2,1,0:T(8,128)S(1)}, f32[8,16,1024]{2,1,0:T(8,128)S(1)}, u32[]{:S(2)}, u32[]{:S(2)}) collective-permute-start(f32[8,16,1024]{2,1,0:T(8,128)S(1)} %get-tuple-element.18), channel_id=1, source_target_pairs={{1,0},{3,2},{5,4},{7,6},{9,8},{11,10},{13,12},{15,14},{17,16},{19,... | collective-permute-start | bytes 1572872 | tf_op jit(solution)/shard_map/ppermute | solution.py:238
  22.8 2.7 %collective-permute-start = (s32[1]{0:T(128)}, s32[1]{0:T(128)}, u32[]{:S(2)}, u32[]{:S(2)}) collective-permute-start(s32[1]{0:T(128)} %param.9), channel_id=1, source_target_pairs={{0,8},{8,16},{16,24},{24,32},{32,40},{40,48},{48,56},{56,64},{64,7... | collective-permute-start | bytes 20 | tf_op jit(solution)/shard_map/ppermute | solution.py:228
  25.5 20.8 %collective-permute-done.drift_ref = s32[1]{0:T(128)} collective-permute-done((s32[1]{0:T(128)}, s32[1]{0:T(128)}, u32[]{:S(2)}, u32[]{:S(2)}) %collective-permute-start) | collective-permute-done | bytes 36 | tf_op jit(solution)/shard_map/ppermute | solution.py:228
  46.4 0.0 collective-permute-done.1.mid_ref
  46.4 0.0 collective-permute-done.4.edge_ref
  46.4 0.0 collective-permute-done.6.upper_ref
  46.4 2.8 %shard_map.71 = (f32[256,64]{1,0:T(8,128)}, f32[8,16,1024]{2,1,0:T(8,128)}) custom-call(s32[1]{0:T(128)} %collective-permute-done.drift_ref, f32[8,32,1024]{2,1,0:T(8,128)S(1)} %bitcast.11, f32[8,16,1024]{2,1,0:T(8,128)S(1)} %collective-permute-done.5.beyond_ref, f32[8,16,1024]{2,1,0:T(8,128)S(1)} %collective-permute-done.1.mid_ref, ...), custom_call_target="tpu_custom_call" | custom-call | flops 1073741824 | bytes 1048576 | tf_op jit(solution)/shard_map/pallas_call | solution.py:241
  49.2 1.3 %collective-permute-start.7 = (f32[8,16,1024]{2,1,0:T(8,128)}, f32[8,16,1024]{2,1,0:T(8,128)S(1)}, u32[]{:S(2)}, u32[]{:S(2)}) collective-permute-start(f32[8,16,1024]{2,1,0:T(8,128)} %get-tuple-element.20), channel_id=1, source_target_pairs={{0,1},{2,3},{4,5},{6,7},{8,9},{10,11},{12,13},{14,15},{16,17},{18,... | collective-permute-start | bytes 1572872 | tf_op jit(solution)/shard_map/ppermute | solution.py:248
  50.5 9.2 %all-to-all-start = ((f32[256,1,64]{2,1,0:T(1,128)}), f32[256,1,64]{2,1,0:T(1,128)S(1)}, u32[]{:S(2)}, u32[]{:S(2)}) async-start(f32[256,1,64]{2,1,0:T(1,128)} %bitcast.4), calls=%async_computation | async-start | bytes 262144 | tf_op jit(solution)/shard_map/all_to_all | solution.py:249
  59.7 0.0 collective-permute-done.7.rim_ref
  59.7 1.9 %shard_map.72 = f32[8,32,1024]{2,1,0:T(8,128)} custom-call(s32[1]{0:T(128)} %collective-permute-done.drift_ref, f32[8,32,1024]{2,1,0:T(8,128)S(1)} %bitcast.12, f32[8,16,1024]{2,1,0:T(8,128)S(1)} %collective-permute-done.1.mid_ref, f32[8,16,1024]{2,1,0:T(8,128)S(1)} %collective-permute-done.4.edge_ref, f32[8,16,1024]{2,1,0:T(8,128)S(1)} %collective-permute-done.7.rim_ref, ...), custom_call_target="tpu_custom_call" | custom-call | flops 1073741824 | bytes 1048576 | tf_op jit(solution)/shard_map/pallas_call | solution.py:250
  61.6 11.0 %all-to-all-done = f32[256,1,64]{2,1,0:T(1,128)S(1)} async-done(((f32[256,1,64]{2,1,0:T(1,128)}), f32[256,1,64]{2,1,0:T(1,128)S(1)}, u32[]{:S(2)}, u32[]{:S(2)}) %all-to-all-start) | async-done | bytes 65568 | tf_op jit(solution)/shard_map/all_to_all | solution.py:249
  72.5 0.1 reduce_sum.9
  72.6 0.7 div.10
  (11 shorter events, 0.1 us)
Async XLA Ops:
  0.6 7.1 %copy-start = (f32[1,8,32,1024]{3,2,1,0:T(8,128)S(1)}, f32[1,8,32,1024]{3,2,1,0:T(8,128)}, u32[]{:S(2)}) copy-start(f32[1,8,32,1024]{3,2,1,0:T(8,128)} %param.5) | copy-start | bytes 3145732
  0.6 7.1 %copy-start.1 = (f32[1,32,1024]{2,1,0:T(8,128)S(1)}, f32[1,32,1024]{2,1,0:T(8,128)}, u32[]{:S(2)}) copy-start(f32[1,32,1024]{2,1,0:T(8,128)} %param.6) | copy-start | bytes 393220
  0.6 7.1 %copy-start.2 = (f32[1,32,1024]{2,1,0:T(8,128)S(1)}, f32[1,32,1024]{2,1,0:T(8,128)}, u32[]{:S(2)}) copy-start(f32[1,32,1024]{2,1,0:T(8,128)} %param.7) | copy-start | bytes 393220
  2.6 7.3 %collective-permute-start.2 = (f32[10,4,1024]{2,1,0:T(4,128)}, f32[10,4,1024]{2,1,0:T(4,128)S(1)}, u32[]{:S(2)}, u32[]{:S(2)}) collective-permute-start(f32[10,4,1024]{2,1,0:T(4,128)} %get-tuple-element.14), channel_id=1, source_target_pairs={{0,1},{1,2},{2,3},{3,4},{4,5},{5,6},{6,7},{7,0},{8,9},{9,10},{10,1... | collective-permute-start | bytes 491528 | tf_op jit(solution)/shard_map/ppermute | solution.py:220
  7.1 7.7 %collective-permute-start.3 = (f32[10,4,1024]{2,1,0:T(4,128)}, f32[10,4,1024]{2,1,0:T(4,128)S(1)}, u32[]{:S(2)}, u32[]{:S(2)}) collective-permute-start(f32[10,4,1024]{2,1,0:T(4,128)} %get-tuple-element.15), channel_id=1, source_target_pairs={{0,7},{1,0},{2,1},{3,2},{4,3},{5,4},{6,5},{7,6},{8,15},{9,8},{10,9... | collective-permute-start | bytes 491528 | tf_op jit(solution)/shard_map/ppermute | solution.py:219
  9.2 37.2 %collective-permute-start.1 = (f32[8,16,1024]{2,1,0:T(8,128)S(1)}, f32[8,16,1024]{2,1,0:T(8,128)S(1)}, u32[]{:S(2)}, u32[]{:S(2)}) collective-permute-start(f32[8,16,1024]{2,1,0:T(8,128)S(1)} %get-tuple-element.13), channel_id=1, source_target_pairs={{0,8},{8,16},{16,24},{24,32},{32,40},{40,48},{48,56},{56,64},{64,7... | collective-permute-start | bytes 1572872 | tf_op jit(solution)/shard_map/ppermute | solution.py:239
  16.9 29.5 %collective-permute-start.4 = (f32[8,16,1024]{2,1,0:T(8,128)S(1)}, f32[8,16,1024]{2,1,0:T(8,128)S(1)}, u32[]{:S(2)}, u32[]{:S(2)}) collective-permute-start(f32[8,16,1024]{2,1,0:T(8,128)S(1)} %get-tuple-element.16), channel_id=1, source_target_pairs={{0,8},{8,16},{16,24},{24,32},{32,40},{40,48},{48,56},{56,64},{64,7... | collective-permute-start | bytes 1572872 | tf_op jit(solution)/shard_map/ppermute | solution.py:240
  17.5 28.9 %collective-permute-start.6 = (f32[8,16,1024]{2,1,0:T(8,128)S(1)}, f32[8,16,1024]{2,1,0:T(8,128)S(1)}, u32[]{:S(2)}, u32[]{:S(2)}) collective-permute-start(f32[8,16,1024]{2,1,0:T(8,128)S(1)} %pad_maximum_fusion), channel_id=1, source_target_pairs={{249,2},{251,4},{253,6},{255,0},{1,10},{3,12},{5,14},{7,8},{9,18},... | collective-permute-start | bytes 1572872 | tf_op jit(solution)/shard_map/ppermute | solution.py:236
  21.5 24.9 %collective-permute-start.5 = (f32[8,16,1024]{2,1,0:T(8,128)S(1)}, f32[8,16,1024]{2,1,0:T(8,128)S(1)}, u32[]{:S(2)}, u32[]{:S(2)}) collective-permute-start(f32[8,16,1024]{2,1,0:T(8,128)S(1)} %get-tuple-element.18), channel_id=1, source_target_pairs={{1,0},{3,2},{5,4},{7,6},{9,8},{11,10},{13,12},{15,14},{17,16},{19,... | collective-permute-start | bytes 1572872 | tf_op jit(solution)/shard_map/ppermute | solution.py:238
  22.8 23.5 %collective-permute-start = (s32[1]{0:T(128)}, s32[1]{0:T(128)}, u32[]{:S(2)}, u32[]{:S(2)}) collective-permute-start(s32[1]{0:T(128)} %param.9), channel_id=1, source_target_pairs={{0,8},{8,16},{16,24},{24,32},{32,40},{40,48},{48,56},{56,64},{64,7... | collective-permute-start | bytes 20 | tf_op jit(solution)/shard_map/ppermute | solution.py:228
  49.2 10.5 %collective-permute-start.7 = (f32[8,16,1024]{2,1,0:T(8,128)}, f32[8,16,1024]{2,1,0:T(8,128)S(1)}, u32[]{:S(2)}, u32[]{:S(2)}) collective-permute-start(f32[8,16,1024]{2,1,0:T(8,128)} %get-tuple-element.20), channel_id=1, source_target_pairs={{0,1},{2,3},{4,5},{6,7},{8,9},{10,11},{12,13},{14,15},{16,17},{18,... | collective-permute-start | bytes 1572872 | tf_op jit(solution)/shard_map/ppermute | solution.py:248
  50.5 22.0 %all-to-all-start = ((f32[256,1,64]{2,1,0:T(1,128)}), f32[256,1,64]{2,1,0:T(1,128)S(1)}, u32[]{:S(2)}, u32[]{:S(2)}) async-start(f32[256,1,64]{2,1,0:T(1,128)} %bitcast.4), calls=%async_computation | async-start | bytes 262144 | tf_op jit(solution)/shard_map/all_to_all | solution.py:249

commit v10 on v4

--- a/solution.py
+++ b/solution.py
@@ -10,9 +10,11 @@
 DRIFT = 16
 TILE = 8
 
+ANY = pl.BlockSpec(memory_space=pl.ANY)
 VMEM = pl.BlockSpec(memory_space=pltpu.VMEM)
 SMEM = pl.BlockSpec(memory_space=pltpu.SMEM)
 LIMIT = 12 * 1024 * 1024
+FULL = 60 * 1024 * 1024
 
 
 def shift_pairs(count, by):
@@ -39,6 +41,24 @@
         + wn * pltpu.roll(q, cols - 1, 1)
         + ws * pltpu.roll(q, 1, 1)
     )
+
+
+def pack_kernel(k_any, ax_any, ay_any, head_ref, tail_ref, low_ref, high_ref, sems):
+    rows = k_any.shape[1]
+    vectors = k_any.shape[0]
+    copies = []
+    for i, (at, target) in enumerate(((0, low_ref), (rows - TILE, high_ref))):
+        copies += [
+            pltpu.make_async_copy(k_any.at[:, pl.ds(at, TILE)], target.at[pl.ds(0, vectors)], sems.at[i, 0]),
+            pltpu.make_async_copy(ax_any.at[pl.ds(at, TILE)], target.at[vectors], sems.at[i, 1]),
+            pltpu.make_async_copy(ay_any.at[pl.ds(at, TILE)], target.at[vectors + 1], sems.at[i, 2]),
+        ]
+    for copy in copies:
+        copy.start()
+    for copy in copies:
+        copy.wait()
+    head_ref[...] = low_ref[:, :STEPS]
+    tail_ref[...] = high_ref[:, TILE - STEPS :]
 
 
 def inner_kernel(count_ref, k_ref, ax_ref, ay_ref, mid_ref, beyond_ref, q_ref, w_ref):
@@ -144,14 +164,14 @@
     return pltpu.VMEM(shape, jnp.float32)
 
 
-def call(kernel, outs, ins, scratch, cost):
+def call(kernel, outs, ins, scratch, cost, limit=LIMIT):
     return pl.pallas_call(
         kernel,
         out_shape=[jax.ShapeDtypeStruct(o, jnp.float32) for o in outs],
         in_specs=ins,
         out_specs=[VMEM] * len(outs),
         scratch_shapes=scratch,
-        compiler_params=pltpu.CompilerParams(vmem_limit_bytes=LIMIT),
+        compiler_params=pltpu.CompilerParams(vmem_limit_bytes=limit),
         cost_estimate=pl.CostEstimate(flops=cost << 30, bytes_accessed=4 << 20, transcendentals=0),
     )
 
@@ -166,9 +186,15 @@
     sideways = functools.partial(lax.ppermute, axis_name="gx", perm=shift_pairs(strips, 1))
     backward = functools.partial(lax.ppermute, axis_name="gx", perm=shift_pairs(strips, -1))
 
-    tail = jnp.concatenate([k[:, rows - STEPS :], ax[None, rows - STEPS :], ay[None, rows - STEPS :]], axis=0)
-    head = jnp.concatenate([k[:, :STEPS], ax[None, :STEPS], ay[None, :STEPS]], axis=0)
-    tail, head, k, ax, ay = lax.optimization_barrier((tail, head, k, ax, ay))
+    fields = vectors + 2
+    head, tail = call(
+        pack_kernel,
+        [(fields, STEPS, cols)] * 2,
+        [ANY] * 3,
+        [buffer(fields, TILE, cols), buffer(fields, TILE, cols), pltpu.SemaphoreType.DMA((2, 3))],
+        1,
+        limit=FULL,
+    )(k, ax, ay)
     right = backward(head)
     left = sideways(tail)
     drift = onward(drifts)
@@ -179,7 +205,7 @@
         [buffer(vectors, rows, cols), buffer(4, rows, cols)],
         64,
     )(step_counts, k, ax, ay)
-    beyond, right = lax.optimization_barrier((beyond, right))
+    beyond, right, left = lax.optimization_barrier((beyond, right, left))
     beyond = backward(beyond)
     mid = lax.ppermute(mid, "seg", [(s, s // half * half + (s + 1) % half) for s in range(segs)])
     (edge,) = call(

time: 71 us -> 78.5 us (1.11); the launches traced: 69.9 us -> 79 us
  starting transfers between devices: 26.2 us -> 41.6 us
  waiting for transfers between devices: 28.5 us -> 24.1 us
  local copies, waits for them, and re-layouts: 3.46 us -> 0.73 us
  Pallas kernels: 10.1 us -> 11.1 us
    all_to_all x1, starting transfers between devices: 7.06 us -> 12.1 us  [body(): gram = lax.all_to_all(gram, ('seg', 'gx'), 0, 0)]
    ppermute x1, starting transfers between devices: 6.92 us -> 11.4 us  [body(): rim_mid = sideways(mid[:, -(DRIFT - TILE):])]
    ppermute x1, waiting for transfers between devices: 3.57 us -> 0.01 us  [body(): left = sideways(tail)]
    ppermute x1, starting transfers between devices: 2.73 us -> 6.27 us  [body(): beyond = backward(beyond)]
    slice x3 -> x0, local copies, waits for them, and re-layouts: 2.73 us -> none  [the longest x1 1.08 us: body(): k[:, :STEPS]]
    ppermute x1, waiting for transfers between devices: 0.38 us -> 2.78 us  [body(): lax.ppermute(mid, 'seg', [(s, s // half * half + (s + 1) % half) for s in...]
    pallas_call x0 -> x1, Pallas kernels: none -> 1.96 us  [body(): call(pack_kernel, [(fields, STEPS, cols)] * 2, [ANY] * 3, [buffer(fields,...]
    ppermute x1, waiting for transfers between devices: 9.84 us -> 8.21 us  [body(): crossed = lax.ppermute(held, 'seg', [(0, half), (half, 0)])]
  transfers between devices with their start and end apart: 10 -> 10, of which waited for: 6 -> 4; matrix products, arithmetic and copies ran while one was open for 0% -> 0% of each run, Pallas kernels for 14% -> 12%
where the time goes in v10:
time: 78.5 us; the launch traced here: 79 us
  starting transfers between devices  41.6 us (53%)
  waiting for transfers between devices  24.1 us (31%)
  Pallas kernels  11.1 us (14%)
  between operations  1.44 us (2%)
    all_to_all x1, starting transfers between devices, body(): gram = lax.all_to_all(gram, ('seg', 'gx'), 0, 0)  12.1 us
    ppermute x1, starting transfers between devices, body(): rim_mid = sideways(mid[:, -(DRIFT - TILE):])  11.4 us
    all_to_all x1, waiting for transfers between devices, body(): gram = lax.all_to_all(gram, ('seg', 'gx'), 0, 0)  11 us
    ppermute x1, waiting for transfers between devices, body(): crossed = lax.ppermute(held, 'seg', [(0, half), (half, 0)])  8.21 us
    ppermute x1, starting transfers between devices, body(): beyond = backward(beyond)  6.27 us
    ppermute x1, starting transfers between devices, body(): crossed = lax.ppermute(held, 'seg', [(0, half), (half, 0)])  4.02 us
    ppermute x1, starting transfers between devices, body(): right = backward(head)  3.32 us
    ppermute x1, waiting for transfers between devices, body(): lax.ppermute(mid, 'seg', [(s, s // half * half + (s + 1) % half) for s in...  2.78 us
  transfers between devices with their start and end apart: 10, of which 4 were waited for; matrix products, arithmetic and copies ran while one was open for 0% of the time, Pallas kernels for 12%

profile of v10, /device:TPU:1, one launch (start us, length us, event | category | flops | bytes accessed | tf_op | source)
XLA Modules:
  0.0 79.0 jit_solution(12269585414646347855)
XLA Ops:
  0.7 2.0 %shard_map.69 = (f32[10,4,1024]{2,1,0:T(4,128)}, f32[10,4,1024]{2,1,0:T(4,128)}) custom-call(f32[8,32,1024]{2,1,0:T(8,128)} %bitcast.8, f32[32,1024]{1,0:T(8,128)} %bitcast.13, f32[32,1024]{1,0:T(8,128)} %bitcast.16), custom_call_target="tpu_custom_call" | custom-call | flops 1073741824 | bytes 4194304 | tf_op jit(solution)/shard_map/pallas_call | solution.py:190
  2.6 3.3 %collective-permute-start.3 = (f32[10,4,1024]{2,1,0:T(4,128)}, f32[10,4,1024]{2,1,0:T(4,128)S(1)}, u32[]{:S(2)}, u32[]{:S(2)}) collective-permute-start(f32[10,4,1024]{2,1,0:T(4,128)} %get-tuple-element.18), channel_id=1, source_target_pairs={{0,7},{1,0},{2,1},{3,2},{4,3},{5,4},{6,5},{7,6},{8,15},{9,8},{10,9... | collective-permute-start | bytes 491528 | tf_op jit(solution)/shard_map/ppermute | solution.py:198
  6.0 1.2 %collective-permute-start.4 = (f32[10,4,1024]{2,1,0:T(4,128)}, f32[10,4,1024]{2,1,0:T(4,128)S(1)}, u32[]{:S(2)}, u32[]{:S(2)}) collective-permute-start(f32[10,4,1024]{2,1,0:T(4,128)} %get-tuple-element.19), channel_id=1, source_target_pairs={{0,1},{1,2},{2,3},{3,4},{4,5},{5,6},{6,7},{7,0},{8,9},{9,10},{10,1... | collective-permute-start | bytes 491528 | tf_op jit(solution)/shard_map/ppermute | solution.py:199
  7.9 2.0 %shard_map.68 = (f32[8,16,1024]{2,1,0:T(8,128)S(1)}, f32[8,16,1024]{2,1,0:T(8,128)S(1)}) custom-call(s32[1]{0:T(128)S(6)} %copy.8.count_ref, f32[8,32,1024]{2,1,0:T(8,128)S(1)} %bitcast.9, f32[32,1024]{1,0:T(8,128)S(1)} %bitcast.14, f32[32,1024]{1,0:T(8,128)S(1)} %bitcast.17), custom_call_target="tpu_custom_call" | custom-call | flops 68719476736 | bytes 4194304 | tf_op jit(solution)/shard_map/pallas_call | solution.py:201
  9.9 0.1 collective-permute-start.1
  10.0 2.0 %collective-permute-done.3.right_ref = f32[10,4,1024]{2,1,0:T(4,128)S(1)} collective-permute-done((f32[10,4,1024]{2,1,0:T(4,128)}, f32[10,4,1024]{2,1,0:T(4,128)S(1)}, u32[]{:S(2)}, u32[]{:S(2)}) %collective-permute-start.3) | collective-permute-done | bytes 163872 | tf_op jit(solution)/shard_map/ppermute | solution.py:198
  12.1 6.3 %collective-permute-start.6 = (f32[8,16,1024]{2,1,0:T(8,128)S(1)}, f32[8,16,1024]{2,1,0:T(8,128)S(1)}, u32[]{:S(2)}, u32[]{:S(2)}) collective-permute-start(f32[8,16,1024]{2,1,0:T(8,128)S(1)} %get-tuple-element.23), channel_id=1, source_target_pairs={{0,7},{1,0},{2,1},{3,2},{4,3},{5,4},{6,5},{7,6},{8,15},{9,8},{10,9... | collective-permute-start | bytes 1572872 | tf_op jit(solution)/shard_map/ppermute | solution.py:209
  18.3 1.3 %collective-permute-start = (s32[1]{0:T(128)}, s32[1]{0:T(128)}, u32[]{:S(2)}, u32[]{:S(2)}) collective-permute-start(s32[1]{0:T(128)} %param.9), channel_id=1, source_target_pairs={{0,8},{8,16},{16,24},{24,32},{32,40},{40,48},{48,56},{56,64},{64,7... | collective-permute-start | bytes 20 | tf_op jit(solution)/shard_map/ppermute | solution.py:200
  19.6 2.6 %shard_map.70 = f32[8,16,1024]{2,1,0:T(8,128)S(1)} custom-call(s32[1]{0:T(128)S(6)} %copy.8.count_ref, f32[8,32,1024]{2,1,0:T(8,128)S(1)} %bitcast.10, f32[32,1024]{1,0:T(8,128)S(1)} %bitcast.15, f32[32,1024]{1,0:T(8,128)S(1)} %bitcast.18, f32[10,4,1024]{2,1,0:T(4,128)S(1)} %collective-permute-done.4.left_ref, ...), custom_call_target="tpu_custom_call" | custom-call | flops 1073741824 | bytes 4194304 | tf_op jit(solution)/shard_map/pallas_call | solution.py:211
  22.2 0.1 collective-permute-start.5
  22.3 2.8 %collective-permute-done.1 = f32[8,16,1024]{2,1,0:T(8,128)} collective-permute-done((f32[8,16,1024]{2,1,0:T(8,128)S(1)}, f32[8,16,1024]{2,1,0:T(8,128)}, u32[]{:S(2)}, u32[]{:S(2)}) %collective-permute-start.1) | collective-permute-done | bytes 524320 | tf_op jit(solution)/shard_map/ppermute | solution.py:210
  25.1 4.0 %collective-permute-start.2 = (f32[8,16,1024]{2,1,0:T(8,128)}, f32[8,16,1024]{2,1,0:T(8,128)S(1)}, u32[]{:S(2)}, u32[]{:S(2)}) collective-permute-start(f32[8,16,1024]{2,1,0:T(8,128)} %collective-permute-done.1), channel_id=1, source_target_pairs={{0,128},{128,0},{1,129},{129,1},{2,130},{130,2},{3,131},{131,3},{4... | collective-permute-start | bytes 1572872 | tf_op jit(solution)/shard_map/ppermute | solution.py:222
  29.1 0.0 collective-permute-done.6.beyond_ref
  29.1 1.1 %shard_map.71 = (f32[64,128]{1,0:T(8,128)S(1)}, f32[8,32,1024]{2,1,0:T(8,128)S(1)}) custom-call(s32[1]{0:T(128)} %collective-permute-done.drift_ref, f32[8,32,1024]{2,1,0:T(8,128)S(1)} %bitcast.11, f32[8,16,1024]{2,1,0:T(8,128)S(1)} %collective-permute-done.6.beyond_ref), custom_call_target="tpu_custom_call" | custom-call | flops 17179869184 | bytes 4194304 | tf_op jit(solution)/shard_map/pallas_call | solution.py:220
  30.3 8.2 %collective-permute-done.2 = f32[8,16,1024]{2,1,0:T(8,128)S(1)} collective-permute-done((f32[8,16,1024]{2,1,0:T(8,128)}, f32[8,16,1024]{2,1,0:T(8,128)S(1)}, u32[]{:S(2)}, u32[]{:S(2)}) %collective-permute-start.2) | collective-permute-done | bytes 524320 | tf_op jit(solution)/shard_map/ppermute | solution.py:222
  38.5 0.1 broadcast_select_fusion.mid_ref
  38.6 11.4 %collective-permute-start.7 = (f32[8,8,1024]{2,1,0:T(8,128)S(1)}, f32[8,8,1024]{2,1,0:T(8,128)S(1)}, u32[]{:S(2)}, u32[]{:S(2)}) collective-permute-start(f32[8,8,1024]{2,1,0:T(8,128)S(1)} %slice.8), channel_id=1, source_target_pairs={{0,1},{1,2},{2,3},{3,4},{4,5},{5,6},{6,7},{7,0},{8,9},{9,10},{10,1... | collective-permute-start | bytes 786440 | tf_op jit(solution)/shard_map/ppermute | solution.py:224
  50.1 1.7 %collective-permute-start.8 = (f32[8,8,1024]{2,1,0:T(8,128)S(1)}, f32[8,8,1024]{2,1,0:T(8,128)S(1)}, u32[]{:S(2)}, u32[]{:S(2)}) collective-permute-start(f32[8,8,1024]{2,1,0:T(8,128)S(1)} %slice.7), channel_id=1, source_target_pairs={{0,1},{1,2},{2,3},{3,4},{4,5},{5,6},{6,7},{7,0},{8,9},{9,10},{10,1... | collective-permute-start | bytes 786440 | tf_op jit(solution)/shard_map/ppermute | solution.py:226
  51.7 1.5 %shard_map.73 = f32[256,64]{1,0:T(8,128)} custom-call(f32[8,32,1024]{2,1,0:T(8,128)S(1)} %get-tuple-element.26.shifted_ref, f32[8,16,1024]{2,1,0:T(8,128)S(1)} %broadcast_select_fusion.mid_ref, f32[8,16,1024]{2,1,0:T(8,128)S(1)} %collective-permute-done.5.edge_ref, f32[64,128]{1,0:T(8,128)S(1)} %get-tuple-element.27.own_ref), custom_call_target="tpu_custom_call" | custom-call | flops 1073741824 | bytes 4194304 | tf_op jit(solution)/shard_map/pallas_call | solution.py:227
  53.2 12.1 %all-to-all-start = ((f32[256,1,64]{2,1,0:T(1,128)}), f32[256,1,64]{2,1,0:T(1,128)S(1)}, u32[]{:S(2)}, u32[]{:S(2)}) async-start(f32[256,1,64]{2,1,0:T(1,128)} %bitcast.4), calls=%async_computation | async-start | bytes 262144 | tf_op jit(solution)/shard_map/all_to_all | solution.py:228
  65.4 1.8 %shard_map.72 = f32[8,32,1024]{2,1,0:T(8,128)} custom-call(s32[1]{0:T(128)} %collective-permute-done.drift_ref, f32[8,32,1024]{2,1,0:T(8,128)S(1)} %bitcast.12, f32[8,16,1024]{2,1,0:T(8,128)S(1)} %broadcast_select_fusion.mid_ref, f32[8,16,1024]{2,1,0:T(8,128)S(1)} %collective-permute-done.5.edge_ref, f32[8,8,1024]{2,1,0:T(8,128)S(1)} %collective-permute-done.7.rim_mid_ref, ...), custom_call_target="tpu_custom_call" | custom-call | flops 1073741824 | bytes 4194304 | tf_op jit(solution)/shard_map/pallas_call | solution.py:229
  67.2 11.0 %all-to-all-done = f32[256,1,64]{2,1,0:T(1,128)S(1)} async-done(((f32[256,1,64]{2,1,0:T(1,128)}), f32[256,1,64]{2,1,0:T(1,128)S(1)}, u32[]{:S(2)}, u32[]{:S(2)}) %all-to-all-start) | async-done | bytes 65568 | tf_op jit(solution)/shard_map/all_to_all | solution.py:228
  78.2 0.1 reduce_sum.9
  78.3 0.7 div.10
  (14 shorter events, 0.1 us)
Async XLA Ops:
  0.6 7.2 %copy-start = (f32[1,8,32,1024]{3,2,1,0:T(8,128)S(1)}, f32[1,8,32,1024]{3,2,1,0:T(8,128)}, u32[]{:S(2)}) copy-start(f32[1,8,32,1024]{3,2,1,0:T(8,128)} %param.5) | copy-start | bytes 3145732
  0.6 7.2 %copy-start.1 = (f32[1,32,1024]{2,1,0:T(8,128)S(1)}, f32[1,32,1024]{2,1,0:T(8,128)}, u32[]{:S(2)}) copy-start(f32[1,32,1024]{2,1,0:T(8,128)} %param.6) | copy-start | bytes 393220
  0.6 7.2 %copy-start.2 = (f32[1,32,1024]{2,1,0:T(8,128)S(1)}, f32[1,32,1024]{2,1,0:T(8,128)}, u32[]{:S(2)}) copy-start(f32[1,32,1024]{2,1,0:T(8,128)} %param.7) | copy-start | bytes 393220
  2.6 9.4 %collective-permute-start.3 = (f32[10,4,1024]{2,1,0:T(4,128)}, f32[10,4,1024]{2,1,0:T(4,128)S(1)}, u32[]{:S(2)}, u32[]{:S(2)}) collective-permute-start(f32[10,4,1024]{2,1,0:T(4,128)} %get-tuple-element.18), channel_id=1, source_target_pairs={{0,7},{1,0},{2,1},{3,2},{4,3},{5,4},{6,5},{7,6},{8,15},{9,8},{10,9... | collective-permute-start | bytes 491528 | tf_op jit(solution)/shard_map/ppermute | solution.py:198
  6.0 6.1 %collective-permute-start.4 = (f32[10,4,1024]{2,1,0:T(4,128)}, f32[10,4,1024]{2,1,0:T(4,128)S(1)}, u32[]{:S(2)}, u32[]{:S(2)}) collective-permute-start(f32[10,4,1024]{2,1,0:T(4,128)} %get-tuple-element.19), channel_id=1, source_target_pairs={{0,1},{1,2},{2,3},{3,4},{4,5},{5,6},{6,7},{7,0},{8,9},{9,10},{10,1... | collective-permute-start | bytes 491528 | tf_op jit(solution)/shard_map/ppermute | solution.py:199
  9.9 15.2 %collective-permute-start.1 = (f32[8,16,1024]{2,1,0:T(8,128)S(1)}, f32[8,16,1024]{2,1,0:T(8,128)}, u32[]{:S(2)}, u32[]{:S(2)}) collective-permute-start(f32[8,16,1024]{2,1,0:T(8,128)S(1)} %get-tuple-element.16), channel_id=1, source_target_pairs={{0,8},{8,16},{16,24},{24,32},{32,40},{40,48},{48,56},{56,64},{64,7... | collective-permute-start | bytes 1572872 | tf_op jit(solution)/shard_map/ppermute | solution.py:210
  12.1 17.1 %collective-permute-start.6 = (f32[8,16,1024]{2,1,0:T(8,128)S(1)}, f32[8,16,1024]{2,1,0:T(8,128)S(1)}, u32[]{:S(2)}, u32[]{:S(2)}) collective-permute-start(f32[8,16,1024]{2,1,0:T(8,128)S(1)} %get-tuple-element.23), channel_id=1, source_target_pairs={{0,7},{1,0},{2,1},{3,2},{4,3},{5,4},{6,5},{7,6},{8,15},{9,8},{10,9... | collective-permute-start | bytes 1572872 | tf_op jit(solution)/shard_map/ppermute | solution.py:209
  18.3 10.8 %collective-permute-start = (s32[1]{0:T(128)}, s32[1]{0:T(128)}, u32[]{:S(2)}, u32[]{:S(2)}) collective-permute-start(s32[1]{0:T(128)} %param.9), channel_id=1, source_target_pairs={{0,8},{8,16},{16,24},{24,32},{32,40},{40,48},{48,56},{56,64},{64,7... | collective-permute-start | bytes 20 | tf_op jit(solution)/shard_map/ppermute | solution.py:200
  22.2 27.8 %collective-permute-start.5 = (f32[8,16,1024]{2,1,0:T(8,128)S(1)}, f32[8,16,1024]{2,1,0:T(8,128)S(1)}, u32[]{:S(2)}, u32[]{:S(2)}) collective-permute-start(f32[8,16,1024]{2,1,0:T(8,128)S(1)} %shard_map.70), channel_id=1, source_target_pairs={{0,8},{8,16},{16,24},{24,32},{32,40},{40,48},{48,56},{56,64},{64,7... | collective-permute-start | bytes 1572872 | tf_op jit(solution)/shard_map/ppermute | solution.py:219
  25.1 13.4 %collective-permute-start.2 = (f32[8,16,1024]{2,1,0:T(8,128)}, f32[8,16,1024]{2,1,0:T(8,128)S(1)}, u32[]{:S(2)}, u32[]{:S(2)}) collective-permute-start(f32[8,16,1024]{2,1,0:T(8,128)} %collective-permute-done.1), channel_id=1, source_target_pairs={{0,128},{128,0},{1,129},{129,1},{2,130},{130,2},{3,131},{131,3},{4... | collective-permute-start | bytes 1572872 | tf_op jit(solution)/shard_map/ppermute | solution.py:222
  38.6 26.7 %collective-permute-start.7 = (f32[8,8,1024]{2,1,0:T(8,128)S(1)}, f32[8,8,1024]{2,1,0:T(8,128)S(1)}, u32[]{:S(2)}, u32[]{:S(2)}) collective-permute-start(f32[8,8,1024]{2,1,0:T(8,128)S(1)} %slice.8), channel_id=1, source_target_pairs={{0,1},{1,2},{2,3},{3,4},{4,5},{5,6},{6,7},{7,0},{8,9},{9,10},{10,1... | collective-permute-start | bytes 786440 | tf_op jit(solution)/shard_map/ppermute | solution.py:224
  50.1 15.3 %collective-permute-start.8 = (f32[8,8,1024]{2,1,0:T(8,128)S(1)}, f32[8,8,1024]{2,1,0:T(8,128)S(1)}, u32[]{:S(2)}, u32[]{:S(2)}) collective-permute-start(f32[8,8,1024]{2,1,0:T(8,128)S(1)} %slice.7), channel_id=1, source_target_pairs={{0,1},{1,2},{2,3},{3,4},{4,5},{5,6},{6,7},{7,0},{8,9},{9,10},{10,1... | collective-permute-start | bytes 786440 | tf_op jit(solution)/shard_map/ppermute | solution.py:226
  53.2 25.0 %all-to-all-start = ((f32[256,1,64]{2,1,0:T(1,128)}), f32[256,1,64]{2,1,0:T(1,128)S(1)}, u32[]{:S(2)}, u32[]{:S(2)}) async-start(f32[256,1,64]{2,1,0:T(1,128)} %bitcast.4), calls=%async_computation | async-start | bytes 262144 | tf_op jit(solution)/shard_map/all_to_all | solution.py:228

commit v11 on v10

--- a/solution.py
+++ b/solution.py
@@ -130,18 +130,31 @@
         shifted_ref[b] = pltpu.roll(joined, by, 0)[:rows]
 
 
-def gram_kernel(shifted_ref, mid_ref, edge_ref, own_ref, gram_ref):
-    vectors, rows, cols = shifted_ref.shape
+def gram_kernel(
+    drift_ref, k_ref, shifted_ref, mid_ref, edge_ref, upper_ref, own_ref, gram_ref, before_ref
+):
+    vectors, rows, cols = k_ref.shape
+    drift = drift_ref[0]
     blocks = rows // TILE
-
-    def arrived(c, block, lane):
+    row = lax.broadcasted_iota(jnp.int32, (DRIFT, cols), 0)
+    for b in range(vectors):
+        before_ref[b] = jnp.where(row < drift, pltpu.roll(upper_ref[b], lax.rem(drift, DRIFT), 0), 0.0)
+
+    def left(a, block, lane):
+        if block < blocks:
+            return tile_of(shifted_ref, a, block, lane)
+        return tile_of(k_ref, a, block - blocks, lane)
+
+    def right(c, block, lane):
         if block == 0:
             return tile_of(edge_ref, c, 1, lane)
+        if block < blocks - 1:
+            return tile_of(mid_ref, c, block - 1, lane)
         if block == blocks - 1:
             return tile_of(edge_ref, c, 0, lane)
-        return tile_of(mid_ref, c, block - 1, lane)
-
-    table = own_ref[...] - pair_sums(functools.partial(tile_of, shifted_ref), arrived, blocks, vectors, cols)
+        return tile_of(before_ref, c, block - blocks, lane)
+
+    table = own_ref[...] - pair_sums(left, right, blocks + DRIFT // TILE, vectors, cols)
     ones = jnp.ones((gram_ref.shape[0], 128), jnp.float32)
     gram_ref[...] = lax.dot_general(
         ones, table, (((1,), (1,)), ((), ())),
@@ -149,13 +162,13 @@
     )
 
 
-def last_kernel(drift_ref, k_ref, mid_ref, edge_ref, rim_mid_ref, rim_hi_ref, product_ref):
+def last_kernel(drift_ref, k_ref, mid_ref, edge_ref, rim_mid_ref, rim_hi_ref, upper_ref, product_ref):
     vectors, rows, _ = k_ref.shape
     total = DRIFT + rows
     by = lax.rem(drift_ref[0] + (total - DRIFT), total)
     for b in range(vectors):
         joined = jnp.concatenate(
-            [rim_mid_ref[b], rim_hi_ref[b], edge_ref[b, TILE:], mid_ref[b], edge_ref[b, :TILE]], axis=0
+            [rim_mid_ref[b] + upper_ref[b, :TILE], rim_hi_ref[b] + upper_ref[b, TILE:], edge_ref[b, TILE:], mid_ref[b], edge_ref[b, :TILE]], axis=0
         )
         product_ref[b] = k_ref[b] - pltpu.roll(joined, by, 0)[:rows]
 
@@ -176,15 +189,26 @@
     )
 
 
+def rim_pairs(segs, strips, direct):
+    pairs = []
+    for s in range(segs):
+        for g in range(strips):
+            busy = (s + 1) % (segs // 2) == 0 and g % 2 == 1
+            if busy == direct:
+                pairs.append(((s - direct) * strips + g, s * strips + (g + 1) % strips))
+    return pairs
+
+
 def body(krylov, advect_x, advect_y, step_counts, drifts):
     k, ax, ay = krylov[0], advect_x[0], advect_y[0]
     vectors, rows, cols = k.shape
     segs, strips = lax.axis_size("seg"), lax.axis_size("gx")
     world, pairs = segs * strips, vectors * vectors
-    half = segs // 2
     onward = functools.partial(lax.ppermute, axis_name="seg", perm=shift_pairs(segs, 1))
-    sideways = functools.partial(lax.ppermute, axis_name="gx", perm=shift_pairs(strips, 1))
-    backward = functools.partial(lax.ppermute, axis_name="gx", perm=shift_pairs(strips, -1))
+    along = rim_pairs(segs, strips, False)
+    sideways = functools.partial(lax.ppermute, axis_name=("seg", "gx"), perm=along)
+    backward = functools.partial(lax.ppermute, axis_name=("seg", "gx"), perm=[(b, a) for a, b in along])
+    ahead = functools.partial(lax.ppermute, axis_name=("seg", "gx"), perm=rim_pairs(segs, strips, True))
 
     fields = vectors + 2
     head, tail = call(
@@ -195,8 +219,8 @@
         1,
         limit=FULL,
     )(k, ax, ay)
-    right = backward(head)
-    left = sideways(tail)
+    right = lax.ppermute(head, "gx", shift_pairs(strips, -1))
+    left = lax.ppermute(tail, "gx", shift_pairs(strips, 1))
     drift = onward(drifts)
     mid, beyond = call(
         inner_kernel,
@@ -207,7 +231,8 @@
     )(step_counts, k, ax, ay)
     beyond, right, left = lax.optimization_barrier((beyond, right, left))
     beyond = backward(beyond)
-    mid = lax.ppermute(mid, "seg", [(s, s // half * half + (s + 1) % half) for s in range(segs)])
+    inner = mid[:, -(DRIFT - TILE) :]
+    mid = onward(mid)
     (edge,) = call(
         outer_kernel,
         [(vectors, 2 * TILE, cols)],
@@ -215,19 +240,19 @@
         [buffer(vectors, 5 * TILE, cols), buffer(4, 5 * TILE, cols)],
         1,
     )(step_counts, k, ax, ay, left, right)
-    sent, kept = lax.optimization_barrier((edge, k))
+    kept, outer = lax.optimization_barrier((k, edge))
     edge = onward(edge)
+    upper = ahead(jnp.concatenate([inner, outer[:, :TILE]], axis=1))
     own, shifted = call(own_kernel, [(pairs, 128), k.shape], [SMEM, VMEM, VMEM], [], 16)(drift, kept, beyond)
-    held, _ = lax.optimization_barrier((mid, sent))
-    crossed = lax.ppermute(held, "seg", [(0, half), (half, 0)])
-    mid = jnp.where(lax.axis_index("seg") % half == 0, crossed, mid)
     rim_mid = sideways(mid[:, -(DRIFT - TILE) :])
     edge, own, _ = lax.optimization_barrier((edge, own, mid))
     rim_hi = sideways(edge[:, :TILE])
-    (gram,) = call(gram_kernel, [(world, pairs)], [VMEM] * 4, [], 1)(shifted, mid, edge, own)
+    (gram,) = call(
+        gram_kernel, [(world, pairs)], [SMEM] + [VMEM] * 6, [buffer(vectors, DRIFT, cols)], 1
+    )(drift, k, shifted, mid, edge, upper, own)
     gram = lax.all_to_all(gram, ("seg", "gx"), 0, 0)
-    (product,) = call(last_kernel, [k.shape], [SMEM] + [VMEM] * 5, [], 1)(
-        drift, k, mid, edge, rim_mid, rim_hi
+    (product,) = call(last_kernel, [k.shape], [SMEM] + [VMEM] * 6, [], 1)(
+        drift, k, mid, edge, rim_mid, rim_hi, upper
     )
     product, gram = lax.optimization_barrier((product, gram))
     cells = world * rows * cols

time: 78.5 us -> 71.9 us (0.916); the launches traced: 79 us -> 70.8 us
  starting transfers between devices: 41.6 us -> 30.6 us
  Pallas kernels: 11.1 us -> 12.2 us
  waiting for transfers between devices: 24.1 us -> 25 us
    ppermute x1, waiting for transfers between devices: 0.01 us -> 8.92 us  [body(): edge = onward(edge)]
    ppermute x1, starting transfers between devices: 11.4 us -> 2.81 us  [body(): rim_mid = sideways(mid[:, -(DRIFT - TILE):])]
    ppermute x4, waiting for transfers between devices: 13 us -> 5.15 us  [the longest x1 3.13 us: body(): mid = onward(mid)]
    ppermute x4, starting transfers between devices: 8.69 us -> 5.37 us  [the longest x1 3.32 us: body(): right = lax.ppermute(head, 'gx', shift_pairs(strips, -1))]
    ppermute x1, starting transfers between devices: 6.27 us -> 8.16 us  [body(): beyond = backward(beyond)]
    all_to_all x1, starting transfers between devices: 12.1 us -> 10.8 us  [body(): gram = lax.all_to_all(gram, ('seg', 'gx'), 0, 0)]
    pallas_call x2, Pallas kernels: 3.31 us -> 4.38 us  [the longest x1 2.47 us: body(): call(gram_kernel, [(world, pairs)], [SMEM] + [VMEM] * 6, [buffer(vectors,...]
  transfers between devices with their start and end apart: 10 -> 10, of which waited for: 4 -> 4; matrix products, arithmetic and copies ran while one was open for 0% -> 1% of each run, Pallas kernels for 12% -> 14%
where the time goes in v11:
time: 71.9 us; the launch traced here: 70.8 us
  starting transfers between devices  30.6 us (43%)
  waiting for transfers between devices  25 us (35%)
  Pallas kernels  12.2 us (17%)
  between operations  1.47 us (2%)
  local copies, waits for them, and re-layouts  1.46 us (2%)
    all_to_all x1, waiting for transfers between devices, body(): gram = lax.all_to_all(gram, ('seg', 'gx'), 0, 0)  10.9 us
    all_to_all x1, starting transfers between devices, body(): gram = lax.all_to_all(gram, ('seg', 'gx'), 0, 0)  10.8 us
    ppermute x1, waiting for transfers between devices, body(): edge = onward(edge)  8.92 us
    ppermute x1, starting transfers between devices, body(): beyond = backward(beyond)  8.16 us
    ppermute x1, starting transfers between devices, body(): right = lax.ppermute(head, 'gx', shift_pairs(strips, -1))  3.32 us
    ppermute x1, waiting for transfers between devices, body(): mid = onward(mid)  3.13 us
    ppermute x1, starting transfers between devices, body(): rim_mid = sideways(mid[:, -(DRIFT - TILE):])  2.81 us
    pallas_call x1, Pallas kernels, body(): call(outer_kernel, [(vectors, 2 * TILE, cols)], [SMEM] + [VMEM] * 5, [buf...  2.6 us
  transfers between devices with their start and end apart: 10, of which 4 were waited for; matrix products, arithmetic and copies ran while one was open for 1% of the time, Pallas kernels for 14%

profile of v11, /device:TPU:1, one launch (start us, length us, event | category | flops | bytes accessed | tf_op | source)
XLA Modules:
  0.0 70.8 jit_solution(392829517262814456)
XLA Ops:
  0.7 2.0 %shard_map.69 = (f32[10,4,1024]{2,1,0:T(4,128)}, f32[10,4,1024]{2,1,0:T(4,128)}) custom-call(f32[8,32,1024]{2,1,0:T(8,128)} %bitcast.8, f32[32,1024]{1,0:T(8,128)} %bitcast.14, f32[32,1024]{1,0:T(8,128)} %bitcast.17), custom_call_target="tpu_custom_call" | custom-call | flops 1073741824 | bytes 4194304 | tf_op jit(solution)/shard_map/pallas_call | solution.py:214
  2.6 3.3 %collective-permute-start.2 = (f32[10,4,1024]{2,1,0:T(4,128)}, f32[10,4,1024]{2,1,0:T(4,128)S(1)}, u32[]{:S(2)}, u32[]{:S(2)}) collective-permute-start(f32[10,4,1024]{2,1,0:T(4,128)} %get-tuple-element.19), channel_id=1, source_target_pairs={{0,7},{1,0},{2,1},{3,2},{4,3},{5,4},{6,5},{7,6},{8,15},{9,8},{10,9... | collective-permute-start | bytes 491528 | tf_op jit(solution)/shard_map/ppermute | solution.py:222
  5.9 1.2 %collective-permute-start.3 = (f32[10,4,1024]{2,1,0:T(4,128)}, f32[10,4,1024]{2,1,0:T(4,128)S(1)}, u32[]{:S(2)}, u32[]{:S(2)}) collective-permute-start(f32[10,4,1024]{2,1,0:T(4,128)} %get-tuple-element.20), channel_id=1, source_target_pairs={{0,1},{1,2},{2,3},{3,4},{4,5},{5,6},{6,7},{7,0},{8,9},{9,10},{10,1... | collective-permute-start | bytes 491528 | tf_op jit(solution)/shard_map/ppermute | solution.py:223
  7.9 2.0 %shard_map.68 = (f32[8,16,1024]{2,1,0:T(8,128)S(1)}, f32[8,16,1024]{2,1,0:T(8,128)S(1)}) custom-call(s32[1]{0:T(128)S(6)} %copy.8.count_ref, f32[8,32,1024]{2,1,0:T(8,128)S(1)} %bitcast.9, f32[32,1024]{1,0:T(8,128)S(1)} %bitcast.15, f32[32,1024]{1,0:T(8,128)S(1)} %bitcast.18), custom_call_target="tpu_custom_call" | custom-call | flops 68719476736 | bytes 4194304 | tf_op jit(solution)/shard_map/pallas_call | solution.py:225
  9.9 0.1 collective-permute-start.1
  10.0 2.0 %collective-permute-done.2.right_ref = f32[10,4,1024]{2,1,0:T(4,128)S(1)} collective-permute-done((f32[10,4,1024]{2,1,0:T(4,128)}, f32[10,4,1024]{2,1,0:T(4,128)S(1)}, u32[]{:S(2)}, u32[]{:S(2)}) %collective-permute-start.2) | collective-permute-done | bytes 163872 | tf_op jit(solution)/shard_map/ppermute | solution.py:222
  12.1 8.2 %collective-permute-start.5 = (f32[8,16,1024]{2,1,0:T(8,128)S(1)}, f32[8,16,1024]{2,1,0:T(8,128)S(1)}, u32[]{:S(2)}, u32[]{:S(2)}) collective-permute-start(f32[8,16,1024]{2,1,0:T(8,128)S(1)} %get-tuple-element.24), channel_id=1, source_target_pairs={{1,0},{2,1},{3,2},{4,3},{5,4},{6,5},{7,6},{0,7},{9,8},{10,9},{11,1... | collective-permute-start | bytes 1572872 | tf_op jit(solution)/shard_map/ppermute | solution.py:233
  20.2 1.4 %collective-permute-start = (s32[1]{0:T(128)}, s32[1]{0:T(128)}, u32[]{:S(2)}, u32[]{:S(2)}) collective-permute-start(s32[1]{0:T(128)} %param.9), channel_id=1, source_target_pairs={{0,8},{8,16},{16,24},{24,32},{32,40},{40,48},{48,56},{56,64},{64,7... | collective-permute-start | bytes 20 | tf_op jit(solution)/shard_map/ppermute | solution.py:224
  21.6 2.6 %shard_map.70 = f32[8,16,1024]{2,1,0:T(8,128)S(1)} custom-call(s32[1]{0:T(128)S(6)} %copy.8.count_ref, f32[8,32,1024]{2,1,0:T(8,128)S(1)} %bitcast.10, f32[32,1024]{1,0:T(8,128)S(1)} %bitcast.16, f32[32,1024]{1,0:T(8,128)S(1)} %bitcast.19, f32[10,4,1024]{2,1,0:T(4,128)S(1)} %collective-permute-done.3.left_ref, ...), custom_call_target="tpu_custom_call" | custom-call | flops 1073741824 | bytes 4194304 | tf_op jit(solution)/shard_map/pallas_call | solution.py:236
  24.2 0.1 collective-permute-start.4
  24.3 0.1 pad_maximum_fusion
  24.4 0.7 collective-permute-start.8
  25.1 3.1 %collective-permute-done.1.mid_ref = f32[8,16,1024]{2,1,0:T(8,128)S(1)} collective-permute-done((f32[8,16,1024]{2,1,0:T(8,128)S(1)}, f32[8,16,1024]{2,1,0:T(8,128)S(1)}, u32[]{:S(2)}, u32[]{:S(2)}) %collective-permute-start.1) | collective-permute-done | bytes 524320 | tf_op jit(solution)/shard_map/ppermute | solution.py:235
  28.2 2.8 %collective-permute-start.6 = (f32[8,8,1024]{2,1,0:T(8,128)S(1)}, f32[8,8,1024]{2,1,0:T(8,128)S(1)}, u32[]{:S(2)}, u32[]{:S(2)}) collective-permute-start(f32[8,8,1024]{2,1,0:T(8,128)S(1)} %slice.16), channel_id=1, source_target_pairs={{0,1},{1,2},{2,3},{3,4},{4,5},{5,6},{6,7},{7,0},{8,9},{9,10},{10,1... | collective-permute-start | bytes 786440 | tf_op jit(solution)/shard_map/ppermute | solution.py:247
  31.1 1.2 %shard_map.71 = (f32[64,128]{1,0:T(8,128)S(1)}, f32[8,32,1024]{2,1,0:T(8,128)S(1)}) custom-call(s32[1]{0:T(128)} %collective-permute-done.drift_ref, f32[8,32,1024]{2,1,0:T(8,128)S(1)} %bitcast.11, f32[8,16,1024]{2,1,0:T(8,128)S(1)} %collective-permute-done.5.beyond_ref), custom_call_target="tpu_custom_call" | custom-call | flops 17179869184 | bytes 4194304 | tf_op jit(solution)/shard_map/pallas_call | solution.py:246
  32.3 8.9 %collective-permute-done.4.edge_ref = f32[8,16,1024]{2,1,0:T(8,128)S(1)} collective-permute-done((f32[8,16,1024]{2,1,0:T(8,128)S(1)}, f32[8,16,1024]{2,1,0:T(8,128)S(1)}, u32[]{:S(2)}, u32[]{:S(2)}) %collective-permute-start.4) | collective-permute-done | bytes 524320 | tf_op jit(solution)/shard_map/ppermute | solution.py:244
  41.3 0.7 %slice.13 = f32[8,8,1024]{2,1,0:T(8,128)} slice(f32[8,16,1024]{2,1,0:T(8,128)S(1)} %collective-permute-done.4.edge_ref), slice={[0:8], [0:8], [0:1024]} | slice | bytes 524288 | tf_op jit(solution)/shard_map/slice | solution.py:249
  42.0 1.9 %collective-permute-start.7 = (f32[8,8,1024]{2,1,0:T(8,128)}, f32[8,8,1024]{2,1,0:T(8,128)S(1)}, u32[]{:S(2)}, u32[]{:S(2)}) collective-permute-start(f32[8,8,1024]{2,1,0:T(8,128)} %slice.13), channel_id=1, source_target_pairs={{0,1},{1,2},{2,3},{3,4},{4,5},{5,6},{6,7},{7,0},{8,9},{9,10},{10,1... | collective-permute-start | bytes 786440 | tf_op jit(solution)/shard_map/ppermute | solution.py:249
  43.9 2.5 %shard_map.73 = f32[256,64]{1,0:T(8,128)} custom-call(s32[1]{0:T(128)} %collective-permute-done.drift_ref, f32[8,32,1024]{2,1,0:T(8,128)S(1)} %bitcast.12, f32[8,32,1024]{2,1,0:T(8,128)S(1)} %get-tuple-element.28.shifted_ref, f32[8,16,1024]{2,1,0:T(8,128)S(1)} %collective-permute-done.1.mid_ref, f32[8,16,1024]{2,1,0:T(8,128)S(1)} %collective-permute-done.4.edge_ref, ...), custom_call_target="tpu_custom_call" | custom-call | flops 1073741824 | bytes 4194304 | tf_op jit(solution)/shard_map/pallas_call | solution.py:250
  46.4 10.8 %all-to-all-start = ((f32[256,1,64]{2,1,0:T(1,128)}), f32[256,1,64]{2,1,0:T(1,128)S(1)}, u32[]{:S(2)}, u32[]{:S(2)}) async-start(f32[256,1,64]{2,1,0:T(1,128)} %bitcast.4), calls=%async_computation | async-start | bytes 262144 | tf_op jit(solution)/shard_map/all_to_all | solution.py:253
  57.2 1.9 %shard_map.72 = f32[8,32,1024]{2,1,0:T(8,128)} custom-call(s32[1]{0:T(128)} %collective-permute-done.drift_ref, f32[8,32,1024]{2,1,0:T(8,128)S(1)} %bitcast.13, f32[8,16,1024]{2,1,0:T(8,128)S(1)} %collective-permute-done.1.mid_ref, f32[8,16,1024]{2,1,0:T(8,128)S(1)} %collective-permute-done.4.edge_ref, f32[8,8,1024]{2,1,0:T(8,128)S(1)} %collective-permute-done.6.rim_mid_ref, ...), custom_call_target="tpu_custom_call" | custom-call | flops 1073741824 | bytes 4194304 | tf_op jit(solution)/shard_map/pallas_call | solution.py:254
  59.2 10.9 %all-to-all-done = f32[256,1,64]{2,1,0:T(1,128)S(1)} async-done(((f32[256,1,64]{2,1,0:T(1,128)}), f32[256,1,64]{2,1,0:T(1,128)S(1)}, u32[]{:S(2)}, u32[]{:S(2)}) %all-to-all-start) | async-done | bytes 65568 | tf_op jit(solution)/shard_map/all_to_all | solution.py:253
  70.1 0.1 reduce_sum.9
  70.2 0.7 div.10
  (16 shorter events, 0.1 us)
Async XLA Ops:
  0.6 7.2 %copy-start = (f32[1,8,32,1024]{3,2,1,0:T(8,128)S(1)}, f32[1,8,32,1024]{3,2,1,0:T(8,128)}, u32[]{:S(2)}) copy-start(f32[1,8,32,1024]{3,2,1,0:T(8,128)} %param.5) | copy-start | bytes 3145732
  0.6 7.2 %copy-start.1 = (f32[1,32,1024]{2,1,0:T(8,128)S(1)}, f32[1,32,1024]{2,1,0:T(8,128)}, u32[]{:S(2)}) copy-start(f32[1,32,1024]{2,1,0:T(8,128)} %param.6) | copy-start | bytes 393220
  0.6 7.2 %copy-start.2 = (f32[1,32,1024]{2,1,0:T(8,128)S(1)}, f32[1,32,1024]{2,1,0:T(8,128)}, u32[]{:S(2)}) copy-start(f32[1,32,1024]{2,1,0:T(8,128)} %param.7) | copy-start | bytes 393220
  2.6 9.4 %collective-permute-start.2 = (f32[10,4,1024]{2,1,0:T(4,128)}, f32[10,4,1024]{2,1,0:T(4,128)S(1)}, u32[]{:S(2)}, u32[]{:S(2)}) collective-permute-start(f32[10,4,1024]{2,1,0:T(4,128)} %get-tuple-element.19), channel_id=1, source_target_pairs={{0,7},{1,0},{2,1},{3,2},{4,3},{5,4},{6,5},{7,6},{8,15},{9,8},{10,9... | collective-permute-start | bytes 491528 | tf_op jit(solution)/shard_map/ppermute | solution.py:222
  5.9 6.1 %collective-permute-start.3 = (f32[10,4,1024]{2,1,0:T(4,128)}, f32[10,4,1024]{2,1,0:T(4,128)S(1)}, u32[]{:S(2)}, u32[]{:S(2)}) collective-permute-start(f32[10,4,1024]{2,1,0:T(4,128)} %get-tuple-element.20), channel_id=1, source_target_pairs={{0,1},{1,2},{2,3},{3,4},{4,5},{5,6},{6,7},{7,0},{8,9},{9,10},{10,1... | collective-permute-start | bytes 491528 | tf_op jit(solution)/shard_map/ppermute | solution.py:223
  9.9 18.3 %collective-permute-start.1 = (f32[8,16,1024]{2,1,0:T(8,128)S(1)}, f32[8,16,1024]{2,1,0:T(8,128)S(1)}, u32[]{:S(2)}, u32[]{:S(2)}) collective-permute-start(f32[8,16,1024]{2,1,0:T(8,128)S(1)} %get-tuple-element.17), channel_id=1, source_target_pairs={{0,8},{8,16},{16,24},{24,32},{32,40},{40,48},{48,56},{56,64},{64,7... | collective-permute-start | bytes 1572872 | tf_op jit(solution)/shard_map/ppermute | solution.py:235
  12.1 19.0 %collective-permute-start.5 = (f32[8,16,1024]{2,1,0:T(8,128)S(1)}, f32[8,16,1024]{2,1,0:T(8,128)S(1)}, u32[]{:S(2)}, u32[]{:S(2)}) collective-permute-start(f32[8,16,1024]{2,1,0:T(8,128)S(1)} %get-tuple-element.24), channel_id=1, source_target_pairs={{1,0},{2,1},{3,2},{4,3},{5,4},{6,5},{7,6},{0,7},{9,8},{10,9},{11,1... | collective-permute-start | bytes 1572872 | tf_op jit(solution)/shard_map/ppermute | solution.py:233
  20.2 10.8 %collective-permute-start = (s32[1]{0:T(128)}, s32[1]{0:T(128)}, u32[]{:S(2)}, u32[]{:S(2)}) collective-permute-start(s32[1]{0:T(128)} %param.9), channel_id=1, source_target_pairs={{0,8},{8,16},{16,24},{24,32},{32,40},{40,48},{48,56},{56,64},{64,7... | collective-permute-start | bytes 20 | tf_op jit(solution)/shard_map/ppermute | solution.py:224
  24.2 17.0 %collective-permute-start.4 = (f32[8,16,1024]{2,1,0:T(8,128)S(1)}, f32[8,16,1024]{2,1,0:T(8,128)S(1)}, u32[]{:S(2)}, u32[]{:S(2)}) collective-permute-start(f32[8,16,1024]{2,1,0:T(8,128)S(1)} %shard_map.70), channel_id=1, source_target_pairs={{0,8},{8,16},{16,24},{24,32},{32,40},{40,48},{48,56},{56,64},{64,7... | collective-permute-start | bytes 1572872 | tf_op jit(solution)/shard_map/ppermute | solution.py:244
  24.4 19.5 %collective-permute-start.8 = (f32[8,16,1024]{2,1,0:T(8,128)S(1)}, f32[8,16,1024]{2,1,0:T(8,128)S(1)}, u32[]{:S(2)}, u32[]{:S(2)}) collective-permute-start(f32[8,16,1024]{2,1,0:T(8,128)S(1)} %pad_maximum_fusion), channel_id=1, source_target_pairs={{113,122},{115,124},{117,126},{119,120},{241,250},{243,252},{245,2... | collective-permute-start | bytes 1572872 | tf_op jit(solution)/shard_map/ppermute | solution.py:245
  28.2 29.0 %collective-permute-start.6 = (f32[8,8,1024]{2,1,0:T(8,128)S(1)}, f32[8,8,1024]{2,1,0:T(8,128)S(1)}, u32[]{:S(2)}, u32[]{:S(2)}) collective-permute-start(f32[8,8,1024]{2,1,0:T(8,128)S(1)} %slice.16), channel_id=1, source_target_pairs={{0,1},{1,2},{2,3},{3,4},{4,5},{5,6},{6,7},{7,0},{8,9},{9,10},{10,1... | collective-permute-start | bytes 786440 | tf_op jit(solution)/shard_map/ppermute | solution.py:247
  42.0 15.3 %collective-permute-start.7 = (f32[8,8,1024]{2,1,0:T(8,128)}, f32[8,8,1024]{2,1,0:T(8,128)S(1)}, u32[]{:S(2)}, u32[]{:S(2)}) collective-permute-start(f32[8,8,1024]{2,1,0:T(8,128)} %slice.13), channel_id=1, source_target_pairs={{0,1},{1,2},{2,3},{3,4},{4,5},{5,6},{6,7},{7,0},{8,9},{9,10},{10,1... | collective-permute-start | bytes 786440 | tf_op jit(solution)/shard_map/ppermute | solution.py:249
  46.4 23.7 %all-to-all-start = ((f32[256,1,64]{2,1,0:T(1,128)}), f32[256,1,64]{2,1,0:T(1,128)S(1)}, u32[]{:S(2)}, u32[]{:S(2)}) async-start(f32[256,1,64]{2,1,0:T(1,128)} %bitcast.4), calls=%async_computation | async-start | bytes 262144 | tf_op jit(solution)/shard_map/all_to_all | solution.py:253

commit v12 on v9

--- a/solution.py
+++ b/solution.py
@@ -190,7 +190,7 @@
     pairs = []
     for s in range(segs):
         for g in range(strips):
-            crosses = g % 2 == 1 and s != segs // 2
+            crosses = g % 2 == 1 and s % (segs // 2) != 0
             if crosses == direct:
                 pairs.append((((s - direct) % segs) * strips + g, s * strips + (g + 1) % strips))
     return pairs

time: 73.5 us -> 72.1 us (0.981)
  waiting for transfers between devices: 36.6 us -> 30.7 us
  Pallas kernels: 10.2 us -> 13.1 us
  starting transfers between devices: 24.2 us -> 25.8 us
    ppermute x1, starting transfers between devices: 1.28 us -> 5.74 us  [body(): rim = sideways(near)]
    ppermute x1, waiting for transfers between devices: 20.8 us -> 16.8 us  [body(): drift = onward(drifts)]
    ppermute x1, waiting for transfers between devices: 0.01 us -> 3.55 us  [body(): rim = sideways(near)]
    all_to_all x1, waiting for transfers between devices: 11 us -> 7.42 us  [body(): gram = lax.all_to_all(gram, ('seg', 'gx'), 0, 0)]
    ppermute x1, starting transfers between devices: 2.7 us -> 0.09 us  [body(): drift = onward(drifts)]
    ppermute x1, starting transfers between devices: 3.97 us -> 1.6 us  [body(): ahead(jnp.concatenate([mid[:, -(DRIFT - TILE):], edge[:, :TILE]], axis=1))]
    ppermute x1, waiting for transfers between devices: 4.76 us -> 2.89 us  [body(): right = lax.ppermute(head, 'gx', shift_pairs(strips, -1))]
    pallas_call x1, Pallas kernels: 2.16 us -> 3.77 us  [body(): call(outer_kernel, [(vectors, 2 * TILE, cols), (pairs, 128)], [SMEM] + [V...]
  transfers between devices with their start and end apart: 9 -> 9, of which waited for: 3 -> 4; matrix products, arithmetic and copies ran while one was open for 0% -> 0% of each run, Pallas kernels for 7% -> 12%
where the time goes in v12:
time: 72.1 us; the launch traced here: 71.9 us
  waiting for transfers between devices  30.7 us (43%)
  starting transfers between devices  25.8 us (36%)
  Pallas kernels  13.1 us (18%)
  between operations  1.43 us (2%)
    ppermute x1, waiting for transfers between devices, body(): drift = onward(drifts)  16.8 us
    all_to_all x1, starting transfers between devices, body(): gram = lax.all_to_all(gram, ('seg', 'gx'), 0, 0)  9.28 us
    all_to_all x1, waiting for transfers between devices, body(): gram = lax.all_to_all(gram, ('seg', 'gx'), 0, 0)  7.42 us
    ppermute x1, starting transfers between devices, body(): rim = sideways(near)  5.74 us
    ppermute x1, starting transfers between devices, body(): left = lax.ppermute(tail, 'gx', shift_pairs(strips, 1))  4.46 us
    pallas_call x1, Pallas kernels, body(): call(outer_kernel, [(vectors, 2 * TILE, cols), (pairs, 128)], [SMEM] + [V...  3.77 us
    ppermute x1, waiting for transfers between devices, body(): rim = sideways(near)  3.55 us
    ppermute x1, waiting for transfers between devices, body(): right = lax.ppermute(head, 'gx', shift_pairs(strips, -1))  2.89 us
  transfers between devices with their start and end apart: 9, of which 4 were waited for; matrix products, arithmetic and copies ran while one was open for 0% of the time, Pallas kernels for 12%

profile of v12, /device:TPU:1, one launch (start us, length us, event | category | flops | bytes accessed | tf_op | source)
XLA Modules:
  0.0 71.9 jit_solution(15813036018832260006)
XLA Ops:
  0.7 2.0 %shard_map.69 = (f32[10,4,1024]{2,1,0:T(4,128)}, f32[10,4,1024]{2,1,0:T(4,128)}) custom-call(f32[8,32,1024]{2,1,0:T(8,128)} %bitcast.8, f32[32,1024]{1,0:T(8,128)} %bitcast.13, f32[32,1024]{1,0:T(8,128)} %bitcast.16), custom_call_target="tpu_custom_call" | custom-call | flops 1073741824 | bytes 1048576 | tf_op jit(solution)/shard_map/pallas_call | solution.py:211
  2.6 4.5 %collective-permute-start.2 = (f32[10,4,1024]{2,1,0:T(4,128)}, f32[10,4,1024]{2,1,0:T(4,128)S(1)}, u32[]{:S(2)}, u32[]{:S(2)}) collective-permute-start(f32[10,4,1024]{2,1,0:T(4,128)} %get-tuple-element.14), channel_id=1, source_target_pairs={{0,1},{1,2},{2,3},{3,4},{4,5},{5,6},{6,7},{7,0},{8,9},{9,10},{10,1... | collective-permute-start | bytes 491528 | tf_op jit(solution)/shard_map/ppermute | solution.py:220
  7.8 2.7 %shard_map.68 = (f32[8,16,1024]{2,1,0:T(8,128)S(1)}, f32[8,16,1024]{2,1,0:T(8,128)S(1)}) custom-call(s32[1]{0:T(128)S(6)} %copy.8.count_ref, f32[8,32,1024]{2,1,0:T(8,128)S(1)} %bitcast.9, f32[32,1024]{1,0:T(8,128)S(1)} %bitcast.14, f32[32,1024]{1,0:T(8,128)S(1)} %bitcast.17), custom_call_target="tpu_custom_call" | custom-call | flops 68719476736 | bytes 67108864 | tf_op jit(solution)/shard_map/pallas_call | solution.py:221
  10.4 1.4 %collective-permute-start.1 = (f32[8,16,1024]{2,1,0:T(8,128)S(1)}, f32[8,16,1024]{2,1,0:T(8,128)S(1)}, u32[]{:S(2)}, u32[]{:S(2)}) collective-permute-start(f32[8,16,1024]{2,1,0:T(8,128)S(1)} %get-tuple-element.13), channel_id=1, source_target_pairs={{0,8},{8,16},{16,24},{24,32},{32,40},{40,48},{48,56},{56,64},{64,7... | collective-permute-start | bytes 1572872 | tf_op jit(solution)/shard_map/ppermute | solution.py:239
  11.8 0.0 collective-permute-done.2.left_ref
  11.8 2.9 %collective-permute-done.3.right_ref = f32[10,4,1024]{2,1,0:T(4,128)S(1)} collective-permute-done((f32[10,4,1024]{2,1,0:T(4,128)}, f32[10,4,1024]{2,1,0:T(4,128)S(1)}, u32[]{:S(2)}, u32[]{:S(2)}) %collective-permute-start.3) | collective-permute-done | bytes 163872 | tf_op jit(solution)/shard_map/ppermute | solution.py:219
  14.7 3.8 %shard_map.70 = (f32[8,16,1024]{2,1,0:T(8,128)S(1)}, f32[64,128]{1,0:T(8,128)S(1)}) custom-call(s32[1]{0:T(128)S(6)} %copy.8.count_ref, f32[8,32,1024]{2,1,0:T(8,128)S(1)} %bitcast.10, f32[32,1024]{1,0:T(8,128)S(1)} %bitcast.15, f32[32,1024]{1,0:T(8,128)S(1)} %bitcast.18, f32[10,4,1024]{2,1,0:T(4,128)S(1)} %collective-permute-done.2.left_ref, ...), custom_call_target="tpu_custom_call" | custom-call | tf_op jit(solution)/shard_map/pallas_call | solution.py:229
  18.5 1.4 %collective-permute-start.4 = (f32[8,16,1024]{2,1,0:T(8,128)S(1)}, f32[8,16,1024]{2,1,0:T(8,128)S(1)}, u32[]{:S(2)}, u32[]{:S(2)}) collective-permute-start(f32[8,16,1024]{2,1,0:T(8,128)S(1)} %get-tuple-element.16), channel_id=1, source_target_pairs={{0,8},{8,16},{16,24},{24,32},{32,40},{40,48},{48,56},{56,64},{64,7... | collective-permute-start | bytes 1572872 | tf_op jit(solution)/shard_map/ppermute | solution.py:240
  20.0 1.6 %collective-permute-start.6 = (f32[8,16,1024]{2,1,0:T(8,128)S(1)}, f32[8,16,1024]{2,1,0:T(8,128)S(1)}, u32[]{:S(2)}, u32[]{:S(2)}) collective-permute-start(f32[8,16,1024]{2,1,0:T(8,128)S(1)} %pad_maximum_fusion), channel_id=1, source_target_pairs={{1,10},{3,12},{5,14},{7,8},{9,18},{11,20},{13,22},{15,16},{17,26},... | collective-permute-start | bytes 1572872 | tf_op jit(solution)/shard_map/ppermute | solution.py:236
  21.6 1.9 %collective-permute-start.5 = (f32[8,16,1024]{2,1,0:T(8,128)S(1)}, f32[8,16,1024]{2,1,0:T(8,128)S(1)}, u32[]{:S(2)}, u32[]{:S(2)}) collective-permute-start(f32[8,16,1024]{2,1,0:T(8,128)S(1)} %get-tuple-element.18), channel_id=1, source_target_pairs={{1,0},{2,1},{3,2},{4,3},{5,4},{6,5},{7,6},{0,7},{9,8},{11,10},{13,... | collective-permute-start | bytes 1572872 | tf_op jit(solution)/shard_map/ppermute | solution.py:238
  23.5 0.1 collective-permute-start
  23.6 16.8 %collective-permute-done.drift_ref = s32[1]{0:T(128)} collective-permute-done((s32[1]{0:T(128)}, s32[1]{0:T(128)}, u32[]{:S(2)}, u32[]{:S(2)}) %collective-permute-start) | collective-permute-done | bytes 36 | tf_op jit(solution)/shard_map/ppermute | solution.py:228
  40.4 0.0 collective-permute-done.1.mid_ref
  40.4 0.0 collective-permute-done.4.edge_ref
  40.4 0.0 collective-permute-done.6.upper_ref
  40.4 0.0 collective-permute-done.5.beyond_ref
  40.4 2.8 %shard_map.71 = (f32[256,64]{1,0:T(8,128)}, f32[8,16,1024]{2,1,0:T(8,128)}) custom-call(s32[1]{0:T(128)} %collective-permute-done.drift_ref, f32[8,32,1024]{2,1,0:T(8,128)S(1)} %bitcast.11, f32[8,16,1024]{2,1,0:T(8,128)S(1)} %collective-permute-done.5.beyond_ref, f32[8,16,1024]{2,1,0:T(8,128)S(1)} %collective-permute-done.1.mid_ref, ...), custom_call_target="tpu_custom_call" | custom-call | flops 1073741824 | bytes 1048576 | tf_op jit(solution)/shard_map/pallas_call | solution.py:241
  43.2 5.7 %collective-permute-start.7 = (f32[8,16,1024]{2,1,0:T(8,128)}, f32[8,16,1024]{2,1,0:T(8,128)S(1)}, u32[]{:S(2)}, u32[]{:S(2)}) collective-permute-start(f32[8,16,1024]{2,1,0:T(8,128)} %get-tuple-element.20), channel_id=1, source_target_pairs={{0,1},{1,2},{2,3},{3,4},{4,5},{5,6},{6,7},{7,0},{8,9},{10,11},{12,... | collective-permute-start | bytes 1572872 | tf_op jit(solution)/shard_map/ppermute | solution.py:248
  48.9 9.3 %all-to-all-start = ((f32[256,1,64]{2,1,0:T(1,128)}), f32[256,1,64]{2,1,0:T(1,128)S(1)}, u32[]{:S(2)}, u32[]{:S(2)}) async-start(f32[256,1,64]{2,1,0:T(1,128)} %bitcast.4), calls=%async_computation | async-start | bytes 262144 | tf_op jit(solution)/shard_map/all_to_all | solution.py:249
  58.2 3.6 %collective-permute-done.7.rim_ref = f32[8,16,1024]{2,1,0:T(8,128)S(1)} collective-permute-done((f32[8,16,1024]{2,1,0:T(8,128)}, f32[8,16,1024]{2,1,0:T(8,128)S(1)}, u32[]{:S(2)}, u32[]{:S(2)}) %collective-permute-start.7) | collective-permute-done | bytes 524320 | tf_op jit(solution)/shard_map/ppermute | solution.py:248
  61.8 1.9 %shard_map.72 = f32[8,32,1024]{2,1,0:T(8,128)} custom-call(s32[1]{0:T(128)} %collective-permute-done.drift_ref, f32[8,32,1024]{2,1,0:T(8,128)S(1)} %bitcast.12, f32[8,16,1024]{2,1,0:T(8,128)S(1)} %collective-permute-done.1.mid_ref, f32[8,16,1024]{2,1,0:T(8,128)S(1)} %collective-permute-done.4.edge_ref, f32[8,16,1024]{2,1,0:T(8,128)S(1)} %collective-permute-done.7.rim_ref, ...), custom_call_target="tpu_custom_call" | custom-call | flops 1073741824 | bytes 1048576 | tf_op jit(solution)/shard_map/pallas_call | solution.py:250
  63.7 7.4 %all-to-all-done = f32[256,1,64]{2,1,0:T(1,128)S(1)} async-done(((f32[256,1,64]{2,1,0:T(1,128)}), f32[256,1,64]{2,1,0:T(1,128)S(1)}, u32[]{:S(2)}, u32[]{:S(2)}) %all-to-all-start) | async-done | bytes 65568 | tf_op jit(solution)/shard_map/all_to_all | solution.py:249
  71.1 0.1 reduce_sum.9
  71.2 0.7 div.10
  (11 shorter events, 0.1 us)
Async XLA Ops:
  0.6 7.1 %copy-start = (f32[1,8,32,1024]{3,2,1,0:T(8,128)S(1)}, f32[1,8,32,1024]{3,2,1,0:T(8,128)}, u32[]{:S(2)}) copy-start(f32[1,8,32,1024]{3,2,1,0:T(8,128)} %param.5) | copy-start | bytes 3145732
  0.6 7.1 %copy-start.1 = (f32[1,32,1024]{2,1,0:T(8,128)S(1)}, f32[1,32,1024]{2,1,0:T(8,128)}, u32[]{:S(2)}) copy-start(f32[1,32,1024]{2,1,0:T(8,128)} %param.6) | copy-start | bytes 393220
  0.6 7.1 %copy-start.2 = (f32[1,32,1024]{2,1,0:T(8,128)S(1)}, f32[1,32,1024]{2,1,0:T(8,128)}, u32[]{:S(2)}) copy-start(f32[1,32,1024]{2,1,0:T(8,128)} %param.7) | copy-start | bytes 393220
  2.6 9.2 %collective-permute-start.2 = (f32[10,4,1024]{2,1,0:T(4,128)}, f32[10,4,1024]{2,1,0:T(4,128)S(1)}, u32[]{:S(2)}, u32[]{:S(2)}) collective-permute-start(f32[10,4,1024]{2,1,0:T(4,128)} %get-tuple-element.14), channel_id=1, source_target_pairs={{0,1},{1,2},{2,3},{3,4},{4,5},{5,6},{6,7},{7,0},{8,9},{9,10},{10,1... | collective-permute-start | bytes 491528 | tf_op jit(solution)/shard_map/ppermute | solution.py:220
  7.1 7.7 %collective-permute-start.3 = (f32[10,4,1024]{2,1,0:T(4,128)}, f32[10,4,1024]{2,1,0:T(4,128)S(1)}, u32[]{:S(2)}, u32[]{:S(2)}) collective-permute-start(f32[10,4,1024]{2,1,0:T(4,128)} %get-tuple-element.15), channel_id=1, source_target_pairs={{0,7},{1,0},{2,1},{3,2},{4,3},{5,4},{6,5},{7,6},{8,15},{9,8},{10,9... | collective-permute-start | bytes 491528 | tf_op jit(solution)/shard_map/ppermute | solution.py:219
  10.4 29.9 %collective-permute-start.1 = (f32[8,16,1024]{2,1,0:T(8,128)S(1)}, f32[8,16,1024]{2,1,0:T(8,128)S(1)}, u32[]{:S(2)}, u32[]{:S(2)}) collective-permute-start(f32[8,16,1024]{2,1,0:T(8,128)S(1)} %get-tuple-element.13), channel_id=1, source_target_pairs={{0,8},{8,16},{16,24},{24,32},{32,40},{40,48},{48,56},{56,64},{64,7... | collective-permute-start | bytes 1572872 | tf_op jit(solution)/shard_map/ppermute | solution.py:239
  18.5 21.9 %collective-permute-start.4 = (f32[8,16,1024]{2,1,0:T(8,128)S(1)}, f32[8,16,1024]{2,1,0:T(8,128)S(1)}, u32[]{:S(2)}, u32[]{:S(2)}) collective-permute-start(f32[8,16,1024]{2,1,0:T(8,128)S(1)} %get-tuple-element.16), channel_id=1, source_target_pairs={{0,8},{8,16},{16,24},{24,32},{32,40},{40,48},{48,56},{56,64},{64,7... | collective-permute-start | bytes 1572872 | tf_op jit(solution)/shard_map/ppermute | solution.py:240
  20.0 20.4 %collective-permute-start.6 = (f32[8,16,1024]{2,1,0:T(8,128)S(1)}, f32[8,16,1024]{2,1,0:T(8,128)S(1)}, u32[]{:S(2)}, u32[]{:S(2)}) collective-permute-start(f32[8,16,1024]{2,1,0:T(8,128)S(1)} %pad_maximum_fusion), channel_id=1, source_target_pairs={{1,10},{3,12},{5,14},{7,8},{9,18},{11,20},{13,22},{15,16},{17,26},... | collective-permute-start | bytes 1572872 | tf_op jit(solution)/shard_map/ppermute | solution.py:236
  21.6 18.8 %collective-permute-start.5 = (f32[8,16,1024]{2,1,0:T(8,128)S(1)}, f32[8,16,1024]{2,1,0:T(8,128)S(1)}, u32[]{:S(2)}, u32[]{:S(2)}) collective-permute-start(f32[8,16,1024]{2,1,0:T(8,128)S(1)} %get-tuple-element.18), channel_id=1, source_target_pairs={{1,0},{2,1},{3,2},{4,3},{5,4},{6,5},{7,6},{0,7},{9,8},{11,10},{13,... | collective-permute-start | bytes 1572872 | tf_op jit(solution)/shard_map/ppermute | solution.py:238
  23.5 16.9 %collective-permute-start = (s32[1]{0:T(128)}, s32[1]{0:T(128)}, u32[]{:S(2)}, u32[]{:S(2)}) collective-permute-start(s32[1]{0:T(128)} %param.9), channel_id=1, source_target_pairs={{0,8},{8,16},{16,24},{24,32},{32,40},{40,48},{48,56},{56,64},{64,7... | collective-permute-start | bytes 20 | tf_op jit(solution)/shard_map/ppermute | solution.py:228
  43.2 18.6 %collective-permute-start.7 = (f32[8,16,1024]{2,1,0:T(8,128)}, f32[8,16,1024]{2,1,0:T(8,128)S(1)}, u32[]{:S(2)}, u32[]{:S(2)}) collective-permute-start(f32[8,16,1024]{2,1,0:T(8,128)} %get-tuple-element.20), channel_id=1, source_target_pairs={{0,1},{1,2},{2,3},{3,4},{4,5},{5,6},{6,7},{7,0},{8,9},{10,11},{12,... | collective-permute-start | bytes 1572872 | tf_op jit(solution)/shard_map/ppermute | solution.py:248
  48.9 22.2 %all-to-all-start = ((f32[256,1,64]{2,1,0:T(1,128)}), f32[256,1,64]{2,1,0:T(1,128)S(1)}, u32[]{:S(2)}, u32[]{:S(2)}) async-start(f32[256,1,64]{2,1,0:T(1,128)} %bitcast.4), calls=%async_computation | async-start | bytes 262144 | tf_op jit(solution)/shard_map/all_to_all | solution.py:249

commit v13 on v11

--- a/solution.py
+++ b/solution.py
@@ -193,9 +193,9 @@
     pairs = []
     for s in range(segs):
         for g in range(strips):
-            busy = (s + 1) % (segs // 2) == 0 and g % 2 == 1
-            if busy == direct:
-                pairs.append(((s - direct) * strips + g, s * strips + (g + 1) % strips))
+            crosses = g % 2 == 1 and s % (segs // 2) != 0
+            if crosses == direct:
+                pairs.append((((s - direct) % segs) * strips + g, s * strips + (g + 1) % strips))
     return pairs
 
 

time: 71.9 us -> 73.5 us (1.022)
  starting transfers between devices: 30.6 us -> 35.8 us
  waiting for transfers between devices: 25 us -> 23.3 us
  Pallas kernels: 12.2 us -> 10.8 us
    ppermute x1, starting transfers between devices: 0.08 us -> 2.99 us  [body(): edge = onward(edge)]
    ppermute x1, starting transfers between devices: 0.13 us -> 2.62 us  [body(): mid = onward(mid)]
    ppermute x1, waiting for transfers between devices: 8.92 us -> 11.3 us  [body(): edge = onward(edge)]
    ppermute x1, waiting for transfers between devices: 3.13 us -> 0.84 us  [body(): mid = onward(mid)]
    ppermute x1, waiting for transfers between devices: 2.02 us -> 0.15 us  [body(): right = lax.ppermute(head, 'gx', shift_pairs(strips, -1))]
    pallas_call x1, Pallas kernels: 2.6 us -> 1.79 us  [body(): call(outer_kernel, [(vectors, 2 * TILE, cols)], [SMEM] + [VMEM] * 5, [buf...]
  transfers between devices with their start and end apart: 10 -> 10, of which waited for: 4 -> 4; matrix products, arithmetic and copies ran while one was open for 1% -> 1% of each run, Pallas kernels for 14% -> 12%
where the time goes in v13:
time: 73.5 us; the launch traced here: 72.9 us
  starting transfers between devices  35.8 us (49%)
  waiting for transfers between devices  23.3 us (32%)
  Pallas kernels  10.8 us (15%)
  local copies, waits for them, and re-layouts  1.46 us (2%)
  between operations  1.45 us (2%)
    ppermute x1, waiting for transfers between devices, body(): edge = onward(edge)  11.3 us
    all_to_all x1, waiting for transfers between devices, body(): gram = lax.all_to_all(gram, ('seg', 'gx'), 0, 0)  10.9 us
    all_to_all x1, starting transfers between devices, body(): gram = lax.all_to_all(gram, ('seg', 'gx'), 0, 0)  10.4 us
    ppermute x1, starting transfers between devices, body(): beyond = backward(beyond)  8.16 us
    ppermute x1, starting transfers between devices, body(): right = lax.ppermute(head, 'gx', shift_pairs(strips, -1))  3.32 us
    ppermute x1, starting transfers between devices, body(): edge = onward(edge)  2.99 us
    ppermute x1, starting transfers between devices, body(): mid = onward(mid)  2.62 us
    pallas_call x1, Pallas kernels, body(): call(gram_kernel, [(world, pairs)], [SMEM] + [VMEM] * 6, [buffer(vectors,...  2.47 us
  transfers between devices with their start and end apart: 10, of which 4 were waited for; matrix products, arithmetic and copies ran while one was open for 1% of the time, Pallas kernels for 12%

profile of v13, /device:TPU:1, one launch (start us, length us, event | category | flops | bytes accessed | tf_op | source)
XLA Modules:
  0.0 72.9 jit_solution(4122357873680248222)
XLA Ops:
  0.7 2.0 %shard_map.69 = (f32[10,4,1024]{2,1,0:T(4,128)}, f32[10,4,1024]{2,1,0:T(4,128)}) custom-call(f32[8,32,1024]{2,1,0:T(8,128)} %bitcast.8, f32[32,1024]{1,0:T(8,128)} %bitcast.14, f32[32,1024]{1,0:T(8,128)} %bitcast.17), custom_call_target="tpu_custom_call" | custom-call | flops 1073741824 | bytes 4194304 | tf_op jit(solution)/shard_map/pallas_call | solution.py:214
  2.6 3.3 %collective-permute-start.2 = (f32[10,4,1024]{2,1,0:T(4,128)}, f32[10,4,1024]{2,1,0:T(4,128)S(1)}, u32[]{:S(2)}, u32[]{:S(2)}) collective-permute-start(f32[10,4,1024]{2,1,0:T(4,128)} %get-tuple-element.19), channel_id=1, source_target_pairs={{0,7},{1,0},{2,1},{3,2},{4,3},{5,4},{6,5},{7,6},{8,15},{9,8},{10,9... | collective-permute-start | bytes 491528 | tf_op jit(solution)/shard_map/ppermute | solution.py:222
  5.9 1.2 %collective-permute-start.3 = (f32[10,4,1024]{2,1,0:T(4,128)}, f32[10,4,1024]{2,1,0:T(4,128)S(1)}, u32[]{:S(2)}, u32[]{:S(2)}) collective-permute-start(f32[10,4,1024]{2,1,0:T(4,128)} %get-tuple-element.20), channel_id=1, source_target_pairs={{0,1},{1,2},{2,3},{3,4},{4,5},{5,6},{6,7},{7,0},{8,9},{9,10},{10,1... | collective-permute-start | bytes 491528 | tf_op jit(solution)/shard_map/ppermute | solution.py:223
  7.9 1.4 %shard_map.68 = (f32[8,16,1024]{2,1,0:T(8,128)S(1)}, f32[8,16,1024]{2,1,0:T(8,128)S(1)}) custom-call(s32[1]{0:T(128)S(6)} %copy.8.count_ref, f32[8,32,1024]{2,1,0:T(8,128)S(1)} %bitcast.9, f32[32,1024]{1,0:T(8,128)S(1)} %bitcast.15, f32[32,1024]{1,0:T(8,128)S(1)} %bitcast.18), custom_call_target="tpu_custom_call" | custom-call | flops 68719476736 | bytes 4194304 | tf_op jit(solution)/shard_map/pallas_call | solution.py:225
  9.3 2.6 %collective-permute-start.1 = (f32[8,16,1024]{2,1,0:T(8,128)S(1)}, f32[8,16,1024]{2,1,0:T(8,128)S(1)}, u32[]{:S(2)}, u32[]{:S(2)}) collective-permute-start(f32[8,16,1024]{2,1,0:T(8,128)S(1)} %get-tuple-element.17), channel_id=1, source_target_pairs={{0,8},{8,16},{16,24},{24,32},{32,40},{40,48},{48,56},{56,64},{64,7... | collective-permute-start | bytes 1572872 | tf_op jit(solution)/shard_map/ppermute | solution.py:235
  11.9 0.1 collective-permute-done.2.right_ref
  12.1 8.2 %collective-permute-start.5 = (f32[8,16,1024]{2,1,0:T(8,128)S(1)}, f32[8,16,1024]{2,1,0:T(8,128)S(1)}, u32[]{:S(2)}, u32[]{:S(2)}) collective-permute-start(f32[8,16,1024]{2,1,0:T(8,128)S(1)} %get-tuple-element.24), channel_id=1, source_target_pairs={{1,0},{2,1},{3,2},{4,3},{5,4},{6,5},{7,6},{0,7},{9,8},{11,10},{13,... | collective-permute-start | bytes 1572872 | tf_op jit(solution)/shard_map/ppermute | solution.py:233
  20.2 1.4 %collective-permute-start = (s32[1]{0:T(128)}, s32[1]{0:T(128)}, u32[]{:S(2)}, u32[]{:S(2)}) collective-permute-start(s32[1]{0:T(128)} %param.9), channel_id=1, source_target_pairs={{0,8},{8,16},{16,24},{24,32},{32,40},{40,48},{48,56},{56,64},{64,7... | collective-permute-start | bytes 20 | tf_op jit(solution)/shard_map/ppermute | solution.py:224
  21.7 1.8 %shard_map.70 = f32[8,16,1024]{2,1,0:T(8,128)S(1)} custom-call(s32[1]{0:T(128)S(6)} %copy.8.count_ref, f32[8,32,1024]{2,1,0:T(8,128)S(1)} %bitcast.10, f32[32,1024]{1,0:T(8,128)S(1)} %bitcast.16, f32[32,1024]{1,0:T(8,128)S(1)} %bitcast.19, f32[10,4,1024]{2,1,0:T(4,128)S(1)} %collective-permute-done.3.left_ref, ...), custom_call_target="tpu_custom_call" | custom-call | flops 1073741824 | bytes 4194304 | tf_op jit(solution)/shard_map/pallas_call | solution.py:236
  23.4 3.0 %collective-permute-start.4 = (f32[8,16,1024]{2,1,0:T(8,128)S(1)}, f32[8,16,1024]{2,1,0:T(8,128)S(1)}, u32[]{:S(2)}, u32[]{:S(2)}) collective-permute-start(f32[8,16,1024]{2,1,0:T(8,128)S(1)} %shard_map.70), channel_id=1, source_target_pairs={{0,8},{8,16},{16,24},{24,32},{32,40},{40,48},{48,56},{56,64},{64,7... | collective-permute-start | bytes 1572872 | tf_op jit(solution)/shard_map/ppermute | solution.py:244
  26.5 0.1 pad_maximum_fusion
  26.5 1.3 %collective-permute-start.8 = (f32[8,16,1024]{2,1,0:T(8,128)S(1)}, f32[8,16,1024]{2,1,0:T(8,128)S(1)}, u32[]{:S(2)}, u32[]{:S(2)}) collective-permute-start(f32[8,16,1024]{2,1,0:T(8,128)S(1)} %pad_maximum_fusion), channel_id=1, source_target_pairs={{1,10},{3,12},{5,14},{7,8},{9,18},{11,20},{13,22},{15,16},{17,26},... | collective-permute-start | bytes 1572872 | tf_op jit(solution)/shard_map/ppermute | solution.py:245
  27.8 0.8 %collective-permute-done.1.mid_ref = f32[8,16,1024]{2,1,0:T(8,128)S(1)} collective-permute-done((f32[8,16,1024]{2,1,0:T(8,128)S(1)}, f32[8,16,1024]{2,1,0:T(8,128)S(1)}, u32[]{:S(2)}, u32[]{:S(2)}) %collective-permute-start.1) | collective-permute-done | bytes 524320 | tf_op jit(solution)/shard_map/ppermute | solution.py:235
  28.7 2.4 %collective-permute-start.6 = (f32[8,8,1024]{2,1,0:T(8,128)S(1)}, f32[8,8,1024]{2,1,0:T(8,128)S(1)}, u32[]{:S(2)}, u32[]{:S(2)}) collective-permute-start(f32[8,8,1024]{2,1,0:T(8,128)S(1)} %slice.16), channel_id=1, source_target_pairs={{0,1},{1,2},{2,3},{3,4},{4,5},{5,6},{6,7},{7,0},{8,9},{10,11},{12,... | collective-permute-start | bytes 786440 | tf_op jit(solution)/shard_map/ppermute | solution.py:247
  31.1 1.2 %shard_map.71 = (f32[64,128]{1,0:T(8,128)S(1)}, f32[8,32,1024]{2,1,0:T(8,128)S(1)}) custom-call(s32[1]{0:T(128)} %collective-permute-done.drift_ref, f32[8,32,1024]{2,1,0:T(8,128)S(1)} %bitcast.11, f32[8,16,1024]{2,1,0:T(8,128)S(1)} %collective-permute-done.5.beyond_ref), custom_call_target="tpu_custom_call" | custom-call | flops 17179869184 | bytes 4194304 | tf_op jit(solution)/shard_map/pallas_call | solution.py:246
  32.4 11.3 %collective-permute-done.4.edge_ref = f32[8,16,1024]{2,1,0:T(8,128)S(1)} collective-permute-done((f32[8,16,1024]{2,1,0:T(8,128)S(1)}, f32[8,16,1024]{2,1,0:T(8,128)S(1)}, u32[]{:S(2)}, u32[]{:S(2)}) %collective-permute-start.4) | collective-permute-done | bytes 524320 | tf_op jit(solution)/shard_map/ppermute | solution.py:244
  43.7 0.7 slice.13
  44.4 1.9 %collective-permute-start.7 = (f32[8,8,1024]{2,1,0:T(8,128)}, f32[8,8,1024]{2,1,0:T(8,128)S(1)}, u32[]{:S(2)}, u32[]{:S(2)}) collective-permute-start(f32[8,8,1024]{2,1,0:T(8,128)} %slice.13), channel_id=1, source_target_pairs={{0,1},{1,2},{2,3},{3,4},{4,5},{5,6},{6,7},{7,0},{8,9},{10,11},{12,... | collective-permute-start | bytes 786440 | tf_op jit(solution)/shard_map/ppermute | solution.py:249
  46.3 2.5 %shard_map.73 = f32[256,64]{1,0:T(8,128)} custom-call(s32[1]{0:T(128)} %collective-permute-done.drift_ref, f32[8,32,1024]{2,1,0:T(8,128)S(1)} %bitcast.12, f32[8,32,1024]{2,1,0:T(8,128)S(1)} %get-tuple-element.28.shifted_ref, f32[8,16,1024]{2,1,0:T(8,128)S(1)} %collective-permute-done.1.mid_ref, f32[8,16,1024]{2,1,0:T(8,128)S(1)} %collective-permute-done.4.edge_ref, ...), custom_call_target="tpu_custom_call" | custom-call | flops 1073741824 | bytes 4194304 | tf_op jit(solution)/shard_map/pallas_call | solution.py:250
  48.8 10.4 %all-to-all-start = ((f32[256,1,64]{2,1,0:T(1,128)}), f32[256,1,64]{2,1,0:T(1,128)S(1)}, u32[]{:S(2)}, u32[]{:S(2)}) async-start(f32[256,1,64]{2,1,0:T(1,128)} %bitcast.4), calls=%async_computation | async-start | bytes 262144 | tf_op jit(solution)/shard_map/all_to_all | solution.py:253
  59.3 1.9 %shard_map.72 = f32[8,32,1024]{2,1,0:T(8,128)} custom-call(s32[1]{0:T(128)} %collective-permute-done.drift_ref, f32[8,32,1024]{2,1,0:T(8,128)S(1)} %bitcast.13, f32[8,16,1024]{2,1,0:T(8,128)S(1)} %collective-permute-done.1.mid_ref, f32[8,16,1024]{2,1,0:T(8,128)S(1)} %collective-permute-done.4.edge_ref, f32[8,8,1024]{2,1,0:T(8,128)S(1)} %collective-permute-done.6.rim_mid_ref, ...), custom_call_target="tpu_custom_call" | custom-call | flops 1073741824 | bytes 4194304 | tf_op jit(solution)/shard_map/pallas_call | solution.py:254
  61.2 10.9 %all-to-all-done = f32[256,1,64]{2,1,0:T(1,128)S(1)} async-done(((f32[256,1,64]{2,1,0:T(1,128)}), f32[256,1,64]{2,1,0:T(1,128)S(1)}, u32[]{:S(2)}, u32[]{:S(2)}) %all-to-all-start) | async-done | bytes 65568 | tf_op jit(solution)/shard_map/all_to_all | solution.py:253
  72.1 0.1 reduce_sum.9
  72.2 0.7 div.10
  (16 shorter events, 0.1 us)
Async XLA Ops:
  0.6 7.2 %copy-start = (f32[1,8,32,1024]{3,2,1,0:T(8,128)S(1)}, f32[1,8,32,1024]{3,2,1,0:T(8,128)}, u32[]{:S(2)}) copy-start(f32[1,8,32,1024]{3,2,1,0:T(8,128)} %param.5) | copy-start | bytes 3145732
  0.6 7.2 %copy-start.1 = (f32[1,32,1024]{2,1,0:T(8,128)S(1)}, f32[1,32,1024]{2,1,0:T(8,128)}, u32[]{:S(2)}) copy-start(f32[1,32,1024]{2,1,0:T(8,128)} %param.6) | copy-start | bytes 393220
  0.6 7.2 %copy-start.2 = (f32[1,32,1024]{2,1,0:T(8,128)S(1)}, f32[1,32,1024]{2,1,0:T(8,128)}, u32[]{:S(2)}) copy-start(f32[1,32,1024]{2,1,0:T(8,128)} %param.7) | copy-start | bytes 393220
  2.6 9.4 %collective-permute-start.2 = (f32[10,4,1024]{2,1,0:T(4,128)}, f32[10,4,1024]{2,1,0:T(4,128)S(1)}, u32[]{:S(2)}, u32[]{:S(2)}) collective-permute-start(f32[10,4,1024]{2,1,0:T(4,128)} %get-tuple-element.19), channel_id=1, source_target_pairs={{0,7},{1,0},{2,1},{3,2},{4,3},{5,4},{6,5},{7,6},{8,15},{9,8},{10,9... | collective-permute-start | bytes 491528 | tf_op jit(solution)/shard_map/ppermute | solution.py:222
  5.9 6.1 %collective-permute-start.3 = (f32[10,4,1024]{2,1,0:T(4,128)}, f32[10,4,1024]{2,1,0:T(4,128)S(1)}, u32[]{:S(2)}, u32[]{:S(2)}) collective-permute-start(f32[10,4,1024]{2,1,0:T(4,128)} %get-tuple-element.20), channel_id=1, source_target_pairs={{0,1},{1,2},{2,3},{3,4},{4,5},{5,6},{6,7},{7,0},{8,9},{9,10},{10,1... | collective-permute-start | bytes 491528 | tf_op jit(solution)/shard_map/ppermute | solution.py:223
  9.3 19.4 %collective-permute-start.1 = (f32[8,16,1024]{2,1,0:T(8,128)S(1)}, f32[8,16,1024]{2,1,0:T(8,128)S(1)}, u32[]{:S(2)}, u32[]{:S(2)}) collective-permute-start(f32[8,16,1024]{2,1,0:T(8,128)S(1)} %get-tuple-element.17), channel_id=1, source_target_pairs={{0,8},{8,16},{16,24},{24,32},{32,40},{40,48},{48,56},{56,64},{64,7... | collective-permute-start | bytes 1572872 | tf_op jit(solution)/shard_map/ppermute | solution.py:235
  12.1 19.1 %collective-permute-start.5 = (f32[8,16,1024]{2,1,0:T(8,128)S(1)}, f32[8,16,1024]{2,1,0:T(8,128)S(1)}, u32[]{:S(2)}, u32[]{:S(2)}) collective-permute-start(f32[8,16,1024]{2,1,0:T(8,128)S(1)} %get-tuple-element.24), channel_id=1, source_target_pairs={{1,0},{2,1},{3,2},{4,3},{5,4},{6,5},{7,6},{0,7},{9,8},{11,10},{13,... | collective-permute-start | bytes 1572872 | tf_op jit(solution)/shard_map/ppermute | solution.py:233
  20.2 10.9 %collective-permute-start = (s32[1]{0:T(128)}, s32[1]{0:T(128)}, u32[]{:S(2)}, u32[]{:S(2)}) collective-permute-start(s32[1]{0:T(128)} %param.9), channel_id=1, source_target_pairs={{0,8},{8,16},{16,24},{24,32},{32,40},{40,48},{48,56},{56,64},{64,7... | collective-permute-start | bytes 20 | tf_op jit(solution)/shard_map/ppermute | solution.py:224
  23.4 20.3 %collective-permute-start.4 = (f32[8,16,1024]{2,1,0:T(8,128)S(1)}, f32[8,16,1024]{2,1,0:T(8,128)S(1)}, u32[]{:S(2)}, u32[]{:S(2)}) collective-permute-start(f32[8,16,1024]{2,1,0:T(8,128)S(1)} %shard_map.70), channel_id=1, source_target_pairs={{0,8},{8,16},{16,24},{24,32},{32,40},{40,48},{48,56},{56,64},{64,7... | collective-permute-start | bytes 1572872 | tf_op jit(solution)/shard_map/ppermute | solution.py:244
  26.5 19.8 %collective-permute-start.8 = (f32[8,16,1024]{2,1,0:T(8,128)S(1)}, f32[8,16,1024]{2,1,0:T(8,128)S(1)}, u32[]{:S(2)}, u32[]{:S(2)}) collective-permute-start(f32[8,16,1024]{2,1,0:T(8,128)S(1)} %pad_maximum_fusion), channel_id=1, source_target_pairs={{1,10},{3,12},{5,14},{7,8},{9,18},{11,20},{13,22},{15,16},{17,26},... | collective-permute-start | bytes 1572872 | tf_op jit(solution)/shard_map/ppermute | solution.py:245
  28.7 30.6 %collective-permute-start.6 = (f32[8,8,1024]{2,1,0:T(8,128)S(1)}, f32[8,8,1024]{2,1,0:T(8,128)S(1)}, u32[]{:S(2)}, u32[]{:S(2)}) collective-permute-start(f32[8,8,1024]{2,1,0:T(8,128)S(1)} %slice.16), channel_id=1, source_target_pairs={{0,1},{1,2},{2,3},{3,4},{4,5},{5,6},{6,7},{7,0},{8,9},{10,11},{12,... | collective-permute-start | bytes 786440 | tf_op jit(solution)/shard_map/ppermute | solution.py:247
  44.4 14.8 %collective-permute-start.7 = (f32[8,8,1024]{2,1,0:T(8,128)}, f32[8,8,1024]{2,1,0:T(8,128)S(1)}, u32[]{:S(2)}, u32[]{:S(2)}) collective-permute-start(f32[8,8,1024]{2,1,0:T(8,128)} %slice.13), channel_id=1, source_target_pairs={{0,1},{1,2},{2,3},{3,4},{4,5},{5,6},{6,7},{7,0},{8,9},{10,11},{12,... | collective-permute-start | bytes 786440 | tf_op jit(solution)/shard_map/ppermute | solution.py:249
  48.8 23.3 %all-to-all-start = ((f32[256,1,64]{2,1,0:T(1,128)}), f32[256,1,64]{2,1,0:T(1,128)S(1)}, u32[]{:S(2)}, u32[]{:S(2)}) async-start(f32[256,1,64]{2,1,0:T(1,128)} %bitcast.4), calls=%async_computation | async-start | bytes 262144 | tf_op jit(solution)/shard_map/all_to_all | solution.py:253

commit v14 on v10

--- a/solution.py
+++ b/solution.py
@@ -205,7 +205,7 @@
         [buffer(vectors, rows, cols), buffer(4, rows, cols)],
         64,
     )(step_counts, k, ax, ay)
-    beyond, right, left = lax.optimization_barrier((beyond, right, left))
+    beyond, right = lax.optimization_barrier((beyond, right))
     beyond = backward(beyond)
     mid = lax.ppermute(mid, "seg", [(s, s // half * half + (s + 1) % half) for s in range(segs)])
     (edge,) = call(

time: 78.5 us -> 68.8 us (0.88)
  starting transfers between devices: 41.6 us -> 21.2 us
  waiting for transfers between devices: 24.1 us -> 33 us
  Pallas kernels: 11.1 us -> 12.7 us
    ppermute x1, starting transfers between devices: 11.4 us -> 0.12 us  [body(): rim_mid = sideways(mid[:, -(DRIFT - TILE):])]
    all_to_all x1, starting transfers between devices: 12.1 us -> 5.41 us  [body(): gram = lax.all_to_all(gram, ('seg', 'gx'), 0, 0)]
    ppermute x1, waiting for transfers between devices: 0.01 us -> 5.85 us  [body(): edge = onward(edge)]
    ppermute x1, waiting for transfers between devices: 0.01 us -> 3.47 us  [body(): left = sideways(tail)]
    ppermute x1, starting transfers between devices: 6.27 us -> 2.84 us  [body(): beyond = backward(beyond)]
    ppermute x1, starting transfers between devices: 1.66 us -> 4.84 us  [body(): rim_hi = sideways(edge[:, :TILE])]
    ppermute x1, waiting for transfers between devices: 2.78 us -> 0.01 us  [body(): lax.ppermute(mid, 'seg', [(s, s // half * half + (s + 1) % half) for s in...]
    ppermute x1, starting transfers between devices: 1.23 us -> 0.01 us  [body(): left = sideways(tail)]
  transfers between devices with their start and end apart: 10 -> 10, of which waited for: 4 -> 7; matrix products, arithmetic and copies ran while one was open for 0% -> 0% of each run, Pallas kernels for 12% -> 15%
where the time goes in v14:
time: 68.8 us; the launch traced here: 69.2 us
  waiting for transfers between devices  33 us (48%)
  starting transfers between devices  21.2 us (31%)
  Pallas kernels  12.7 us (18%)
  between operations  1.44 us (2%)
  local copies, waits for them, and re-layouts  0.73 us (1%)
    all_to_all x1, waiting for transfers between devices, body(): gram = lax.all_to_all(gram, ('seg', 'gx'), 0, 0)  10.8 us
    ppermute x1, waiting for transfers between devices, body(): crossed = lax.ppermute(held, 'seg', [(0, half), (half, 0)])  9.04 us
    ppermute x1, waiting for transfers between devices, body(): edge = onward(edge)  5.85 us
    all_to_all x1, starting transfers between devices, body(): gram = lax.all_to_all(gram, ('seg', 'gx'), 0, 0)  5.41 us
    ppermute x1, starting transfers between devices, body(): rim_hi = sideways(edge[:, :TILE])  4.84 us
    ppermute x1, waiting for transfers between devices, body(): left = sideways(tail)  3.47 us
    pallas_call x1, Pallas kernels, body(): call(outer_kernel, [(vectors, 2 * TILE, cols)], [SMEM] + [VMEM] * 5, [buf...  3.4 us
    ppermute x1, starting transfers between devices, body(): right = backward(head)  3.32 us
  transfers between devices with their start and end apart: 10, of which 7 were waited for; matrix products, arithmetic and copies ran while one was open for 0% of the time, Pallas kernels for 15%

profile of v14, /device:TPU:1, one launch (start us, length us, event | category | flops | bytes accessed | tf_op | source)
XLA Modules:
  0.0 69.2 jit_solution(10581220266492642909)
XLA Ops:
  0.7 2.0 %shard_map.69 = (f32[10,4,1024]{2,1,0:T(4,128)}, f32[10,4,1024]{2,1,0:T(4,128)}) custom-call(f32[8,32,1024]{2,1,0:T(8,128)} %bitcast.8, f32[32,1024]{1,0:T(8,128)} %bitcast.13, f32[32,1024]{1,0:T(8,128)} %bitcast.16), custom_call_target="tpu_custom_call" | custom-call | flops 1073741824 | bytes 4194304 | tf_op jit(solution)/shard_map/pallas_call | solution.py:190
  2.6 3.3 %collective-permute-start.4 = (f32[10,4,1024]{2,1,0:T(4,128)}, f32[10,4,1024]{2,1,0:T(4,128)S(1)}, u32[]{:S(2)}, u32[]{:S(2)}) collective-permute-start(f32[10,4,1024]{2,1,0:T(4,128)} %get-tuple-element.18), channel_id=1, source_target_pairs={{0,7},{1,0},{2,1},{3,2},{4,3},{5,4},{6,5},{7,6},{8,15},{9,8},{10,9... | collective-permute-start | bytes 491528 | tf_op jit(solution)/shard_map/ppermute | solution.py:198
  6.6 2.7 %shard_map.68 = (f32[8,16,1024]{2,1,0:T(8,128)S(1)}, f32[8,16,1024]{2,1,0:T(8,128)S(1)}) custom-call(s32[1]{0:T(128)S(6)} %copy.8.count_ref, f32[8,32,1024]{2,1,0:T(8,128)S(1)} %bitcast.9, f32[32,1024]{1,0:T(8,128)S(1)} %bitcast.14, f32[32,1024]{1,0:T(8,128)S(1)} %bitcast.17), custom_call_target="tpu_custom_call" | custom-call | flops 68719476736 | bytes 4194304 | tf_op jit(solution)/shard_map/pallas_call | solution.py:201
  9.3 0.1 collective-permute-start.1
  9.4 2.7 %collective-permute-done.4.right_ref = f32[10,4,1024]{2,1,0:T(4,128)S(1)} collective-permute-done((f32[10,4,1024]{2,1,0:T(4,128)}, f32[10,4,1024]{2,1,0:T(4,128)S(1)}, u32[]{:S(2)}, u32[]{:S(2)}) %collective-permute-start.4) | collective-permute-done | bytes 163872 | tf_op jit(solution)/shard_map/ppermute | solution.py:198
  12.1 2.8 %collective-permute-start.6 = (f32[8,16,1024]{2,1,0:T(8,128)S(1)}, f32[8,16,1024]{2,1,0:T(8,128)S(1)}, u32[]{:S(2)}, u32[]{:S(2)}) collective-permute-start(f32[8,16,1024]{2,1,0:T(8,128)S(1)} %get-tuple-element.21), channel_id=1, source_target_pairs={{0,7},{1,0},{2,1},{3,2},{4,3},{5,4},{6,5},{7,6},{8,15},{9,8},{10,9... | collective-permute-start | bytes 1572872 | tf_op jit(solution)/shard_map/ppermute | solution.py:209
  14.9 1.3 %collective-permute-start = (s32[1]{0:T(128)}, s32[1]{0:T(128)}, u32[]{:S(2)}, u32[]{:S(2)}) collective-permute-start(s32[1]{0:T(128)} %param.9), channel_id=1, source_target_pairs={{0,8},{8,16},{16,24},{24,32},{32,40},{40,48},{48,56},{56,64},{64,7... | collective-permute-start | bytes 20 | tf_op jit(solution)/shard_map/ppermute | solution.py:200
  16.2 3.5 %collective-permute-done.3.left_ref = f32[10,4,1024]{2,1,0:T(4,128)S(1)} collective-permute-done((f32[10,4,1024]{2,1,0:T(4,128)S(1)}, f32[10,4,1024]{2,1,0:T(4,128)S(1)}, u32[]{:S(2)}, u32[]{:S(2)}) %collective-permute-start.3) | collective-permute-done | bytes 163872 | tf_op jit(solution)/shard_map/ppermute | solution.py:199
  19.7 3.4 %shard_map.70 = f32[8,16,1024]{2,1,0:T(8,128)S(1)} custom-call(s32[1]{0:T(128)S(6)} %copy.8.count_ref, f32[8,32,1024]{2,1,0:T(8,128)S(1)} %bitcast.10, f32[32,1024]{1,0:T(8,128)S(1)} %bitcast.15, f32[32,1024]{1,0:T(8,128)S(1)} %bitcast.18, f32[10,4,1024]{2,1,0:T(4,128)S(1)} %collective-permute-done.3.left_ref, ...), custom_call_target="tpu_custom_call" | custom-call | flops 1073741824 | bytes 4194304 | tf_op jit(solution)/shard_map/pallas_call | solution.py:211
  23.1 0.1 collective-permute-start.5
  23.2 3.2 %collective-permute-start.2 = (f32[8,16,1024]{2,1,0:T(8,128)}, f32[8,16,1024]{2,1,0:T(8,128)S(1)}, u32[]{:S(2)}, u32[]{:S(2)}) collective-permute-start(f32[8,16,1024]{2,1,0:T(8,128)} %collective-permute-done.1), channel_id=1, source_target_pairs={{0,128},{128,0},{1,129},{129,1},{2,130},{130,2},{3,131},{131,3},{4... | collective-permute-start | bytes 1572872 | tf_op jit(solution)/shard_map/ppermute | solution.py:222
  26.4 0.8 %collective-permute-done.6.beyond_ref = f32[8,16,1024]{2,1,0:T(8,128)S(1)} collective-permute-done((f32[8,16,1024]{2,1,0:T(8,128)S(1)}, f32[8,16,1024]{2,1,0:T(8,128)S(1)}, u32[]{:S(2)}, u32[]{:S(2)}) %collective-permute-start.6) | collective-permute-done | bytes 524320 | tf_op jit(solution)/shard_map/ppermute | solution.py:209
  27.2 1.2 %shard_map.71 = (f32[64,128]{1,0:T(8,128)S(1)}, f32[8,32,1024]{2,1,0:T(8,128)S(1)}) custom-call(s32[1]{0:T(128)} %collective-permute-done.drift_ref, f32[8,32,1024]{2,1,0:T(8,128)S(1)} %bitcast.11, f32[8,16,1024]{2,1,0:T(8,128)S(1)} %collective-permute-done.6.beyond_ref), custom_call_target="tpu_custom_call" | custom-call | flops 17179869184 | bytes 4194304 | tf_op jit(solution)/shard_map/pallas_call | solution.py:220
  28.5 9.0 %collective-permute-done.2 = f32[8,16,1024]{2,1,0:T(8,128)S(1)} collective-permute-done((f32[8,16,1024]{2,1,0:T(8,128)}, f32[8,16,1024]{2,1,0:T(8,128)S(1)}, u32[]{:S(2)}, u32[]{:S(2)}) %collective-permute-start.2) | collective-permute-done | bytes 524320 | tf_op jit(solution)/shard_map/ppermute | solution.py:222
  37.5 0.1 broadcast_select_fusion.mid_ref
  37.6 5.8 %collective-permute-done.5.edge_ref = f32[8,16,1024]{2,1,0:T(8,128)S(1)} collective-permute-done((f32[8,16,1024]{2,1,0:T(8,128)S(1)}, f32[8,16,1024]{2,1,0:T(8,128)S(1)}, u32[]{:S(2)}, u32[]{:S(2)}) %collective-permute-start.5) | collective-permute-done | bytes 524320 | tf_op jit(solution)/shard_map/ppermute | solution.py:219
  43.5 4.8 %collective-permute-start.8 = (f32[8,8,1024]{2,1,0:T(8,128)S(1)}, f32[8,8,1024]{2,1,0:T(8,128)S(1)}, u32[]{:S(2)}, u32[]{:S(2)}) collective-permute-start(f32[8,8,1024]{2,1,0:T(8,128)S(1)} %slice.7), channel_id=1, source_target_pairs={{0,1},{1,2},{2,3},{3,4},{4,5},{5,6},{6,7},{7,0},{8,9},{9,10},{10,1... | collective-permute-start | bytes 786440 | tf_op jit(solution)/shard_map/ppermute | solution.py:226
  48.3 0.1 collective-permute-start.7
  48.5 1.5 %shard_map.73 = f32[256,64]{1,0:T(8,128)} custom-call(f32[8,32,1024]{2,1,0:T(8,128)S(1)} %get-tuple-element.24.shifted_ref, f32[8,16,1024]{2,1,0:T(8,128)S(1)} %broadcast_select_fusion.mid_ref, f32[8,16,1024]{2,1,0:T(8,128)S(1)} %collective-permute-done.5.edge_ref, f32[64,128]{1,0:T(8,128)S(1)} %get-tuple-element.25.own_ref), custom_call_target="tpu_custom_call" | custom-call | flops 1073741824 | bytes 4194304 | tf_op jit(solution)/shard_map/pallas_call | solution.py:227
  50.0 5.4 %all-to-all-start = ((f32[256,1,64]{2,1,0:T(1,128)}), f32[256,1,64]{2,1,0:T(1,128)S(1)}, u32[]{:S(2)}, u32[]{:S(2)}) async-start(f32[256,1,64]{2,1,0:T(1,128)} %bitcast.4), calls=%async_computation | async-start | bytes 262144 | tf_op jit(solution)/shard_map/all_to_all | solution.py:228
  55.4 0.3 collective-permute-done.7.rim_mid_ref
  55.7 1.9 %shard_map.72 = f32[8,32,1024]{2,1,0:T(8,128)} custom-call(s32[1]{0:T(128)} %collective-permute-done.drift_ref, f32[8,32,1024]{2,1,0:T(8,128)S(1)} %bitcast.12, f32[8,16,1024]{2,1,0:T(8,128)S(1)} %broadcast_select_fusion.mid_ref, f32[8,16,1024]{2,1,0:T(8,128)S(1)} %collective-permute-done.5.edge_ref, f32[8,8,1024]{2,1,0:T(8,128)S(1)} %collective-permute-done.7.rim_mid_ref, ...), custom_call_target="tpu_custom_call" | custom-call | flops 1073741824 | bytes 4194304 | tf_op jit(solution)/shard_map/pallas_call | solution.py:229
  57.6 10.8 %all-to-all-done = f32[256,1,64]{2,1,0:T(1,128)S(1)} async-done(((f32[256,1,64]{2,1,0:T(1,128)}), f32[256,1,64]{2,1,0:T(1,128)S(1)}, u32[]{:S(2)}, u32[]{:S(2)}) %all-to-all-start) | async-done | bytes 65568 | tf_op jit(solution)/shard_map/all_to_all | solution.py:228
  68.5 0.7 div.10
  (16 shorter events, 0.1 us)
Async XLA Ops:
  0.6 6.0 %copy-start = (f32[1,8,32,1024]{3,2,1,0:T(8,128)S(1)}, f32[1,8,32,1024]{3,2,1,0:T(8,128)}, u32[]{:S(2)}) copy-start(f32[1,8,32,1024]{3,2,1,0:T(8,128)} %param.5) | copy-start | bytes 3145732
  0.6 6.0 %copy-start.1 = (f32[1,32,1024]{2,1,0:T(8,128)S(1)}, f32[1,32,1024]{2,1,0:T(8,128)}, u32[]{:S(2)}) copy-start(f32[1,32,1024]{2,1,0:T(8,128)} %param.6) | copy-start | bytes 393220
  0.6 6.0 %copy-start.2 = (f32[1,32,1024]{2,1,0:T(8,128)S(1)}, f32[1,32,1024]{2,1,0:T(8,128)}, u32[]{:S(2)}) copy-start(f32[1,32,1024]{2,1,0:T(8,128)} %param.7) | copy-start | bytes 393220
  2.6 9.4 %collective-permute-start.4 = (f32[10,4,1024]{2,1,0:T(4,128)}, f32[10,4,1024]{2,1,0:T(4,128)S(1)}, u32[]{:S(2)}, u32[]{:S(2)}) collective-permute-start(f32[10,4,1024]{2,1,0:T(4,128)} %get-tuple-element.18), channel_id=1, source_target_pairs={{0,7},{1,0},{2,1},{3,2},{4,3},{5,4},{6,5},{7,6},{8,15},{9,8},{10,9... | collective-permute-start | bytes 491528 | tf_op jit(solution)/shard_map/ppermute | solution.py:198
  6.6 8.3 %copy-start.3 = (f32[10,4,1024]{2,1,0:T(4,128)S(1)}, f32[10,4,1024]{2,1,0:T(4,128)}, u32[]{:S(2)}) copy-start(f32[10,4,1024]{2,1,0:T(4,128)} %get-tuple-element.16) | copy-start | bytes 491524
  9.3 13.9 %collective-permute-start.1 = (f32[8,16,1024]{2,1,0:T(8,128)S(1)}, f32[8,16,1024]{2,1,0:T(8,128)}, u32[]{:S(2)}, u32[]{:S(2)}) collective-permute-start(f32[8,16,1024]{2,1,0:T(8,128)S(1)} %get-tuple-element.15), channel_id=1, source_target_pairs={{0,8},{8,16},{16,24},{24,32},{32,40},{40,48},{48,56},{56,64},{64,7... | collective-permute-start | bytes 1572872 | tf_op jit(solution)/shard_map/ppermute | solution.py:210
  12.1 15.2 %collective-permute-start.6 = (f32[8,16,1024]{2,1,0:T(8,128)S(1)}, f32[8,16,1024]{2,1,0:T(8,128)S(1)}, u32[]{:S(2)}, u32[]{:S(2)}) collective-permute-start(f32[8,16,1024]{2,1,0:T(8,128)S(1)} %get-tuple-element.21), channel_id=1, source_target_pairs={{0,7},{1,0},{2,1},{3,2},{4,3},{5,4},{6,5},{7,6},{8,15},{9,8},{10,9... | collective-permute-start | bytes 1572872 | tf_op jit(solution)/shard_map/ppermute | solution.py:209
  14.9 4.8 %collective-permute-start.3 = (f32[10,4,1024]{2,1,0:T(4,128)S(1)}, f32[10,4,1024]{2,1,0:T(4,128)S(1)}, u32[]{:S(2)}, u32[]{:S(2)}) collective-permute-start(f32[10,4,1024]{2,1,0:T(4,128)S(1)} %copy-done.3), channel_id=1, source_target_pairs={{0,1},{1,2},{2,3},{3,4},{4,5},{5,6},{6,7},{7,0},{8,9},{9,10},{10,1... | collective-permute-start | bytes 491528 | tf_op jit(solution)/shard_map/ppermute | solution.py:199
  14.9 11.5 %collective-permute-start = (s32[1]{0:T(128)}, s32[1]{0:T(128)}, u32[]{:S(2)}, u32[]{:S(2)}) collective-permute-start(s32[1]{0:T(128)} %param.9), channel_id=1, source_target_pairs={{0,8},{8,16},{16,24},{24,32},{32,40},{40,48},{48,56},{56,64},{64,7... | collective-permute-start | bytes 20 | tf_op jit(solution)/shard_map/ppermute | solution.py:200
  23.1 20.4 %collective-permute-start.5 = (f32[8,16,1024]{2,1,0:T(8,128)S(1)}, f32[8,16,1024]{2,1,0:T(8,128)S(1)}, u32[]{:S(2)}, u32[]{:S(2)}) collective-permute-start(f32[8,16,1024]{2,1,0:T(8,128)S(1)} %shard_map.70), channel_id=1, source_target_pairs={{0,8},{8,16},{16,24},{24,32},{32,40},{40,48},{48,56},{56,64},{64,7... | collective-permute-start | bytes 1572872 | tf_op jit(solution)/shard_map/ppermute | solution.py:219
  23.2 14.4 %collective-permute-start.2 = (f32[8,16,1024]{2,1,0:T(8,128)}, f32[8,16,1024]{2,1,0:T(8,128)S(1)}, u32[]{:S(2)}, u32[]{:S(2)}) collective-permute-start(f32[8,16,1024]{2,1,0:T(8,128)} %collective-permute-done.1), channel_id=1, source_target_pairs={{0,128},{128,0},{1,129},{129,1},{2,130},{130,2},{3,131},{131,3},{4... | collective-permute-start | bytes 1572872 | tf_op jit(solution)/shard_map/ppermute | solution.py:222
  43.5 11.9 %collective-permute-start.8 = (f32[8,8,1024]{2,1,0:T(8,128)S(1)}, f32[8,8,1024]{2,1,0:T(8,128)S(1)}, u32[]{:S(2)}, u32[]{:S(2)}) collective-permute-start(f32[8,8,1024]{2,1,0:T(8,128)S(1)} %slice.7), channel_id=1, source_target_pairs={{0,1},{1,2},{2,3},{3,4},{4,5},{5,6},{6,7},{7,0},{8,9},{9,10},{10,1... | collective-permute-start | bytes 786440 | tf_op jit(solution)/shard_map/ppermute | solution.py:226
  48.3 7.4 %collective-permute-start.7 = (f32[8,8,1024]{2,1,0:T(8,128)S(1)}, f32[8,8,1024]{2,1,0:T(8,128)S(1)}, u32[]{:S(2)}, u32[]{:S(2)}) collective-permute-start(f32[8,8,1024]{2,1,0:T(8,128)S(1)} %slice.8), channel_id=1, source_target_pairs={{0,1},{1,2},{2,3},{3,4},{4,5},{5,6},{6,7},{7,0},{8,9},{9,10},{10,1... | collective-permute-start | bytes 786440 | tf_op jit(solution)/shard_map/ppermute | solution.py:224
  50.0 18.5 %all-to-all-start = ((f32[256,1,64]{2,1,0:T(1,128)}), f32[256,1,64]{2,1,0:T(1,128)S(1)}, u32[]{:S(2)}, u32[]{:S(2)}) async-start(f32[256,1,64]{2,1,0:T(1,128)} %bitcast.4), calls=%async_computation | async-start | bytes 262144 | tf_op jit(solution)/shard_map/all_to_all | solution.py:228
